TPU v7x, 32 devices: a whole 2x2x4 slice. The times are simulated.
32 devices in a mesh: parts: 2 (over y), seq: 16 (over z, x, core).
Axes of the slice: x: 2, y: 2, z: 4, core: 2. Of those that a mesh axis runs over, the one named last changes fastest.
Arguments:
- points: bfloat16 [8192, 128], P(('parts', 'seq')), parts along dimension 0, may hold values from -6 to 6
- route: int32 [2, 256], P(None, ('parts', 'seq')), parts along dimension 1, may hold values from 0 to 15, as said below
- owned: int32 [32], P(('parts', 'seq')), parts along dimension 0, may hold values from 0 to 16, as said below
- cotangent: bfloat16 [8192, 128], P(('parts', 'seq')), parts along dimension 0, may hold values from -6 to 6
- gain: float32 [128], replicated, may hold values from 0.1 to 1.9
- w_qkv: bfloat16 [128, 384], replicated, may hold values from -0.5 to 0.5
- b_qkv: float32 [384], replicated, may hold values from -3 to 3
- w_out: bfloat16 [128, 128], replicated, may hold values from -0.5 to 0.5
- b_out: float32 [128], replicated, may hold values from -3 to 3
Outputs:
- mixed: bfloat16 [8192, 128], P(('parts', 'seq')), parts along dimension 0
- grad_points: bfloat16 [8192, 128], P(('parts', 'seq')), parts along dimension 0
- grad_gain: float32 [256], P('parts'), parts along dimension 0
- grad_w_qkv: float32 [256, 384], P('parts'), parts along dimension 0
- grad_b_qkv: float32 [768], P('parts'), parts along dimension 0
- grad_w_out: float32 [256, 128], P('parts'), parts along dimension 0
- grad_b_out: float32 [256], P('parts'), parts along dimension 0
There are 2 independent parts, one for each index of `parts`. A program takes and returns all parts, laid end to end along the dimension named above; an argument that names none is the same for every part. Nothing has to cross between parts.
Inputs may be any that keep to these rules, and one draw needn't show every extreme that they name: `route`: row 0 names each block's owner, row 1 its slot there. Every slot below owned[o] of every owner o receives exactly one block, slots are numbered in Hilbert order of the owner's range; no device's Z-order blocks name the same owner twice. `owned`: the counts sum to 128; some device holds exactly 16 blocks and some none.
All inputs are finite; a program needn't handle non-finite values.
Results may differ from a plain program's by a relative error of at most 0.0095.
Values may be sent and summed in bfloat16 or wider, within the bound.
No kernel may reach another device: no remote copies, remote signals or barrier semaphores. Data moves between devices by JAX's collectives and lax.ppermute only.
A program may use at most 64 MiB of HBM per device.

v0:
```python
import functools

import jax
import jax.numpy as jnp
from jax import lax
from jax.experimental import pallas as pl
from jax.experimental.pallas import tpu as pltpu
from jax.sharding import PartitionSpec as P

HEADS = 8
EPS = 1e-05
EMPTY = 64.0
MASKED = -1e30

F32 = jnp.float32
BF16 = jnp.bfloat16

VMEM = pl.BlockSpec(memory_space=pltpu.VMEM)
ANY = pl.BlockSpec(memory_space=pl.ANY)
SMEM = pl.BlockSpec(memory_space=pltpu.SMEM)
MIB = 1024 * 1024
LARGE = pltpu.CompilerParams(vmem_limit_bytes=32 * MIB)
SMALL = pltpu.CompilerParams(vmem_limit_bytes=8 * MIB)


def matmul(left, right, dims=((1,), (0,))):
    return lax.dot_general(left, right, (dims, ((), ())), preferred_element_type=F32)


def send_rows(route_ref, shape, axis, block_rows):
    place = lax.broadcasted_iota(jnp.int32, shape, axis)
    target = jnp.zeros(shape, jnp.int32)
    for block in range(shape[axis] // block_rows):
        first = block * block_rows
        moved = route_ref[0, block] * block_rows + place - first
        target = jnp.where(place >= first, moved, target)
    return target


def scatter_kernel(block_rows, route_hbm, points_hbm, cot_hbm, out_ref, route_ref, points_ref, cot_ref, sems):
    copies = [
        pltpu.make_async_copy(source, target, sems.at[at])
        for at, (source, target) in enumerate(
            ((route_hbm, route_ref), (points_hbm, points_ref), (cot_hbm, cot_ref))
        )
    ]
    for copy in copies:
        copy.start()
    for copy in copies:
        copy.wait()
    rows, width = points_ref.shape
    target = send_rows(route_ref, (1, rows), 1, block_rows)
    index = lax.broadcasted_iota(jnp.int32, (out_ref.shape[0], rows), 0)
    pick = jnp.where(index == target, 1.0, 0.0).astype(BF16)
    ones = jnp.ones((rows, width), BF16)
    moved = matmul(pick, jnp.concatenate([points_ref[...], ones], axis=1))
    empty = (1.0 - moved[:, width:]) * EMPTY
    out_ref[:, :width] = (moved[:, :width] + empty).astype(BF16)
    out_ref[:, width:] = matmul(pick, cot_ref[...]).astype(BF16)


def normalize(points):
    centered = points - jnp.mean(points, axis=-1, keepdims=True)
    rstd = lax.rsqrt(jnp.mean(centered * centered, axis=-1, keepdims=True) + EPS)
    return centered * rstd, rstd


def owner_kernel(near, got_ref, vectors_ref, w_qkv_hbm, w_out_hbm, attn_ref, d_normed_ref, *refs):
    *outs, w_qkv_ref, w_out_ref, both_ref, sems = refs
    copies = [
        pltpu.make_async_copy(w_qkv_hbm, w_qkv_ref, sems.at[0]),
        pltpu.make_async_copy(w_out_hbm, w_out_ref, sems.at[1]),
    ]
    for copy in copies:
        copy.start()
    rows = got_ref.shape[0]
    width = got_ref.shape[1] // 2
    head = width // HEADS
    scale = head ** (-0.5)
    gain = vectors_ref[:, :width]
    b_qkv = vectors_ref[:, 2 * width :]

    points = got_ref[:, :width].astype(F32)
    cot = got_ref[:, width:]
    xhat, _ = normalize(points)
    normed = (xhat * gain).astype(BF16)
    for copy in copies:
        copy.wait()
    w_qkv = w_qkv_ref[...]
    w_out = w_out_ref[...]
    qkv = (matmul(normed, w_qkv) + b_qkv).astype(BF16)
    query, keys, values = qkv[:, :width], qkv[:, width : 2 * width], qkv[:, 2 * width :]
    d_attn = matmul(cot, w_out, ((1,), (1,))).astype(BF16)
    d_attn_t = matmul(w_out, cot, ((1,), (1,))).astype(BF16)
    d_attn_s = (d_attn.astype(F32) * scale).astype(BF16)

    keys_t = keys.T
    values_t = values.T
    keys_s = (keys.astype(F32) * scale).astype(BF16)
    lane = lax.broadcasted_iota(jnp.int32, (rows, width), 1)
    hidden = jnp.where(points > EMPTY / 2, MASKED, 0.0).astype(BF16)
    query_x = jnp.concatenate([query, jnp.where(lane == 0, 1.0, 0.0).astype(BF16)], axis=1)

    attn_t, dq_t = [], []
    d_keys = jnp.zeros((rows, width), F32)
    d_values = jnp.zeros((rows, width), F32)
    for h in range(HEADS):
        lo, hi = h * head, (h + 1) * head
        mine = (lane >= lo) & (lane < hi)
        keys_h = jnp.concatenate([jnp.where(mine, keys_s, 0), hidden], axis=1)
        scores = matmul(keys_h, query_x, ((1,), (1,)))
        expo = jnp.exp(scores - jnp.max(scores, axis=0, keepdims=True))
        probs = expo * (1.0 / jnp.sum(expo, axis=0, keepdims=True))
        probs_b = probs.astype(BF16)
        out_t = matmul(values_t[lo:hi, :], probs_b)
        attn_t.append(out_t)
        inner = jnp.sum(out_t * d_attn_t[lo:hi, :].astype(F32), axis=0, keepdims=True) * scale
        d_probs = matmul(jnp.where(mine, values, 0), d_attn_s, ((1,), (1,)))
        d_score = (probs * (d_probs - inner)).astype(BF16)
        dq_t.append(matmul(keys_t[lo:hi, :], d_score))
        d_values = jnp.where(mine, matmul(probs_b, d_attn), d_values)
        d_keys = jnp.where(mine, matmul(d_score, query), d_keys)

    attn_t = jnp.concatenate(attn_t, axis=0)
    attn_ref[...] = attn_t.T.astype(BF16)
    grad_w_out = matmul(attn_t.astype(BF16), cot)
    grad_b_out = jnp.sum(cot.astype(F32), axis=0, keepdims=True)

    d_query = jnp.concatenate(dq_t, axis=0).T
    d_qkv = jnp.concatenate([d_query, d_keys, d_values], axis=1).astype(BF16)
    d_normed = matmul(d_qkv, w_qkv, ((1,), (1,)))
    grad_w_qkv = matmul(normed, d_qkv, ((0,), (0,)))
    grad_b_qkv = jnp.sum(d_qkv.astype(F32), axis=0, keepdims=True)
    grad_gain = jnp.sum(d_normed * xhat, axis=0, keepdims=True)
    d_normed_ref[...] = d_normed
    sums = jnp.concatenate(
        [
            grad_b_qkv[:, : 2 * width],
            jnp.concatenate([grad_b_qkv[:, 2 * width :], grad_b_out], axis=1),
            jnp.concatenate([grad_gain, jnp.zeros_like(grad_gain)], axis=1),
            jnp.zeros((5, 2 * width), F32),
        ],
        axis=0,
    )
    left = grad_w_qkv[:, : 2 * width]
    right = jnp.concatenate([grad_w_qkv[:, 2 * width :], grad_w_out], axis=1)
    if near == 1:
        left_ref, right_ref, sums_ref = outs
        left_ref[...] = left.astype(BF16)
        right_ref[...] = right.astype(BF16)
        sums_ref[...] = sums.astype(BF16)
        return
    mine_ref, theirs_ref = outs
    both_ref[:width] = left
    both_ref[width:] = right
    core = lax.axis_index("seq") & 1
    for half, half_ref in ((core, mine_ref), (core ^ 1, theirs_ref)):
        span = pl.ds(pl.multiple_of(half * width, width), width)
        half_ref[:width] = both_ref[span].astype(half_ref.dtype)
        half_ref[width:] = sums.astype(half_ref.dtype)


def rows_kernel(got_ref, attn_ref, d_normed_ref, vectors_ref, w_out_ref, back_ref, token_ref):
    token_ref[...] = jnp.zeros_like(token_ref)
    width = attn_ref.shape[1]
    gain = vectors_ref[:, :width]
    b_out = vectors_ref[:, width : 2 * width]
    points = got_ref[:, :width].astype(F32)
    cot = got_ref[:, width:].astype(F32)
    xhat, rstd = normalize(points)
    mixed = points + (matmul(attn_ref[...], w_out_ref[...]) + b_out)
    d_xhat = d_normed_ref[...] * gain
    inner = (
        d_xhat
        - jnp.mean(d_xhat, axis=-1, keepdims=True)
        - xhat * jnp.mean(d_xhat * xhat, axis=-1, keepdims=True)
    )
    back_ref[:, :width] = mixed.astype(BF16)
    back_ref[:, width:] = (cot + rstd * inner).astype(BF16)


def sum_kernel(count, *refs):
    piece_refs, out_ref = refs[:count], refs[-1]
    values = [piece_ref[...].astype(F32) for piece_ref in piece_refs]
    while len(values) > 1:
        values = [left + right for left, right in zip(values[::2], values[1::2])]
    out_ref[...] = values[0].astype(BF16)


def tie_kernel(rows_ref, other_ref, out_ref):
    pass


def pick_kernel(block_rows, route_hbm, pick_ref, route_ref, sem):
    copy = pltpu.make_async_copy(route_hbm, route_ref, sem)
    copy.start()
    copy.wait()
    target = send_rows(route_ref, (pick_ref.shape[0], 1), 0, block_rows)
    index = lax.broadcasted_iota(jnp.int32, pick_ref.shape, 1)
    pick_ref[...] = jnp.where(index == target, 1.0, 0.0).astype(BF16)


def return_kernel(pick_ref, back_ref, mixed_ref, grad_ref, token_ref):
    token_ref[...] = jnp.zeros_like(token_ref)
    width = mixed_ref.shape[1]
    moved = matmul(pick_ref[...], back_ref[...]).astype(BF16)
    mixed_ref[...] = moved[:, :width]
    grad_ref[...] = moved[:, width:]


def weights_kernel(*refs):
    *half_refs, _, gain_ref, w_qkv_ref, b_qkv_ref, w_out_ref, b_out_ref, both_ref = refs
    width = w_out_ref.shape[1]
    core = lax.axis_index("seq") & 1
    for step, half_ref in enumerate(half_refs):
        place = core ^ step
        half = half_ref[...].astype(F32)
        both_ref[pl.ds(pl.multiple_of(place * width, width), width)] = half[:width]

        @pl.when(place == 0)
        def _():
            sums = half[width:]
            gain_ref[...] = sums[2, :width]
            b_qkv_ref[: 2 * width] = sums[0]
            b_qkv_ref[2 * width :] = sums[1, :width]
            b_out_ref[...] = sums[1, width:]

    w_qkv_ref[:, : 2 * width] = both_ref[:width]
    w_qkv_ref[:, 2 * width :] = both_ref[width:, :width]
    w_out_ref[...] = both_ref[width:, width:]


def exchange(message):
    return lax.all_to_all(message, "seq", split_axis=0, concat_axis=0, tiled=True)


def swap(piece, step, devs):
    return lax.ppermute(piece, "seq", [(dev, dev ^ step) for dev in range(devs)])


def local(points, route, owned, cotangent, gain, w_qkv, b_qkv, w_out, b_out):
    devs = lax.axis_size("seq")
    rows, width = points.shape
    block_rows = rows // route.shape[1]
    held = devs * block_rows
    share = width // devs
    near = 4 if devs == 16 and width % 64 == 0 else 1

    def shape(*dims, dtype=BF16):
        return jax.ShapeDtypeStruct(dims, dtype)

    sent = pl.pallas_call(
        functools.partial(scatter_kernel, block_rows),
        out_shape=shape(held, 2 * width),
        in_specs=[ANY] * 3,
        out_specs=VMEM,
        scratch_shapes=[
            pltpu.SMEM(route.shape, route.dtype),
            pltpu.VMEM(points.shape, points.dtype),
            pltpu.VMEM(cotangent.shape, cotangent.dtype),
            pltpu.SemaphoreType.DMA((3,)),
        ],
    )(route, points, cotangent)
    got = exchange(sent.reshape(devs, block_rows, 2 * width)).reshape(held, 2 * width)

    half = shape(width + 8, 2 * width)
    if near > 1:
        sums_shapes = (half, half)
    else:
        sums_shapes = (shape(width, 2 * width),) * 2 + (shape(8, 2 * width),)
    vectors = jnp.concatenate([gain, b_out, b_qkv])[None, :]
    attn, d_normed, *parts = pl.pallas_call(
        functools.partial(owner_kernel, near),
        out_shape=(shape(held, width), shape(held, width, dtype=F32)) + sums_shapes,
        in_specs=[VMEM, VMEM, ANY, ANY],
        out_specs=(VMEM,) * (2 + len(sums_shapes)),
        scratch_shapes=[
            pltpu.VMEM(w_qkv.shape, w_qkv.dtype),
            pltpu.VMEM(w_out.shape, w_out.dtype),
            pltpu.VMEM((2 * width, 2 * width), F32),
            pltpu.SemaphoreType.DMA((2,)),
        ],
        compiler_params=LARGE,
    )(got, vectors, w_qkv, w_out)
    back, token = pl.pallas_call(
        rows_kernel,
        out_shape=(shape(held, 2 * width), shape(8, 128, dtype=F32)),
        in_specs=[VMEM] * 5,
        out_specs=(VMEM,) * 2,
        compiler_params=SMALL,
        cost_estimate=pl.CostEstimate(
            flops=64 * held * width * width, bytes_accessed=16 * held * width, transcendentals=0
        ),
    )(got, attn, d_normed, vectors, w_out)

    pick = pl.pallas_call(
        functools.partial(pick_kernel, block_rows),
        out_shape=shape(rows, held),
        in_specs=[ANY],
        out_specs=VMEM,
        scratch_shapes=[pltpu.SMEM(route.shape, route.dtype), pltpu.SemaphoreType.DMA],
        compiler_params=SMALL,
    )(route)

    def give_back(back):
        return pl.pallas_call(
            return_kernel,
            out_shape=(shape(rows, width), shape(rows, width), shape(8, 128, dtype=F32)),
            in_specs=[VMEM] * 2,
            out_specs=(VMEM,) * 3,
            compiler_params=SMALL,
        )(pick, back)

    if near > 1:
        mine, theirs = parts

        def add(*pieces, after=(), flops=0):
            return pl.pallas_call(
                functools.partial(sum_kernel, len(pieces)),
                out_shape=half,
                in_specs=[VMEM] * (len(pieces) + len(after)),
                out_specs=VMEM,
                compiler_params=SMALL,
                cost_estimate=pl.CostEstimate(flops=flops, bytes_accessed=0, transcendentals=0),
            )(*pieces, *after)

        total = add(mine, swap(theirs, 1, devs), after=(token,))
        back = pl.pallas_call(
            tie_kernel,
            out_shape=back,
            in_specs=[ANY, VMEM],
            out_specs=ANY,
            input_output_aliases={0: 0},
            compiler_params=SMALL,
        )(back, total)
        back = exchange(back.reshape(devs, block_rows, 2 * width)).reshape(held, 2 * width)
        mixed, grad_points, token = give_back(back)
        total = add(total, swap(total, devs // 2, devs), flops=40_000_000_000)
        steps = [step for step in range(2, devs // 2, 2)]
        total = add(total, *(swap(total, step, devs) for step in steps))
        parts = [total, swap(total, 1, devs)]
        grad_gain, grad_wq, grad_bq, grad_wo, grad_bo = pl.pallas_call(
            weights_kernel,
            out_shape=tuple(
                shape(*dims, dtype=F32)
                for dims in ((width,), (width, 3 * width), (3 * width,), (width, width), (width,))
            ),
            in_specs=[VMEM] * 3,
            out_specs=(VMEM,) * 5,
            scratch_shapes=[pltpu.VMEM((2 * width, 2 * width), F32)],
            compiler_params=SMALL,
        )(*parts, token)
    else:
        left, right, sums = parts
        message = jnp.concatenate(
            [
                back.reshape(devs, block_rows, 2 * width),
                left.reshape(devs, share, 2 * width),
                right.reshape(devs, share, 2 * width),
                jnp.broadcast_to(sums[None], (devs, 8, 2 * width)),
            ],
            axis=1,
        )
        message = exchange(message)
        total = jnp.sum(message[:, block_rows:].astype(F32), axis=0)
        mine = total[: 2 * share].astype(BF16)
        both = exchange(jnp.broadcast_to(mine[None], (devs, 2 * share, 2 * width))).astype(F32)
        mixed, grad_points, _ = give_back(message[:, :block_rows].reshape(held, 2 * width))
        left = both[:, :share].reshape(width, 2 * width)
        right = both[:, share:].reshape(width, 2 * width)
        grad_wq = jnp.concatenate([left, right[:, :width]], axis=1)
        grad_wo = right[:, width:]
        flat = total[2 * share :].reshape(-1)
        grad_bq = flat[: 3 * width]
        grad_bo = flat[3 * width : 4 * width]
        grad_gain = flat[4 * width : 5 * width]

    return (mixed, grad_points, grad_gain, grad_wq, grad_bq, grad_wo, grad_bo)


def solution(mesh):
    placed = (
        P(("parts", "seq"), None),
        P(None, ("parts", "seq")),
        P(("parts", "seq")),
        P(("parts", "seq"), None),
        P(),
        P(),
        P(),
        P(),
        P(),
    )
    return jax.shard_map(
        local,
        mesh=mesh,
        in_specs=placed,
        out_specs=(
            P(("parts", "seq"), None),
            P(("parts", "seq"), None),
            P("parts"),
            P("parts", None),
            P("parts"),
            P("parts", None),
            P("parts"),
        ),
        check_vma=False,
    )
```

profile of v0, /device:TPU:0, one launch (start us, length us, event | category | flops | bytes accessed | tf_op | source)
XLA Modules:
  0.0 49.5 jit_solution(11057449714881045267)
XLA Ops:
  0.6 1.9 %shard_map.136 = bf16[512,256]{1,0:T(8,128)(2,1)} custom-call(s32[2,8]{1,0:T(2,128)} %route_hbm.3, bf16[256,128]{1,0:T(8,128)(2,1)} %points_hbm.1, bf16[256,128]{1,0:T(8,128)(2,1)} %cot_hbm.1), custom_call_target="tpu_custom_call" | custom-call | tf_op jit(solution)/shard_map/pallas_call | solution.py:252
  2.5 0.0 copy-start.3
  2.5 0.0 copy-start.4
  2.6 0.0 copy-start.5
  2.6 0.0 copy-start
  2.6 0.0 copy-start.1
  2.6 7.5 %all-to-all-start = ((bf16[16,32,256]{2,1,0:T(8,128)(2,1)}), bf16[16,32,256]{2,1,0:T(8,128)(2,1)S(1)}, u32[]{:S(2)}, u32[]{:S(2)}) async-start(bf16[16,32,256]{2,1,0:T(8,128)(2,1)} %bitcast.7), calls=%async_computation | async-start | bytes 524288 | tf_op jit(solution)/shard_map/all_to_all | solution.py:234
  10.1 0.0 copy-done.3
  10.1 0.0 copy-done.4
  10.1 0.0 copy-done.5
  10.2 10.0 %all-to-all-done = bf16[16,32,256]{2,1,0:T(8,128)(2,1)S(1)} async-done(((bf16[16,32,256]{2,1,0:T(8,128)(2,1)}), bf16[16,32,256]{2,1,0:T(8,128)(2,1)S(1)}, u32[]{:S(2)}, u32[]{:S(2)}) %all-to-all-start) | async-done | bytes 262176 | tf_op jit(solution)/shard_map/all_to_all | solution.py:234
  20.1 0.0 copy-done
  20.1 0.0 copy-done.1
  20.1 9.8 %shard_map.137 = (bf16[512,128]{1,0:T(8,128)(2,1)S(1)}, f32[512,128]{1,0:T(8,128)S(1)}, bf16[136,256]{1,0:T(8,128)(2,1)S(1)}, bf16[136,256]{1,0:T(8,128)(2,1)S(1)}) custom-call(bf16[512,256]{1,0:T(8,128)(2,1)S(1)} %bitcast.5, f32[1,640]{1,0:T(1,128)S(1)} %broadcast_in_dim.3.vectors_ref, bf16[128,384]{1,0:T(8,128)(2,1)S(1)} %copy-done, ...), custom_call_target="tpu_custom_call" | custom-call | tf_op jit(solution)/shard_map/pallas_call | solution.py:272
  30.0 0.1 collective-permute-start
  30.1 1.1 %shard_map.138 = (bf16[512,256]{1,0:T(8,128)(2,1)}, f32[8,128]{1,0:T(8,128)S(1)}) custom-call(bf16[512,256]{1,0:T(8,128)(2,1)S(1)} %bitcast.6, bf16[512,128]{1,0:T(8,128)(2,1)S(1)} %get-tuple-element.21.attn_ref, f32[512,128]{1,0:T(8,128)S(1)} %get-tuple-element.22.d_normed_ref, f32[1,640]{1,0:T(1,128)S(1)} %broadcast_in_dim.3.vectors_ref, ...), custom_call_target="tpu_custom_call" | custom-call | flops 536870912 | bytes 1048576 | tf_op jit(solution)/shard_map/pallas_call | solution.py:285
  31.1 0.2 collective-permute-done.refs_1_
  31.3 1.1 %collective-permute-start.1 = (bf16[136,256]{1,0:T(8,128)(2,1)S(1)}, bf16[136,256]{1,0:T(8,128)(2,1)S(1)}, u32[]{:S(2)}, u32[]{:S(2)}) collective-permute-start(bf16[136,256]{1,0:T(8,128)(2,1)S(1)} %shard_map.139.other_ref.refs_0_), channel_id=1, source_target_pairs={{0,8},{1,9},{2,10},{3,11},{4,12},{5,13},{6,14},{7,15},{8,0},{9,1},... | collective-permute-start | bytes 208904 | tf_op jit(solution)/shard_map/ppermute | solution.py:238
  32.5 3.5 %all-to-all-start.1 = ((bf16[16,32,256]{2,1,0:T(8,128)(2,1)}), bf16[16,32,256]{2,1,0:T(8,128)(2,1)S(1)}, u32[]{:S(2)}, u32[]{:S(2)}) async-start(bf16[16,32,256]{2,1,0:T(8,128)(2,1)} %bitcast.2), calls=%async_computation.1 | async-start | bytes 524288 | tf_op jit(solution)/shard_map/all_to_all | solution.py:234
  36.0 2.0 %collective-permute-done.1.refs_1_ = bf16[136,256]{1,0:T(8,128)(2,1)S(1)} collective-permute-done((bf16[136,256]{1,0:T(8,128)(2,1)S(1)}, bf16[136,256]{1,0:T(8,128)(2,1)S(1)}, u32[]{:S(2)}, u32[]{:S(2)}) %collective-permute-start.1) | collective-permute-done | bytes 69664 | tf_op jit(solution)/shard_map/ppermute | solution.py:238
  38.0 0.0 copy-start.2
  38.1 0.5 collective-permute-start.2
  38.5 0.9 %collective-permute-start.3 = (bf16[136,256]{1,0:T(8,128)(2,1)S(1)}, bf16[136,256]{1,0:T(8,128)(2,1)S(1)}, u32[]{:S(2)}, u32[]{:S(2)}) collective-permute-start(bf16[136,256]{1,0:T(8,128)(2,1)S(1)} %shard_map.142.refs_0_), channel_id=1, source_target_pairs={{0,4},{1,5},{2,6},{3,7},{4,0},{5,1},{6,2},{7,3},{8,12},{9,13},{10,... | collective-permute-start | bytes 208904 | tf_op jit(solution)/shard_map/ppermute | solution.py:238
  39.4 2.2 %collective-permute-start.4 = (bf16[136,256]{1,0:T(8,128)(2,1)S(1)}, bf16[136,256]{1,0:T(8,128)(2,1)S(1)}, u32[]{:S(2)}, u32[]{:S(2)}) collective-permute-start(bf16[136,256]{1,0:T(8,128)(2,1)S(1)} %shard_map.142.refs_0_), channel_id=1, source_target_pairs={{0,6},{1,7},{2,4},{3,5},{4,2},{5,3},{6,0},{7,1},{8,14},{9,15},{10,... | collective-permute-start | bytes 208904 | tf_op jit(solution)/shard_map/ppermute | solution.py:238
  41.6 1.3 %collective-permute-done.2.refs_1_ = bf16[136,256]{1,0:T(8,128)(2,1)S(1)} collective-permute-done((bf16[136,256]{1,0:T(8,128)(2,1)S(1)}, bf16[136,256]{1,0:T(8,128)(2,1)S(1)}, u32[]{:S(2)}, u32[]{:S(2)}) %collective-permute-start.2) | collective-permute-done | bytes 69664 | tf_op jit(solution)/shard_map/ppermute | solution.py:238
  42.9 1.7 %collective-permute-done.3.refs_2_ = bf16[136,256]{1,0:T(8,128)(2,1)S(1)} collective-permute-done((bf16[136,256]{1,0:T(8,128)(2,1)S(1)}, bf16[136,256]{1,0:T(8,128)(2,1)S(1)}, u32[]{:S(2)}, u32[]{:S(2)}) %collective-permute-start.3) | collective-permute-done | bytes 69664 | tf_op jit(solution)/shard_map/ppermute | solution.py:238
  44.7 2.5 %collective-permute-done.4.refs_3_ = bf16[136,256]{1,0:T(8,128)(2,1)S(1)} collective-permute-done((bf16[136,256]{1,0:T(8,128)(2,1)S(1)}, bf16[136,256]{1,0:T(8,128)(2,1)S(1)}, u32[]{:S(2)}, u32[]{:S(2)}) %collective-permute-start.4) | collective-permute-done | bytes 69664 | tf_op jit(solution)/shard_map/ppermute | solution.py:238
  47.2 0.1 collective-permute-start.5
  47.3 0.0 copy-done.2
  47.3 0.6 %shard_map.135.pick_ref = bf16[256,512]{1,0:T(8,128)(2,1)S(1)} custom-call(s32[2,8]{1,0:T(2,128)S(1)} %copy-done.2), custom_call_target="tpu_custom_call" | custom-call | tf_op jit(solution)/shard_map/pallas_call | solution.py:296
  47.9 0.0 all-to-all-done.1
  47.9 0.9 %shard_map.141 = (bf16[256,128]{1,0:T(8,128)(2,1)}, bf16[256,128]{1,0:T(8,128)(2,1)}, f32[8,128]{1,0:T(8,128)S(1)}) custom-call(bf16[256,512]{1,0:T(8,128)(2,1)S(1)} %shard_map.135.pick_ref, bf16[512,256]{1,0:T(8,128)(2,1)S(1)} %bitcast.4), custom_call_target="tpu_custom_call" | custom-call | tf_op jit(solution)/shard_map/pallas_call | solution.py:306
  48.8 0.0 collective-permute-done.5.refs_1_
  48.8 0.7 %shard_map.144 = (f32[128]{0:T(128)}, f32[128,384]{1,0:T(8,128)}, f32[384]{0:T(512)}, f32[128,128]{1,0:T(8,128)}, f32[128]{0:T(128)}) custom-call(bf16[136,256]{1,0:T(8,128)(2,1)S(1)} %shard_map.143.refs_0_, bf16[136,256]{1,0:T(8,128)(2,1)S(1)} %collective-permute-done.5.refs_1_, f32[8,128]{1,0:T(8,128)S(1)} %get-tuple-element.29.refs_2_), custom_call_target="tpu_custom_call" | custom-call | tf_op jit(solution)/shard_map/pallas_call | solution.py:342
  (6 shorter events, 0.1 us)
Async XLA Ops:
  2.5 7.6 %copy-start.3 = (f32[384]{0:T(512)S(1)}, f32[384]{0:T(512)}, u32[]{:S(2)}) copy-start(f32[384]{0:T(512)} %param.14) | copy-start | bytes 4612
  2.5 7.6 %copy-start.4 = (f32[128]{0:T(128)S(1)}, f32[128]{0:T(128)}, u32[]{:S(2)}) copy-start(f32[128]{0:T(128)} %param.16) | copy-start | bytes 1540
  2.6 7.6 %copy-start.5 = (f32[128]{0:T(128)S(1)}, f32[128]{0:T(128)}, u32[]{:S(2)}) copy-start(f32[128]{0:T(128)} %param.12) | copy-start | bytes 1540
  2.6 17.6 %copy-start = (bf16[128,384]{1,0:T(8,128)(2,1)S(1)}, bf16[128,384]{1,0:T(8,128)(2,1)}, u32[]{:S(2)}) copy-start(bf16[128,384]{1,0:T(8,128)(2,1)} %w_qkv_hbm.1) | copy-start | bytes 294916
  2.6 17.6 %copy-start.1 = (bf16[128,128]{1,0:T(8,128)(2,1)S(1)}, bf16[128,128]{1,0:T(8,128)(2,1)}, u32[]{:S(2)}) copy-start(bf16[128,128]{1,0:T(8,128)(2,1)} %w_out_ref.1) | copy-start | bytes 98308
  2.6 17.6 %all-to-all-start = ((bf16[16,32,256]{2,1,0:T(8,128)(2,1)}), bf16[16,32,256]{2,1,0:T(8,128)(2,1)S(1)}, u32[]{:S(2)}, u32[]{:S(2)}) async-start(bf16[16,32,256]{2,1,0:T(8,128)(2,1)} %bitcast.7), calls=%async_computation | async-start | bytes 524288 | tf_op jit(solution)/shard_map/all_to_all | solution.py:234
  30.0 1.3 %collective-permute-start = (bf16[136,256]{1,0:T(8,128)(2,1)S(1)}, bf16[136,256]{1,0:T(8,128)(2,1)S(1)}, u32[]{:S(2)}, u32[]{:S(2)}) collective-permute-start(bf16[136,256]{1,0:T(8,128)(2,1)S(1)} %get-tuple-element.25), channel_id=1, source_target_pairs={{0,1},{1,0},{2,3},{3,2},{4,5},{5,4},{6,7},{7,6},{8,9},{9,8},{10,11... | collective-permute-start | bytes 208904 | tf_op jit(solution)/shard_map/ppermute | solution.py:238
  31.3 6.7 %collective-permute-start.1 = (bf16[136,256]{1,0:T(8,128)(2,1)S(1)}, bf16[136,256]{1,0:T(8,128)(2,1)S(1)}, u32[]{:S(2)}, u32[]{:S(2)}) collective-permute-start(bf16[136,256]{1,0:T(8,128)(2,1)S(1)} %shard_map.139.other_ref.refs_0_), channel_id=1, source_target_pairs={{0,8},{1,9},{2,10},{3,11},{4,12},{5,13},{6,14},{7,15},{8,0},{9,1},... | collective-permute-start | bytes 208904 | tf_op jit(solution)/shard_map/ppermute | solution.py:238
  32.5 15.4 %all-to-all-start.1 = ((bf16[16,32,256]{2,1,0:T(8,128)(2,1)}), bf16[16,32,256]{2,1,0:T(8,128)(2,1)S(1)}, u32[]{:S(2)}, u32[]{:S(2)}) async-start(bf16[16,32,256]{2,1,0:T(8,128)(2,1)} %bitcast.2), calls=%async_computation.1 | async-start | bytes 524288 | tf_op jit(solution)/shard_map/all_to_all | solution.py:234
  38.0 9.2 %copy-start.2 = (s32[2,8]{1,0:T(2,128)S(1)}, s32[2,8]{1,0:T(2,128)}, u32[]{:S(2)}) copy-start(s32[2,8]{1,0:T(2,128)} %route_hbm.3) | copy-start | bytes 196
  38.1 4.9 %collective-permute-start.2 = (bf16[136,256]{1,0:T(8,128)(2,1)S(1)}, bf16[136,256]{1,0:T(8,128)(2,1)S(1)}, u32[]{:S(2)}, u32[]{:S(2)}) collective-permute-start(bf16[136,256]{1,0:T(8,128)(2,1)S(1)} %shard_map.142.refs_0_), channel_id=1, source_target_pairs={{0,2},{1,3},{2,0},{3,1},{4,6},{5,7},{6,4},{7,5},{8,10},{9,11},{10,... | collective-permute-start | bytes 208904 | tf_op jit(solution)/shard_map/ppermute | solution.py:238
  38.5 6.2 %collective-permute-start.3 = (bf16[136,256]{1,0:T(8,128)(2,1)S(1)}, bf16[136,256]{1,0:T(8,128)(2,1)S(1)}, u32[]{:S(2)}, u32[]{:S(2)}) collective-permute-start(bf16[136,256]{1,0:T(8,128)(2,1)S(1)} %shard_map.142.refs_0_), channel_id=1, source_target_pairs={{0,4},{1,5},{2,6},{3,7},{4,0},{5,1},{6,2},{7,3},{8,12},{9,13},{10,... | collective-permute-start | bytes 208904 | tf_op jit(solution)/shard_map/ppermute | solution.py:238
  39.4 7.7 %collective-permute-start.4 = (bf16[136,256]{1,0:T(8,128)(2,1)S(1)}, bf16[136,256]{1,0:T(8,128)(2,1)S(1)}, u32[]{:S(2)}, u32[]{:S(2)}) collective-permute-start(bf16[136,256]{1,0:T(8,128)(2,1)S(1)} %shard_map.142.refs_0_), channel_id=1, source_target_pairs={{0,6},{1,7},{2,4},{3,5},{4,2},{5,3},{6,0},{7,1},{8,14},{9,15},{10,... | collective-permute-start | bytes 208904 | tf_op jit(solution)/shard_map/ppermute | solution.py:238
  47.2 1.6 %collective-permute-start.5 = (bf16[136,256]{1,0:T(8,128)(2,1)S(1)}, bf16[136,256]{1,0:T(8,128)(2,1)S(1)}, u32[]{:S(2)}, u32[]{:S(2)}) collective-permute-start(bf16[136,256]{1,0:T(8,128)(2,1)S(1)} %shard_map.143.refs_0_), channel_id=1, source_target_pairs={{0,1},{1,0},{2,3},{3,2},{4,5},{5,4},{6,7},{7,6},{8,9},{9,8},{10,11... | collective-permute-start | bytes 208904 | tf_op jit(solution)/shard_map/ppermute | solution.py:238
where the time goes:
time: 50 us; the launch traced here: 49.5 us
  waiting for transfers between devices  17.7 us (35%)
  starting transfers between devices  15.8 us (32%)
  Pallas kernels  15.1 us (30%)
  between operations  0.8 us (2%)
    all_to_all x2, starting transfers between devices, exchange(): lax.all_to_all(message, 'seq', split_axis=0, concat_axis=0, tiled=True)  11 us
    all_to_all x2, waiting for transfers between devices, exchange(): lax.all_to_all(message, 'seq', split_axis=0, concat_axis=0, tiled=True)  9.99 us
    pallas_call x1, Pallas kernels, local(): pl.pallas_call(functools.partial(owner_kernel, near), out_shape=(shape(he...  9.83 us
    ppermute x6, waiting for transfers between devices, swap(): lax.ppermute(piece, 'seq', [(dev, dev ^ step) for dev in range(devs)])  7.71 us
    ppermute x6, starting transfers between devices, swap(): lax.ppermute(piece, 'seq', [(dev, dev ^ step) for dev in range(devs)])  4.82 us
    pallas_call x1, Pallas kernels, local(): pl.pallas_call(functools.partial(scatter_kernel, block_rows), out_shape=s...  1.89 us
    pallas_call x1, Pallas kernels, local(): pl.pallas_call(rows_kernel, out_shape=(shape(held, 2 * width), shape(8, 1...  1.08 us
  transfers between devices with their start and end apart: 8, of which 6 were waited for; matrix products, arithmetic and copies ran while one was open for 0% of the time, Pallas kernels for 5%

commit v1 on v0

--- a/solution.py
+++ b/solution.py
@@ -27,12 +27,20 @@
     return lax.dot_general(left, right, (dims, ((), ())), preferred_element_type=F32)
 
 
-def send_rows(route_ref, shape, axis, block_rows):
+def turned(index, devs):
+    top = devs.bit_length() - 2
+    place = 0
+    for bit in range(top + 1):
+        place = place + (((index >> bit) & 1) << (top - bit))
+    return place
+
+
+def send_rows(route_ref, shape, axis, block_rows, devs):
     place = lax.broadcasted_iota(jnp.int32, shape, axis)
     target = jnp.zeros(shape, jnp.int32)
     for block in range(shape[axis] // block_rows):
         first = block * block_rows
-        moved = route_ref[0, block] * block_rows + place - first
+        moved = turned(route_ref[0, block], devs) * block_rows + place - first
         target = jnp.where(place >= first, moved, target)
     return target
 
@@ -49,7 +57,7 @@
     for copy in copies:
         copy.wait()
     rows, width = points_ref.shape
-    target = send_rows(route_ref, (1, rows), 1, block_rows)
+    target = send_rows(route_ref, (1, rows), 1, block_rows, out_ref.shape[0] // block_rows)
     index = lax.broadcasted_iota(jnp.int32, (out_ref.shape[0], rows), 0)
     pick = jnp.where(index == target, 1.0, 0.0).astype(BF16)
     ones = jnp.ones((rows, width), BF16)
@@ -65,7 +73,7 @@
     return centered * rstd, rstd
 
 
-def owner_kernel(near, got_ref, vectors_ref, w_qkv_hbm, w_out_hbm, attn_ref, d_normed_ref, *refs):
+def owner_kernel(near, got_ref, vectors_ref, w_qkv_hbm, w_out_hbm, _, attn_ref, d_normed_ref, *refs):
     *outs, w_qkv_ref, w_out_ref, both_ref, sems = refs
     copies = [
         pltpu.make_async_copy(w_qkv_hbm, w_qkv_ref, sems.at[0]),
@@ -191,11 +199,13 @@
     pass
 
 
-def pick_kernel(block_rows, route_hbm, pick_ref, route_ref, sem):
+def pick_kernel(block_rows, route_hbm, pick_ref, token_ref, route_ref, sem):
+    token_ref[...] = jnp.zeros_like(token_ref)
     copy = pltpu.make_async_copy(route_hbm, route_ref, sem)
     copy.start()
     copy.wait()
-    target = send_rows(route_ref, (pick_ref.shape[0], 1), 0, block_rows)
+    rows, held = pick_ref.shape
+    target = send_rows(route_ref, (rows, 1), 0, block_rows, held // block_rows)
     index = lax.broadcasted_iota(jnp.int32, pick_ref.shape, 1)
     pick_ref[...] = jnp.where(index == target, 1.0, 0.0).astype(BF16)
 
@@ -231,7 +241,11 @@
 
 
 def exchange(message):
-    return lax.all_to_all(message, "seq", split_axis=0, concat_axis=0, tiled=True)
+    devs = message.shape[0]
+    order = [turned(place, devs) for place in range(devs)]
+    return lax.all_to_all(
+        message, "seq", split_axis=0, concat_axis=0, axis_index_groups=[order], tiled=True
+    )
 
 
 def swap(piece, step, devs):
@@ -263,6 +277,15 @@
     )(route, points, cotangent)
     got = exchange(sent.reshape(devs, block_rows, 2 * width)).reshape(held, 2 * width)
 
+    pick, early = pl.pallas_call(
+        functools.partial(pick_kernel, block_rows),
+        out_shape=(shape(rows, held), shape(8, 128, dtype=F32)),
+        in_specs=[ANY],
+        out_specs=(VMEM,) * 2,
+        scratch_shapes=[pltpu.SMEM(route.shape, route.dtype), pltpu.SemaphoreType.DMA],
+        compiler_params=SMALL,
+    )(route)
+
     half = shape(width + 8, 2 * width)
     if near > 1:
         sums_shapes = (half, half)
@@ -272,7 +295,7 @@
     attn, d_normed, *parts = pl.pallas_call(
         functools.partial(owner_kernel, near),
         out_shape=(shape(held, width), shape(held, width, dtype=F32)) + sums_shapes,
-        in_specs=[VMEM, VMEM, ANY, ANY],
+        in_specs=[VMEM, VMEM, ANY, ANY, VMEM],
         out_specs=(VMEM,) * (2 + len(sums_shapes)),
         scratch_shapes=[
             pltpu.VMEM(w_qkv.shape, w_qkv.dtype),
@@ -281,7 +304,7 @@
             pltpu.SemaphoreType.DMA((2,)),
         ],
         compiler_params=LARGE,
-    )(got, vectors, w_qkv, w_out)
+    )(got, vectors, w_qkv, w_out, early)
     back, token = pl.pallas_call(
         rows_kernel,
         out_shape=(shape(held, 2 * width), shape(8, 128, dtype=F32)),
@@ -292,15 +315,6 @@
             flops=64 * held * width * width, bytes_accessed=16 * held * width, transcendentals=0
         ),
     )(got, attn, d_normed, vectors, w_out)
-
-    pick = pl.pallas_call(
-        functools.partial(pick_kernel, block_rows),
-        out_shape=shape(rows, held),
-        in_specs=[ANY],
-        out_specs=VMEM,
-        scratch_shapes=[pltpu.SMEM(route.shape, route.dtype), pltpu.SemaphoreType.DMA],
-        compiler_params=SMALL,
-    )(route)
 
     def give_back(back):
         return pl.pallas_call(

time: 50 us -> 49.1 us (0.982)
  waiting for transfers between devices: 17.7 us -> 16.7 us
    all_to_all x2, starting transfers between devices: 11 us -> 11.6 us  [exchange(): lax.all_to_all(message, 'seq', split_axis=0, concat_axis=0, axis_index_gr...]
    all_to_all x2, waiting for transfers between devices: 9.99 us -> 9.48 us  [exchange(): lax.all_to_all(message, 'seq', split_axis=0, concat_axis=0, axis_index_gr...]
where the time goes in v1:
time: 49.1 us; the launch traced here: 48.6 us
  waiting for transfers between devices  16.7 us (34%)
  starting transfers between devices  15.9 us (32%)
  Pallas kernels  15.2 us (31%)
  between operations  0.81 us (2%)
    all_to_all x2, starting transfers between devices, exchange(): lax.all_to_all(message, 'seq', split_axis=0, concat_axis=0, axis_index_gr...  11.6 us
    pallas_call x1, Pallas kernels, local(): pl.pallas_call(functools.partial(owner_kernel, near), out_shape=(shape(he...  9.83 us
    all_to_all x2, waiting for transfers between devices, exchange(): lax.all_to_all(message, 'seq', split_axis=0, concat_axis=0, axis_index_gr...  9.48 us
    ppermute x6, waiting for transfers between devices, swap(): lax.ppermute(piece, 'seq', [(dev, dev ^ step) for dev in range(devs)])  7.25 us
    ppermute x6, starting transfers between devices, swap(): lax.ppermute(piece, 'seq', [(dev, dev ^ step) for dev in range(devs)])  4.34 us
    pallas_call x1, Pallas kernels, local(): pl.pallas_call(functools.partial(scatter_kernel, block_rows), out_shape=s...  1.9 us
    pallas_call x1, Pallas kernels, local(): pl.pallas_call(rows_kernel, out_shape=(shape(held, 2 * width), shape(8, 1...  1.09 us
  transfers between devices with their start and end apart: 8, of which 6 were waited for; matrix products, arithmetic and copies ran while one was open for 0% of the time, Pallas kernels for 5%

profile of v1, /device:TPU:0, one launch (start us, length us, event | category | flops | bytes accessed | tf_op | source)
XLA Modules:
  0.0 48.6 jit_solution(7100086122480462519)
XLA Ops:
  0.6 1.9 %shard_map.136 = bf16[512,256]{1,0:T(8,128)(2,1)} custom-call(s32[2,8]{1,0:T(2,128)} %route_hbm.3, bf16[256,128]{1,0:T(8,128)(2,1)} %points_hbm.1, bf16[256,128]{1,0:T(8,128)(2,1)} %cot_hbm.1), custom_call_target="tpu_custom_call" | custom-call | tf_op jit(solution)/shard_map/pallas_call | solution.py:266
  2.5 0.0 copy-start.2
  2.6 0.0 copy-start.3
  2.6 0.0 copy-start
  2.6 0.0 copy-start.1
  2.6 7.5 %all-to-all-start = ((bf16[16,32,256]{2,1,0:T(8,128)(2,1)}), bf16[16,32,256]{2,1,0:T(8,128)(2,1)S(1)}, u32[]{:S(2)}, u32[]{:S(2)}) async-start(bf16[16,32,256]{2,1,0:T(8,128)(2,1)} %bitcast.7), calls=%async_computation | async-start | bytes 524288 | tf_op jit(solution)/shard_map/all_to_all | solution.py:246
  10.1 0.0 copy-done.2
  10.1 0.0 copy-start.4
  10.1 0.0 copy-start.5
  10.1 0.6 %shard_map.135 = (bf16[256,512]{1,0:T(8,128)(2,1)S(1)}, f32[8,128]{1,0:T(8,128)S(1)}) custom-call(s32[2,8]{1,0:T(2,128)S(1)} %copy-done.2), custom_call_target="tpu_custom_call" | custom-call | tf_op jit(solution)/shard_map/pallas_call | solution.py:280
  10.8 0.0 copy-done.3
  10.8 0.0 copy-done.4
  10.8 0.0 copy-done.5
  10.8 9.5 %all-to-all-done = bf16[16,32,256]{2,1,0:T(8,128)(2,1)S(1)} async-done(((bf16[16,32,256]{2,1,0:T(8,128)(2,1)}), bf16[16,32,256]{2,1,0:T(8,128)(2,1)S(1)}, u32[]{:S(2)}, u32[]{:S(2)}) %all-to-all-start) | async-done | bytes 262176 | tf_op jit(solution)/shard_map/all_to_all | solution.py:246
  20.3 0.0 copy-done
  20.3 0.0 copy-done.1
  20.3 9.8 %shard_map.137 = (bf16[512,128]{1,0:T(8,128)(2,1)S(1)}, f32[512,128]{1,0:T(8,128)S(1)}, bf16[136,256]{1,0:T(8,128)(2,1)S(1)}, bf16[136,256]{1,0:T(8,128)(2,1)S(1)}) custom-call(bf16[512,256]{1,0:T(8,128)(2,1)S(1)} %bitcast.5, f32[1,640]{1,0:T(1,128)S(1)} %broadcast_in_dim.3.vectors_ref, bf16[128,384]{1,0:T(8,128)(2,1)S(1)} %copy-done, ...), custom_call_target="tpu_custom_call" | custom-call | tf_op jit(solution)/shard_map/pallas_call | solution.py:295
  30.1 0.1 collective-permute-start
  30.2 1.1 %shard_map.138 = (bf16[512,256]{1,0:T(8,128)(2,1)}, f32[8,128]{1,0:T(8,128)S(1)}) custom-call(bf16[512,256]{1,0:T(8,128)(2,1)S(1)} %bitcast.6, bf16[512,128]{1,0:T(8,128)(2,1)S(1)} %get-tuple-element.25.attn_ref, f32[512,128]{1,0:T(8,128)S(1)} %get-tuple-element.26.d_normed_ref, f32[1,640]{1,0:T(1,128)S(1)} %broadcast_in_dim.3.vectors_ref, ...), custom_call_target="tpu_custom_call" | custom-call | flops 536870912 | bytes 1048576 | tf_op jit(solution)/shard_map/pallas_call | solution.py:308
  31.3 0.2 collective-permute-done.refs_1_
  31.5 0.6 %collective-permute-start.1 = (bf16[136,256]{1,0:T(8,128)(2,1)S(1)}, bf16[136,256]{1,0:T(8,128)(2,1)S(1)}, u32[]{:S(2)}, u32[]{:S(2)}) collective-permute-start(bf16[136,256]{1,0:T(8,128)(2,1)S(1)} %shard_map.139.other_ref.refs_0_), channel_id=1, source_target_pairs={{0,8},{1,9},{2,10},{3,11},{4,12},{5,13},{6,14},{7,15},{8,0},{9,1},... | collective-permute-start | bytes 208904 | tf_op jit(solution)/shard_map/ppermute | solution.py:252
  32.1 4.1 %all-to-all-start.1 = ((bf16[16,32,256]{2,1,0:T(8,128)(2,1)}), bf16[16,32,256]{2,1,0:T(8,128)(2,1)S(1)}, u32[]{:S(2)}, u32[]{:S(2)}) async-start(bf16[16,32,256]{2,1,0:T(8,128)(2,1)} %bitcast.2), calls=%async_computation.1 | async-start | bytes 524288 | tf_op jit(solution)/shard_map/all_to_all | solution.py:246
  36.2 2.2 %collective-permute-done.1.refs_1_ = bf16[136,256]{1,0:T(8,128)(2,1)S(1)} collective-permute-done((bf16[136,256]{1,0:T(8,128)(2,1)S(1)}, bf16[136,256]{1,0:T(8,128)(2,1)S(1)}, u32[]{:S(2)}, u32[]{:S(2)}) %collective-permute-start.1) | collective-permute-done | bytes 69664 | tf_op jit(solution)/shard_map/ppermute | solution.py:252
  38.4 0.7 %collective-permute-start.4 = (bf16[136,256]{1,0:T(8,128)(2,1)S(1)}, bf16[136,256]{1,0:T(8,128)(2,1)S(1)}, u32[]{:S(2)}, u32[]{:S(2)}) collective-permute-start(bf16[136,256]{1,0:T(8,128)(2,1)S(1)} %shard_map.142.refs_0_), channel_id=1, source_target_pairs={{0,6},{1,7},{2,4},{3,5},{4,2},{5,3},{6,0},{7,1},{8,14},{9,15},{10,... | collective-permute-start | bytes 208904 | tf_op jit(solution)/shard_map/ppermute | solution.py:252
  39.1 1.0 %collective-permute-start.3 = (bf16[136,256]{1,0:T(8,128)(2,1)S(1)}, bf16[136,256]{1,0:T(8,128)(2,1)S(1)}, u32[]{:S(2)}, u32[]{:S(2)}) collective-permute-start(bf16[136,256]{1,0:T(8,128)(2,1)S(1)} %shard_map.142.refs_0_), channel_id=1, source_target_pairs={{0,4},{1,5},{2,6},{3,7},{4,0},{5,1},{6,2},{7,3},{8,12},{9,13},{10,... | collective-permute-start | bytes 208904 | tf_op jit(solution)/shard_map/ppermute | solution.py:252
  40.2 1.8 %collective-permute-start.2 = (bf16[136,256]{1,0:T(8,128)(2,1)S(1)}, bf16[136,256]{1,0:T(8,128)(2,1)S(1)}, u32[]{:S(2)}, u32[]{:S(2)}) collective-permute-start(bf16[136,256]{1,0:T(8,128)(2,1)S(1)} %shard_map.142.refs_0_), channel_id=1, source_target_pairs={{0,2},{1,3},{2,0},{3,1},{4,6},{5,7},{6,4},{7,5},{8,10},{9,11},{10,... | collective-permute-start | bytes 208904 | tf_op jit(solution)/shard_map/ppermute | solution.py:252
  41.9 3.7 %collective-permute-done.4.refs_3_ = bf16[136,256]{1,0:T(8,128)(2,1)S(1)} collective-permute-done((bf16[136,256]{1,0:T(8,128)(2,1)S(1)}, bf16[136,256]{1,0:T(8,128)(2,1)S(1)}, u32[]{:S(2)}, u32[]{:S(2)}) %collective-permute-start.4) | collective-permute-done | bytes 69664 | tf_op jit(solution)/shard_map/ppermute | solution.py:252
  45.7 0.9 %collective-permute-done.3.refs_2_ = bf16[136,256]{1,0:T(8,128)(2,1)S(1)} collective-permute-done((bf16[136,256]{1,0:T(8,128)(2,1)S(1)}, bf16[136,256]{1,0:T(8,128)(2,1)S(1)}, u32[]{:S(2)}, u32[]{:S(2)}) %collective-permute-start.3) | collective-permute-done | bytes 69664 | tf_op jit(solution)/shard_map/ppermute | solution.py:252
  46.5 0.0 collective-permute-done.2.refs_1_
  46.6 0.1 collective-permute-start.5
  46.7 0.0 all-to-all-done.1
  46.7 0.9 %shard_map.141 = (bf16[256,128]{1,0:T(8,128)(2,1)}, bf16[256,128]{1,0:T(8,128)(2,1)}, f32[8,128]{1,0:T(8,128)S(1)}) custom-call(bf16[256,512]{1,0:T(8,128)(2,1)S(1)} %get-tuple-element.23.pick_ref, bf16[512,256]{1,0:T(8,128)(2,1)S(1)} %bitcast.4), custom_call_target="tpu_custom_call" | custom-call | tf_op jit(solution)/shard_map/pallas_call | solution.py:320
  47.6 0.3 collective-permute-done.5.refs_1_
  47.9 0.7 %shard_map.144 = (f32[128]{0:T(128)}, f32[128,384]{1,0:T(8,128)}, f32[384]{0:T(512)}, f32[128,128]{1,0:T(8,128)}, f32[128]{0:T(128)}) custom-call(bf16[136,256]{1,0:T(8,128)(2,1)S(1)} %shard_map.143.refs_0_, bf16[136,256]{1,0:T(8,128)(2,1)S(1)} %collective-permute-done.5.refs_1_, f32[8,128]{1,0:T(8,128)S(1)} %get-tuple-element.33.refs_2_), custom_call_target="tpu_custom_call" | custom-call | tf_op jit(solution)/shard_map/pallas_call | solution.py:356
  (6 shorter events, 0.1 us)
Async XLA Ops:
  2.5 7.6 %copy-start.2 = (s32[2,8]{1,0:T(2,128)S(1)}, s32[2,8]{1,0:T(2,128)}, u32[]{:S(2)}) copy-start(s32[2,8]{1,0:T(2,128)} %route_hbm.3) | copy-start | bytes 196
  2.6 8.2 %copy-start.3 = (f32[384]{0:T(512)S(1)}, f32[384]{0:T(512)}, u32[]{:S(2)}) copy-start(f32[384]{0:T(512)} %param.14) | copy-start | bytes 4612
  2.6 17.7 %copy-start = (bf16[128,384]{1,0:T(8,128)(2,1)S(1)}, bf16[128,384]{1,0:T(8,128)(2,1)}, u32[]{:S(2)}) copy-start(bf16[128,384]{1,0:T(8,128)(2,1)} %w_qkv_hbm.1) | copy-start | bytes 294916
  2.6 17.7 %copy-start.1 = (bf16[128,128]{1,0:T(8,128)(2,1)S(1)}, bf16[128,128]{1,0:T(8,128)(2,1)}, u32[]{:S(2)}) copy-start(bf16[128,128]{1,0:T(8,128)(2,1)} %w_out_ref.1) | copy-start | bytes 98308
  2.6 17.7 %all-to-all-start = ((bf16[16,32,256]{2,1,0:T(8,128)(2,1)}), bf16[16,32,256]{2,1,0:T(8,128)(2,1)S(1)}, u32[]{:S(2)}, u32[]{:S(2)}) async-start(bf16[16,32,256]{2,1,0:T(8,128)(2,1)} %bitcast.7), calls=%async_computation | async-start | bytes 524288 | tf_op jit(solution)/shard_map/all_to_all | solution.py:246
  10.1 0.7 %copy-start.4 = (f32[128]{0:T(128)S(1)}, f32[128]{0:T(128)}, u32[]{:S(2)}) copy-start(f32[128]{0:T(128)} %param.16) | copy-start | bytes 1540
  10.1 0.7 %copy-start.5 = (f32[128]{0:T(128)S(1)}, f32[128]{0:T(128)}, u32[]{:S(2)}) copy-start(f32[128]{0:T(128)} %param.12) | copy-start | bytes 1540
  30.1 1.3 %collective-permute-start = (bf16[136,256]{1,0:T(8,128)(2,1)S(1)}, bf16[136,256]{1,0:T(8,128)(2,1)S(1)}, u32[]{:S(2)}, u32[]{:S(2)}) collective-permute-start(bf16[136,256]{1,0:T(8,128)(2,1)S(1)} %get-tuple-element.29), channel_id=1, source_target_pairs={{0,1},{1,0},{2,3},{3,2},{4,5},{5,4},{6,7},{7,6},{8,9},{9,8},{10,11... | collective-permute-start | bytes 208904 | tf_op jit(solution)/shard_map/ppermute | solution.py:252
  31.5 6.9 %collective-permute-start.1 = (bf16[136,256]{1,0:T(8,128)(2,1)S(1)}, bf16[136,256]{1,0:T(8,128)(2,1)S(1)}, u32[]{:S(2)}, u32[]{:S(2)}) collective-permute-start(bf16[136,256]{1,0:T(8,128)(2,1)S(1)} %shard_map.139.other_ref.refs_0_), channel_id=1, source_target_pairs={{0,8},{1,9},{2,10},{3,11},{4,12},{5,13},{6,14},{7,15},{8,0},{9,1},... | collective-permute-start | bytes 208904 | tf_op jit(solution)/shard_map/ppermute | solution.py:252
  32.1 14.5 %all-to-all-start.1 = ((bf16[16,32,256]{2,1,0:T(8,128)(2,1)}), bf16[16,32,256]{2,1,0:T(8,128)(2,1)S(1)}, u32[]{:S(2)}, u32[]{:S(2)}) async-start(bf16[16,32,256]{2,1,0:T(8,128)(2,1)} %bitcast.2), calls=%async_computation.1 | async-start | bytes 524288 | tf_op jit(solution)/shard_map/all_to_all | solution.py:246
  38.4 7.3 %collective-permute-start.4 = (bf16[136,256]{1,0:T(8,128)(2,1)S(1)}, bf16[136,256]{1,0:T(8,128)(2,1)S(1)}, u32[]{:S(2)}, u32[]{:S(2)}) collective-permute-start(bf16[136,256]{1,0:T(8,128)(2,1)S(1)} %shard_map.142.refs_0_), channel_id=1, source_target_pairs={{0,6},{1,7},{2,4},{3,5},{4,2},{5,3},{6,0},{7,1},{8,14},{9,15},{10,... | collective-permute-start | bytes 208904 | tf_op jit(solution)/shard_map/ppermute | solution.py:252
  39.1 7.4 %collective-permute-start.3 = (bf16[136,256]{1,0:T(8,128)(2,1)S(1)}, bf16[136,256]{1,0:T(8,128)(2,1)S(1)}, u32[]{:S(2)}, u32[]{:S(2)}) collective-permute-start(bf16[136,256]{1,0:T(8,128)(2,1)S(1)} %shard_map.142.refs_0_), channel_id=1, source_target_pairs={{0,4},{1,5},{2,6},{3,7},{4,0},{5,1},{6,2},{7,3},{8,12},{9,13},{10,... | collective-permute-start | bytes 208904 | tf_op jit(solution)/shard_map/ppermute | solution.py:252
  40.2 6.4 %collective-permute-start.2 = (bf16[136,256]{1,0:T(8,128)(2,1)S(1)}, bf16[136,256]{1,0:T(8,128)(2,1)S(1)}, u32[]{:S(2)}, u32[]{:S(2)}) collective-permute-start(bf16[136,256]{1,0:T(8,128)(2,1)S(1)} %shard_map.142.refs_0_), channel_id=1, source_target_pairs={{0,2},{1,3},{2,0},{3,1},{4,6},{5,7},{6,4},{7,5},{8,10},{9,11},{10,... | collective-permute-start | bytes 208904 | tf_op jit(solution)/shard_map/ppermute | solution.py:252
  46.6 1.3 %collective-permute-start.5 = (bf16[136,256]{1,0:T(8,128)(2,1)S(1)}, bf16[136,256]{1,0:T(8,128)(2,1)S(1)}, u32[]{:S(2)}, u32[]{:S(2)}) collective-permute-start(bf16[136,256]{1,0:T(8,128)(2,1)S(1)} %shard_map.143.refs_0_), channel_id=1, source_target_pairs={{0,1},{1,0},{2,3},{3,2},{4,5},{5,4},{6,7},{7,6},{8,9},{9,8},{10,11... | collective-permute-start | bytes 208904 | tf_op jit(solution)/shard_map/ppermute | solution.py:252

commit v2 on v1

--- a/solution.py
+++ b/solution.py
@@ -74,7 +74,7 @@
 
 
 def owner_kernel(near, got_ref, vectors_ref, w_qkv_hbm, w_out_hbm, _, attn_ref, d_normed_ref, *refs):
-    *outs, w_qkv_ref, w_out_ref, both_ref, sems = refs
+    *outs, w_qkv_ref, w_out_ref, both_ref, d_keys_ref, d_values_ref, sems = refs
     copies = [
         pltpu.make_async_copy(w_qkv_hbm, w_qkv_ref, sems.at[0]),
         pltpu.make_async_copy(w_out_hbm, w_out_ref, sems.at[1]),
@@ -106,17 +106,13 @@
     values_t = values.T
     keys_s = (keys.astype(F32) * scale).astype(BF16)
     lane = lax.broadcasted_iota(jnp.int32, (rows, width), 1)
-    hidden = jnp.where(points > EMPTY / 2, MASKED, 0.0).astype(BF16)
-    query_x = jnp.concatenate([query, jnp.where(lane == 0, 1.0, 0.0).astype(BF16)], axis=1)
+    hidden = jnp.where(points[:, :1] > EMPTY / 2, MASKED, 0.0)
 
     attn_t, dq_t = [], []
-    d_keys = jnp.zeros((rows, width), F32)
-    d_values = jnp.zeros((rows, width), F32)
     for h in range(HEADS):
         lo, hi = h * head, (h + 1) * head
         mine = (lane >= lo) & (lane < hi)
-        keys_h = jnp.concatenate([jnp.where(mine, keys_s, 0), hidden], axis=1)
-        scores = matmul(keys_h, query_x, ((1,), (1,)))
+        scores = matmul(jnp.where(mine, keys_s, 0), query, ((1,), (1,))) + hidden
         expo = jnp.exp(scores - jnp.max(scores, axis=0, keepdims=True))
         probs = expo * (1.0 / jnp.sum(expo, axis=0, keepdims=True))
         probs_b = probs.astype(BF16)
@@ -126,8 +122,8 @@
         d_probs = matmul(jnp.where(mine, values, 0), d_attn_s, ((1,), (1,)))
         d_score = (probs * (d_probs - inner)).astype(BF16)
         dq_t.append(matmul(keys_t[lo:hi, :], d_score))
-        d_values = jnp.where(mine, matmul(probs_b, d_attn), d_values)
-        d_keys = jnp.where(mine, matmul(d_score, query), d_keys)
+        d_values_ref[:, lo:hi] = matmul(probs_b, d_attn)[:, lo:hi]
+        d_keys_ref[:, lo:hi] = matmul(d_score, query)[:, lo:hi]
 
     attn_t = jnp.concatenate(attn_t, axis=0)
     attn_ref[...] = attn_t.T.astype(BF16)
@@ -135,7 +131,7 @@
     grad_b_out = jnp.sum(cot.astype(F32), axis=0, keepdims=True)
 
     d_query = jnp.concatenate(dq_t, axis=0).T
-    d_qkv = jnp.concatenate([d_query, d_keys, d_values], axis=1).astype(BF16)
+    d_qkv = jnp.concatenate([d_query, d_keys_ref[...], d_values_ref[...]], axis=1).astype(BF16)
     d_normed = matmul(d_qkv, w_qkv, ((1,), (1,)))
     grad_w_qkv = matmul(normed, d_qkv, ((0,), (0,)))
     grad_b_qkv = jnp.sum(d_qkv.astype(F32), axis=0, keepdims=True)
@@ -301,6 +297,8 @@
             pltpu.VMEM(w_qkv.shape, w_qkv.dtype),
             pltpu.VMEM(w_out.shape, w_out.dtype),
             pltpu.VMEM((2 * width, 2 * width), F32),
+            pltpu.VMEM((held, width), F32),
+            pltpu.VMEM((held, width), F32),
             pltpu.SemaphoreType.DMA((2,)),
         ],
         compiler_params=LARGE,

time: 49.1 us -> 49.1 us (level)
  no operation moved by 1% of the time
where the time goes in v2:
time: 49.1 us; the launch traced here: 48.7 us
  waiting for transfers between devices  16.7 us (34%)
  starting transfers between devices  15.9 us (32%)
  Pallas kernels  15.2 us (31%)
  between operations  0.81 us (2%)
    all_to_all x2, starting transfers between devices, exchange(): lax.all_to_all(message, 'seq', split_axis=0, concat_axis=0, axis_index_gr...  11.6 us
    pallas_call x1, Pallas kernels, local(): pl.pallas_call(functools.partial(owner_kernel, near), out_shape=(shape(he...  9.87 us
    all_to_all x2, waiting for transfers between devices, exchange(): lax.all_to_all(message, 'seq', split_axis=0, concat_axis=0, axis_index_gr...  9.48 us
    ppermute x6, waiting for transfers between devices, swap(): lax.ppermute(piece, 'seq', [(dev, dev ^ step) for dev in range(devs)])  7.25 us
    ppermute x6, starting transfers between devices, swap(): lax.ppermute(piece, 'seq', [(dev, dev ^ step) for dev in range(devs)])  4.35 us
    pallas_call x1, Pallas kernels, local(): pl.pallas_call(functools.partial(scatter_kernel, block_rows), out_shape=s...  1.9 us
    pallas_call x1, Pallas kernels, local(): pl.pallas_call(rows_kernel, out_shape=(shape(held, 2 * width), shape(8, 1...  1.09 us
  transfers between devices with their start and end apart: 8, of which 6 were waited for; matrix products, arithmetic and copies ran while one was open for 0% of the time, Pallas kernels for 5%

profile of v2, /device:TPU:0, one launch (start us, length us, event | category | flops | bytes accessed | tf_op | source)
XLA Modules:
  0.0 48.7 jit_solution(11413829167489528832)
XLA Ops:
  0.6 1.9 %shard_map.136 = bf16[512,256]{1,0:T(8,128)(2,1)} custom-call(s32[2,8]{1,0:T(2,128)} %route_hbm.3, bf16[256,128]{1,0:T(8,128)(2,1)} %points_hbm.1, bf16[256,128]{1,0:T(8,128)(2,1)} %cot_hbm.1), custom_call_target="tpu_custom_call" | custom-call | tf_op jit(solution)/shard_map/pallas_call | solution.py:262
  2.5 0.0 copy-start.2
  2.6 0.0 copy-start.3
  2.6 0.0 copy-start
  2.6 0.0 copy-start.1
  2.6 7.5 %all-to-all-start = ((bf16[16,32,256]{2,1,0:T(8,128)(2,1)}), bf16[16,32,256]{2,1,0:T(8,128)(2,1)S(1)}, u32[]{:S(2)}, u32[]{:S(2)}) async-start(bf16[16,32,256]{2,1,0:T(8,128)(2,1)} %bitcast.7), calls=%async_computation | async-start | bytes 524288 | tf_op jit(solution)/shard_map/all_to_all | solution.py:242
  10.1 0.0 copy-done.2
  10.1 0.0 copy-start.4
  10.1 0.0 copy-start.5
  10.1 0.6 %shard_map.135 = (bf16[256,512]{1,0:T(8,128)(2,1)S(1)}, f32[8,128]{1,0:T(8,128)S(1)}) custom-call(s32[2,8]{1,0:T(2,128)S(1)} %copy-done.2), custom_call_target="tpu_custom_call" | custom-call | tf_op jit(solution)/shard_map/pallas_call | solution.py:276
  10.8 0.0 copy-done.3
  10.8 0.0 copy-done.4
  10.8 0.0 copy-done.5
  10.8 9.5 %all-to-all-done = bf16[16,32,256]{2,1,0:T(8,128)(2,1)S(1)} async-done(((bf16[16,32,256]{2,1,0:T(8,128)(2,1)}), bf16[16,32,256]{2,1,0:T(8,128)(2,1)S(1)}, u32[]{:S(2)}, u32[]{:S(2)}) %all-to-all-start) | async-done | bytes 262176 | tf_op jit(solution)/shard_map/all_to_all | solution.py:242
  20.3 0.0 copy-done
  20.3 0.0 copy-done.1
  20.3 9.9 %shard_map.137 = (bf16[512,128]{1,0:T(8,128)(2,1)S(1)}, f32[512,128]{1,0:T(8,128)S(1)}, bf16[136,256]{1,0:T(8,128)(2,1)S(1)}, bf16[136,256]{1,0:T(8,128)(2,1)S(1)}) custom-call(bf16[512,256]{1,0:T(8,128)(2,1)S(1)} %bitcast.5, f32[1,640]{1,0:T(1,128)S(1)} %broadcast_in_dim.3.vectors_ref, bf16[128,384]{1,0:T(8,128)(2,1)S(1)} %copy-done, ...), custom_call_target="tpu_custom_call" | custom-call | tf_op jit(solution)/shard_map/pallas_call | solution.py:291
  30.2 0.1 collective-permute-start
  30.3 1.1 %shard_map.138 = (bf16[512,256]{1,0:T(8,128)(2,1)}, f32[8,128]{1,0:T(8,128)S(1)}) custom-call(bf16[512,256]{1,0:T(8,128)(2,1)S(1)} %bitcast.6, bf16[512,128]{1,0:T(8,128)(2,1)S(1)} %get-tuple-element.25.attn_ref, f32[512,128]{1,0:T(8,128)S(1)} %get-tuple-element.26.d_normed_ref, f32[1,640]{1,0:T(1,128)S(1)} %broadcast_in_dim.3.vectors_ref, ...), custom_call_target="tpu_custom_call" | custom-call | flops 536870912 | bytes 1048576 | tf_op jit(solution)/shard_map/pallas_call | solution.py:306
  31.3 0.2 collective-permute-done.refs_1_
  31.5 0.7 %collective-permute-start.1 = (bf16[136,256]{1,0:T(8,128)(2,1)S(1)}, bf16[136,256]{1,0:T(8,128)(2,1)S(1)}, u32[]{:S(2)}, u32[]{:S(2)}) collective-permute-start(bf16[136,256]{1,0:T(8,128)(2,1)S(1)} %shard_map.139.other_ref.refs_0_), channel_id=1, source_target_pairs={{0,8},{1,9},{2,10},{3,11},{4,12},{5,13},{6,14},{7,15},{8,0},{9,1},... | collective-permute-start | bytes 208904 | tf_op jit(solution)/shard_map/ppermute | solution.py:248
  32.2 4.1 %all-to-all-start.1 = ((bf16[16,32,256]{2,1,0:T(8,128)(2,1)}), bf16[16,32,256]{2,1,0:T(8,128)(2,1)S(1)}, u32[]{:S(2)}, u32[]{:S(2)}) async-start(bf16[16,32,256]{2,1,0:T(8,128)(2,1)} %bitcast.2), calls=%async_computation.1 | async-start | bytes 524288 | tf_op jit(solution)/shard_map/all_to_all | solution.py:242
  36.3 2.2 %collective-permute-done.1.refs_1_ = bf16[136,256]{1,0:T(8,128)(2,1)S(1)} collective-permute-done((bf16[136,256]{1,0:T(8,128)(2,1)S(1)}, bf16[136,256]{1,0:T(8,128)(2,1)S(1)}, u32[]{:S(2)}, u32[]{:S(2)}) %collective-permute-start.1) | collective-permute-done | bytes 69664 | tf_op jit(solution)/shard_map/ppermute | solution.py:248
  38.4 0.7 %collective-permute-start.4 = (bf16[136,256]{1,0:T(8,128)(2,1)S(1)}, bf16[136,256]{1,0:T(8,128)(2,1)S(1)}, u32[]{:S(2)}, u32[]{:S(2)}) collective-permute-start(bf16[136,256]{1,0:T(8,128)(2,1)S(1)} %shard_map.142.refs_0_), channel_id=1, source_target_pairs={{0,6},{1,7},{2,4},{3,5},{4,2},{5,3},{6,0},{7,1},{8,14},{9,15},{10,... | collective-permute-start | bytes 208904 | tf_op jit(solution)/shard_map/ppermute | solution.py:248
  39.2 1.0 %collective-permute-start.3 = (bf16[136,256]{1,0:T(8,128)(2,1)S(1)}, bf16[136,256]{1,0:T(8,128)(2,1)S(1)}, u32[]{:S(2)}, u32[]{:S(2)}) collective-permute-start(bf16[136,256]{1,0:T(8,128)(2,1)S(1)} %shard_map.142.refs_0_), channel_id=1, source_target_pairs={{0,4},{1,5},{2,6},{3,7},{4,0},{5,1},{6,2},{7,3},{8,12},{9,13},{10,... | collective-permute-start | bytes 208904 | tf_op jit(solution)/shard_map/ppermute | solution.py:248
  40.2 1.8 %collective-permute-start.2 = (bf16[136,256]{1,0:T(8,128)(2,1)S(1)}, bf16[136,256]{1,0:T(8,128)(2,1)S(1)}, u32[]{:S(2)}, u32[]{:S(2)}) collective-permute-start(bf16[136,256]{1,0:T(8,128)(2,1)S(1)} %shard_map.142.refs_0_), channel_id=1, source_target_pairs={{0,2},{1,3},{2,0},{3,1},{4,6},{5,7},{6,4},{7,5},{8,10},{9,11},{10,... | collective-permute-start | bytes 208904 | tf_op jit(solution)/shard_map/ppermute | solution.py:248
  42.0 3.7 %collective-permute-done.4.refs_3_ = bf16[136,256]{1,0:T(8,128)(2,1)S(1)} collective-permute-done((bf16[136,256]{1,0:T(8,128)(2,1)S(1)}, bf16[136,256]{1,0:T(8,128)(2,1)S(1)}, u32[]{:S(2)}, u32[]{:S(2)}) %collective-permute-start.4) | collective-permute-done | bytes 69664 | tf_op jit(solution)/shard_map/ppermute | solution.py:248
  45.7 0.9 %collective-permute-done.3.refs_2_ = bf16[136,256]{1,0:T(8,128)(2,1)S(1)} collective-permute-done((bf16[136,256]{1,0:T(8,128)(2,1)S(1)}, bf16[136,256]{1,0:T(8,128)(2,1)S(1)}, u32[]{:S(2)}, u32[]{:S(2)}) %collective-permute-start.3) | collective-permute-done | bytes 69664 | tf_op jit(solution)/shard_map/ppermute | solution.py:248
  46.6 0.0 collective-permute-done.2.refs_1_
  46.6 0.1 collective-permute-start.5
  46.7 0.0 all-to-all-done.1
  46.7 0.9 %shard_map.141 = (bf16[256,128]{1,0:T(8,128)(2,1)}, bf16[256,128]{1,0:T(8,128)(2,1)}, f32[8,128]{1,0:T(8,128)S(1)}) custom-call(bf16[256,512]{1,0:T(8,128)(2,1)S(1)} %get-tuple-element.23.pick_ref, bf16[512,256]{1,0:T(8,128)(2,1)S(1)} %bitcast.4), custom_call_target="tpu_custom_call" | custom-call | tf_op jit(solution)/shard_map/pallas_call | solution.py:318
  47.6 0.3 collective-permute-done.5.refs_1_
  48.0 0.7 %shard_map.144 = (f32[128]{0:T(128)}, f32[128,384]{1,0:T(8,128)}, f32[384]{0:T(512)}, f32[128,128]{1,0:T(8,128)}, f32[128]{0:T(128)}) custom-call(bf16[136,256]{1,0:T(8,128)(2,1)S(1)} %shard_map.143.refs_0_, bf16[136,256]{1,0:T(8,128)(2,1)S(1)} %collective-permute-done.5.refs_1_, f32[8,128]{1,0:T(8,128)S(1)} %get-tuple-element.33.refs_2_), custom_call_target="tpu_custom_call" | custom-call | tf_op jit(solution)/shard_map/pallas_call | solution.py:354
  (6 shorter events, 0.1 us)
Async XLA Ops:
  2.5 7.6 %copy-start.2 = (s32[2,8]{1,0:T(2,128)S(1)}, s32[2,8]{1,0:T(2,128)}, u32[]{:S(2)}) copy-start(s32[2,8]{1,0:T(2,128)} %route_hbm.3) | copy-start | bytes 196
  2.6 8.2 %copy-start.3 = (f32[384]{0:T(512)S(1)}, f32[384]{0:T(512)}, u32[]{:S(2)}) copy-start(f32[384]{0:T(512)} %param.14) | copy-start | bytes 4612
  2.6 17.7 %copy-start = (bf16[128,384]{1,0:T(8,128)(2,1)S(1)}, bf16[128,384]{1,0:T(8,128)(2,1)}, u32[]{:S(2)}) copy-start(bf16[128,384]{1,0:T(8,128)(2,1)} %w_qkv_hbm.1) | copy-start | bytes 294916
  2.6 17.7 %copy-start.1 = (bf16[128,128]{1,0:T(8,128)(2,1)S(1)}, bf16[128,128]{1,0:T(8,128)(2,1)}, u32[]{:S(2)}) copy-start(bf16[128,128]{1,0:T(8,128)(2,1)} %w_out_ref.1) | copy-start | bytes 98308
  2.6 17.7 %all-to-all-start = ((bf16[16,32,256]{2,1,0:T(8,128)(2,1)}), bf16[16,32,256]{2,1,0:T(8,128)(2,1)S(1)}, u32[]{:S(2)}, u32[]{:S(2)}) async-start(bf16[16,32,256]{2,1,0:T(8,128)(2,1)} %bitcast.7), calls=%async_computation | async-start | bytes 524288 | tf_op jit(solution)/shard_map/all_to_all | solution.py:242
  10.1 0.7 %copy-start.4 = (f32[128]{0:T(128)S(1)}, f32[128]{0:T(128)}, u32[]{:S(2)}) copy-start(f32[128]{0:T(128)} %param.16) | copy-start | bytes 1540
  10.1 0.7 %copy-start.5 = (f32[128]{0:T(128)S(1)}, f32[128]{0:T(128)}, u32[]{:S(2)}) copy-start(f32[128]{0:T(128)} %param.12) | copy-start | bytes 1540
  30.2 1.3 %collective-permute-start = (bf16[136,256]{1,0:T(8,128)(2,1)S(1)}, bf16[136,256]{1,0:T(8,128)(2,1)S(1)}, u32[]{:S(2)}, u32[]{:S(2)}) collective-permute-start(bf16[136,256]{1,0:T(8,128)(2,1)S(1)} %get-tuple-element.29), channel_id=1, source_target_pairs={{0,1},{1,0},{2,3},{3,2},{4,5},{5,4},{6,7},{7,6},{8,9},{9,8},{10,11... | collective-permute-start | bytes 208904 | tf_op jit(solution)/shard_map/ppermute | solution.py:248
  31.5 6.9 %collective-permute-start.1 = (bf16[136,256]{1,0:T(8,128)(2,1)S(1)}, bf16[136,256]{1,0:T(8,128)(2,1)S(1)}, u32[]{:S(2)}, u32[]{:S(2)}) collective-permute-start(bf16[136,256]{1,0:T(8,128)(2,1)S(1)} %shard_map.139.other_ref.refs_0_), channel_id=1, source_target_pairs={{0,8},{1,9},{2,10},{3,11},{4,12},{5,13},{6,14},{7,15},{8,0},{9,1},... | collective-permute-start | bytes 208904 | tf_op jit(solution)/shard_map/ppermute | solution.py:248
  32.2 14.5 %all-to-all-start.1 = ((bf16[16,32,256]{2,1,0:T(8,128)(2,1)}), bf16[16,32,256]{2,1,0:T(8,128)(2,1)S(1)}, u32[]{:S(2)}, u32[]{:S(2)}) async-start(bf16[16,32,256]{2,1,0:T(8,128)(2,1)} %bitcast.2), calls=%async_computation.1 | async-start | bytes 524288 | tf_op jit(solution)/shard_map/all_to_all | solution.py:242
  38.4 7.3 %collective-permute-start.4 = (bf16[136,256]{1,0:T(8,128)(2,1)S(1)}, bf16[136,256]{1,0:T(8,128)(2,1)S(1)}, u32[]{:S(2)}, u32[]{:S(2)}) collective-permute-start(bf16[136,256]{1,0:T(8,128)(2,1)S(1)} %shard_map.142.refs_0_), channel_id=1, source_target_pairs={{0,6},{1,7},{2,4},{3,5},{4,2},{5,3},{6,0},{7,1},{8,14},{9,15},{10,... | collective-permute-start | bytes 208904 | tf_op jit(solution)/shard_map/ppermute | solution.py:248
  39.2 7.4 %collective-permute-start.3 = (bf16[136,256]{1,0:T(8,128)(2,1)S(1)}, bf16[136,256]{1,0:T(8,128)(2,1)S(1)}, u32[]{:S(2)}, u32[]{:S(2)}) collective-permute-start(bf16[136,256]{1,0:T(8,128)(2,1)S(1)} %shard_map.142.refs_0_), channel_id=1, source_target_pairs={{0,4},{1,5},{2,6},{3,7},{4,0},{5,1},{6,2},{7,3},{8,12},{9,13},{10,... | collective-permute-start | bytes 208904 | tf_op jit(solution)/shard_map/ppermute | solution.py:248
  40.2 6.4 %collective-permute-start.2 = (bf16[136,256]{1,0:T(8,128)(2,1)S(1)}, bf16[136,256]{1,0:T(8,128)(2,1)S(1)}, u32[]{:S(2)}, u32[]{:S(2)}) collective-permute-start(bf16[136,256]{1,0:T(8,128)(2,1)S(1)} %shard_map.142.refs_0_), channel_id=1, source_target_pairs={{0,2},{1,3},{2,0},{3,1},{4,6},{5,7},{6,4},{7,5},{8,10},{9,11},{10,... | collective-permute-start | bytes 208904 | tf_op jit(solution)/shard_map/ppermute | solution.py:248
  46.6 1.3 %collective-permute-start.5 = (bf16[136,256]{1,0:T(8,128)(2,1)S(1)}, bf16[136,256]{1,0:T(8,128)(2,1)S(1)}, u32[]{:S(2)}, u32[]{:S(2)}) collective-permute-start(bf16[136,256]{1,0:T(8,128)(2,1)S(1)} %shard_map.143.refs_0_), channel_id=1, source_target_pairs={{0,1},{1,0},{2,3},{3,2},{4,5},{5,4},{6,7},{7,6},{8,9},{9,8},{10,11... | collective-permute-start | bytes 208904 | tf_op jit(solution)/shard_map/ppermute | solution.py:248

commit v3 on v2

--- a/solution.py
+++ b/solution.py
@@ -35,17 +35,18 @@
     return place
 
 
-def send_rows(route_ref, shape, axis, block_rows, devs):
+def send_rows(route_ref, shape, axis, block_rows, place_of):
     place = lax.broadcasted_iota(jnp.int32, shape, axis)
     target = jnp.zeros(shape, jnp.int32)
     for block in range(shape[axis] // block_rows):
         first = block * block_rows
-        moved = turned(route_ref[0, block], devs) * block_rows + place - first
+        moved = place_of(route_ref[0, block]) * block_rows + place - first
         target = jnp.where(place >= first, moved, target)
     return target
 
 
-def scatter_kernel(block_rows, route_hbm, points_hbm, cot_hbm, out_ref, route_ref, points_ref, cot_ref, sems):
+def scatter_kernel(block_rows, route_hbm, points_hbm, cot_hbm, *refs):
+    *outs, route_ref, points_ref, cot_ref, sems = refs
     copies = [
         pltpu.make_async_copy(source, target, sems.at[at])
         for at, (source, target) in enumerate(
@@ -57,14 +58,33 @@
     for copy in copies:
         copy.wait()
     rows, width = points_ref.shape
-    target = send_rows(route_ref, (1, rows), 1, block_rows, out_ref.shape[0] // block_rows)
-    index = lax.broadcasted_iota(jnp.int32, (out_ref.shape[0], rows), 0)
+    part = outs[0].shape[0]
+    held = part * len(outs)
+    if len(outs) > 1:
+        me = lax.axis_index("seq")
+        target = send_rows(route_ref, (1, rows), 1, block_rows, lambda owner: owner ^ me)
+    else:
+        devs = held // block_rows
+        target = send_rows(route_ref, (1, rows), 1, block_rows, lambda owner: turned(owner, devs))
+    index = lax.broadcasted_iota(jnp.int32, (held, rows), 0)
     pick = jnp.where(index == target, 1.0, 0.0).astype(BF16)
     ones = jnp.ones((rows, width), BF16)
     moved = matmul(pick, jnp.concatenate([points_ref[...], ones], axis=1))
     empty = (1.0 - moved[:, width:]) * EMPTY
-    out_ref[:, :width] = (moved[:, :width] + empty).astype(BF16)
-    out_ref[:, width:] = matmul(pick, cot_ref[...]).astype(BF16)
+    points = (moved[:, :width] + empty).astype(BF16)
+    cot = matmul(pick, cot_ref[...]).astype(BF16)
+    for at, out_ref in enumerate(outs):
+        span = slice(at * part, (at + 1) * part)
+        out_ref[:, :width] = points[span]
+        out_ref[:, width:] = cot[span]
+
+
+def regroup_kernel(block_rows, *refs):
+    count = len(refs) // 2
+    for high, got_ref in enumerate(refs[:count]):
+        for low, out_ref in enumerate(refs[count:]):
+            block = got_ref[low * block_rows : (low + 1) * block_rows]
+            out_ref[high * block_rows : (high + 1) * block_rows] = block
 
 
 def normalize(points):
@@ -73,7 +93,9 @@
     return centered * rstd, rstd
 
 
-def owner_kernel(near, got_ref, vectors_ref, w_qkv_hbm, w_out_hbm, _, attn_ref, d_normed_ref, *refs):
+def owner_kernel(near, *refs):
+    got_refs, refs = refs[:near], refs[near:]
+    vectors_ref, w_qkv_hbm, w_out_hbm, _, attn_ref, d_normed_ref, *refs = refs
     *outs, w_qkv_ref, w_out_ref, both_ref, d_keys_ref, d_values_ref, sems = refs
     copies = [
         pltpu.make_async_copy(w_qkv_hbm, w_qkv_ref, sems.at[0]),
@@ -81,15 +103,15 @@
     ]
     for copy in copies:
         copy.start()
-    rows = got_ref.shape[0]
-    width = got_ref.shape[1] // 2
+    got = jnp.concatenate([got_ref[...] for got_ref in got_refs], axis=0)
+    rows, width = got.shape[0], got.shape[1] // 2
     head = width // HEADS
     scale = head ** (-0.5)
     gain = vectors_ref[:, :width]
     b_qkv = vectors_ref[:, 2 * width :]
 
-    points = got_ref[:, :width].astype(F32)
-    cot = got_ref[:, width:]
+    points = got[:, :width].astype(F32)
+    cot = got[:, width:]
     xhat, _ = normalize(points)
     normed = (xhat * gain).astype(BF16)
     for copy in copies:
@@ -164,13 +186,16 @@
         half_ref[width:] = sums.astype(half_ref.dtype)
 
 
-def rows_kernel(got_ref, attn_ref, d_normed_ref, vectors_ref, w_out_ref, back_ref, token_ref):
+def rows_kernel(near, block_rows, *refs):
+    got_refs, refs = refs[:near], refs[near:]
+    attn_ref, d_normed_ref, vectors_ref, w_out_ref, back_ref, token_ref = refs
     token_ref[...] = jnp.zeros_like(token_ref)
     width = attn_ref.shape[1]
     gain = vectors_ref[:, :width]
     b_out = vectors_ref[:, width : 2 * width]
-    points = got_ref[:, :width].astype(F32)
-    cot = got_ref[:, width:].astype(F32)
+    got = jnp.concatenate([got_ref[...] for got_ref in got_refs], axis=0)
+    points = got[:, :width].astype(F32)
+    cot = got[:, width:].astype(F32)
     xhat, rstd = normalize(points)
     mixed = points + (matmul(attn_ref[...], w_out_ref[...]) + b_out)
     d_xhat = d_normed_ref[...] * gain
@@ -179,8 +204,20 @@
         - jnp.mean(d_xhat, axis=-1, keepdims=True)
         - xhat * jnp.mean(d_xhat * xhat, axis=-1, keepdims=True)
     )
-    back_ref[:, :width] = mixed.astype(BF16)
-    back_ref[:, width:] = (cot + rstd * inner).astype(BF16)
+    mixed = mixed.astype(BF16)
+    grad = (cot + rstd * inner).astype(BF16)
+    if near == 1:
+        back_ref[:, :width] = mixed
+        back_ref[:, width:] = grad
+        return
+    me = lax.axis_index("seq")
+    devs = got.shape[0] // block_rows
+    for at in range(devs):
+        source = me ^ (at % (devs // near) * near + at // (devs // near))
+        held = slice(at * block_rows, (at + 1) * block_rows)
+        span = pl.ds(pl.multiple_of(turned(source, devs) * block_rows, block_rows), block_rows)
+        back_ref[span, :width] = mixed[held]
+        back_ref[span, width:] = grad[held]
 
 
 def sum_kernel(count, *refs):
@@ -201,7 +238,8 @@
     copy.start()
     copy.wait()
     rows, held = pick_ref.shape
-    target = send_rows(route_ref, (rows, 1), 0, block_rows, held // block_rows)
+    devs = held // block_rows
+    target = send_rows(route_ref, (rows, 1), 0, block_rows, lambda owner: turned(owner, devs))
     index = lax.broadcasted_iota(jnp.int32, pick_ref.shape, 1)
     pick_ref[...] = jnp.where(index == target, 1.0, 0.0).astype(BF16)
 
@@ -261,9 +299,9 @@
 
     sent = pl.pallas_call(
         functools.partial(scatter_kernel, block_rows),
-        out_shape=shape(held, 2 * width),
+        out_shape=(shape(held // near, 2 * width),) * near,
         in_specs=[ANY] * 3,
-        out_specs=VMEM,
+        out_specs=(VMEM,) * near,
         scratch_shapes=[
             pltpu.SMEM(route.shape, route.dtype),
             pltpu.VMEM(points.shape, points.dtype),
@@ -271,7 +309,18 @@
             pltpu.SemaphoreType.DMA((3,)),
         ],
     )(route, points, cotangent)
-    got = exchange(sent.reshape(devs, block_rows, 2 * width)).reshape(held, 2 * width)
+    if near > 1:
+        got = [sent[0]] + [swap(sent[step], near * step, devs) for step in range(1, near)]
+        got = pl.pallas_call(
+            functools.partial(regroup_kernel, block_rows),
+            out_shape=(shape(held // near, 2 * width),) * near,
+            in_specs=[VMEM] * near,
+            out_specs=(VMEM,) * near,
+            compiler_params=SMALL,
+        )(*got)
+        got = [got[0]] + [swap(got[step], step, devs) for step in range(1, near)]
+    else:
+        got = [exchange(sent[0].reshape(devs, block_rows, 2 * width)).reshape(held, 2 * width)]
 
     pick, early = pl.pallas_call(
         functools.partial(pick_kernel, block_rows),
@@ -291,7 +340,7 @@
     attn, d_normed, *parts = pl.pallas_call(
         functools.partial(owner_kernel, near),
         out_shape=(shape(held, width), shape(held, width, dtype=F32)) + sums_shapes,
-        in_specs=[VMEM, VMEM, ANY, ANY, VMEM],
+        in_specs=[VMEM] * (near + 1) + [ANY, ANY, VMEM],
         out_specs=(VMEM,) * (2 + len(sums_shapes)),
         scratch_shapes=[
             pltpu.VMEM(w_qkv.shape, w_qkv.dtype),
@@ -302,17 +351,17 @@
             pltpu.SemaphoreType.DMA((2,)),
         ],
         compiler_params=LARGE,
-    )(got, vectors, w_qkv, w_out, early)
+    )(*got, vectors, w_qkv, w_out, early)
     back, token = pl.pallas_call(
-        rows_kernel,
+        functools.partial(rows_kernel, near, block_rows),
         out_shape=(shape(held, 2 * width), shape(8, 128, dtype=F32)),
-        in_specs=[VMEM] * 5,
+        in_specs=[VMEM] * (near + 4),
         out_specs=(VMEM,) * 2,
         compiler_params=SMALL,
         cost_estimate=pl.CostEstimate(
             flops=64 * held * width * width, bytes_accessed=16 * held * width, transcendentals=0
         ),
-    )(got, attn, d_normed, vectors, w_out)
+    )(*got, attn, d_normed, vectors, w_out)
 
     def give_back(back):
         return pl.pallas_call(

time: 49.1 us -> 50.2 us (1.022)
  local copies, waits for them, and re-layouts: 0.04 us -> 0.87 us
  starting transfers between devices: 15.9 us -> 16.7 us
    all_to_all x2 -> x1, waiting for transfers between devices: 9.48 us -> 0.01 us  [exchange(): lax.all_to_all(message, 'seq', split_axis=0, concat_axis=0, axis_index_gr...]
    ppermute x6 -> x12, waiting for transfers between devices: 7.25 us -> 16.5 us  [swap(): lax.ppermute(piece, 'seq', [(dev, dev ^ step) for dev in range(devs)])]
    ppermute x6 -> x12, starting transfers between devices: 4.35 us -> 13.1 us  [swap(): lax.ppermute(piece, 'seq', [(dev, dev ^ step) for dev in range(devs)])]
    all_to_all x2 -> x1, starting transfers between devices: 11.6 us -> 3.59 us  [exchange(): lax.all_to_all(message, 'seq', split_axis=0, concat_axis=0, axis_index_gr...]
    unnamed x12 -> x14, local copies, waits for them, and re-layouts: 0.04 us -> 0.87 us
    pallas_call x2 -> x3, Pallas kernels: 3 us -> 2.94 us  [the longest x1 1.83 us: local(): pl.pallas_call(functools.partial(scatter_kernel, block_rows), out_shape=(...]
  transfers between devices with their start and end apart: 8 -> 13, of which waited for: 6 -> 8; matrix products, arithmetic and copies ran while one was open for 0% -> 0% of each run, Pallas kernels for 5% -> 5%
where the time goes in v3:
time: 50.2 us; the launch traced here: 49.9 us
  starting transfers between devices  16.7 us (33%)
  waiting for transfers between devices  16.5 us (33%)
  Pallas kernels  15.1 us (30%)
  local copies, waits for them, and re-layouts  0.87 us (2%)
  between operations  0.77 us (2%)
    ppermute x12, waiting for transfers between devices, swap(): lax.ppermute(piece, 'seq', [(dev, dev ^ step) for dev in range(devs)])  16.5 us
    ppermute x12, starting transfers between devices, swap(): lax.ppermute(piece, 'seq', [(dev, dev ^ step) for dev in range(devs)])  13.1 us
    pallas_call x1, Pallas kernels, local(): pl.pallas_call(functools.partial(owner_kernel, near), out_shape=(shape(he...  9.86 us
    all_to_all x1, starting transfers between devices, exchange(): lax.all_to_all(message, 'seq', split_axis=0, concat_axis=0, axis_index_gr...  3.59 us
    pallas_call x1, Pallas kernels, local(): pl.pallas_call(functools.partial(scatter_kernel, block_rows), out_shape=(...  1.83 us
    pallas_call x1, Pallas kernels, local(): pl.pallas_call(functools.partial(rows_kernel, near, block_rows), out_shap...  1.09 us
  transfers between devices with their start and end apart: 13, of which 8 were waited for; matrix products, arithmetic and copies ran while one was open for 0% of the time, Pallas kernels for 5%

profile of v3, /device:TPU:0, one launch (start us, length us, event | category | flops | bytes accessed | tf_op | source)
XLA Modules:
  0.0 49.9 jit_solution(12313073481148639662)
XLA Ops:
  0.6 1.8 %shard_map.136 = (bf16[128,256]{1,0:T(8,128)(2,1)}, bf16[128,256]{1,0:T(8,128)(2,1)}, bf16[128,256]{1,0:T(8,128)(2,1)}, bf16[128,256]{1,0:T(8,128)(2,1)}) custom-call(s32[2,8]{1,0:T(2,128)} %route_hbm.3, bf16[256,128]{1,0:T(8,128)(2,1)} %points_hbm.1, bf16[256,128]{1,0:T(8,128)(2,1)} %cot_hbm.1), custom_call_target="tpu_custom_call" | custom-call | tf_op jit(solution)/shard_map/pallas_call | solution.py:300
  2.5 3.1 %collective-permute-start = (bf16[128,256]{1,0:T(8,128)(2,1)}, bf16[128,256]{1,0:T(8,128)(2,1)S(1)}, u32[]{:S(2)}, u32[]{:S(2)}) collective-permute-start(bf16[128,256]{1,0:T(8,128)(2,1)} %get-tuple-element.33), channel_id=1, source_target_pairs={{0,4},{1,5},{2,6},{3,7},{4,0},{5,1},{6,2},{7,3},{8,12},{9,13},{10,... | collective-permute-start | bytes 196616 | tf_op jit(solution)/shard_map/ppermute | solution.py:286
  5.6 0.0 copy-start.3
  5.6 2.6 %collective-permute-start.1 = (bf16[128,256]{1,0:T(8,128)(2,1)}, bf16[128,256]{1,0:T(8,128)(2,1)S(1)}, u32[]{:S(2)}, u32[]{:S(2)}) collective-permute-start(bf16[128,256]{1,0:T(8,128)(2,1)} %get-tuple-element.34), channel_id=1, source_target_pairs={{0,8},{1,9},{2,10},{3,11},{4,12},{5,13},{6,14},{7,15},{8,0},{9,1},... | collective-permute-start | bytes 196616 | tf_op jit(solution)/shard_map/ppermute | solution.py:286
  8.2 0.0 collective-permute-start.2
  8.2 0.0 copy-done.3
  8.2 0.6 %shard_map.135 = (bf16[256,512]{1,0:T(8,128)(2,1)S(1)}, f32[8,128]{1,0:T(8,128)S(1)}) custom-call(s32[2,8]{1,0:T(2,128)S(1)} %copy-done.3), custom_call_target="tpu_custom_call" | custom-call | tf_op jit(solution)/shard_map/pallas_call | solution.py:325
  8.8 0.0 collective-permute-done.refs_1_
  8.8 4.2 %collective-permute-done.1.refs_2_ = bf16[128,256]{1,0:T(8,128)(2,1)S(1)} collective-permute-done((bf16[128,256]{1,0:T(8,128)(2,1)}, bf16[128,256]{1,0:T(8,128)(2,1)S(1)}, u32[]{:S(2)}, u32[]{:S(2)}) %collective-permute-start.1) | collective-permute-done | bytes 65568 | tf_op jit(solution)/shard_map/ppermute | solution.py:286
  13.0 1.4 %collective-permute-done.2.refs_3_ = bf16[128,256]{1,0:T(8,128)(2,1)S(1)} collective-permute-done((bf16[128,256]{1,0:T(8,128)(2,1)}, bf16[128,256]{1,0:T(8,128)(2,1)S(1)}, u32[]{:S(2)}, u32[]{:S(2)}) %collective-permute-start.2) | collective-permute-done | bytes 65568 | tf_op jit(solution)/shard_map/ppermute | solution.py:286
  14.4 0.0 copy-start.1
  14.4 0.8 %copy-done.1 = bf16[128,256]{1,0:T(8,128)(2,1)S(1)} copy-done((bf16[128,256]{1,0:T(8,128)(2,1)S(1)}, bf16[128,256]{1,0:T(8,128)(2,1)}, u32[]{:S(2)}) %copy-start.1) | copy-done | bytes 65560
  15.3 0.0 copy-start
  15.3 0.0 copy-start.2
  15.3 0.0 copy-start.4
  15.3 0.1 collective-permute-start.3
  15.4 0.0 copy-start.5
  15.4 0.0 copy-start.6
  15.4 1.6 %collective-permute-start.4 = (bf16[128,256]{1,0:T(8,128)(2,1)S(1)}, bf16[128,256]{1,0:T(8,128)(2,1)S(1)}, u32[]{:S(2)}, u32[]{:S(2)}) collective-permute-start(bf16[128,256]{1,0:T(8,128)(2,1)S(1)} %get-tuple-element.38), channel_id=1, source_target_pairs={{0,2},{1,3},{2,0},{3,1},{4,6},{5,7},{6,4},{7,5},{8,10},{9,11},{10,... | collective-permute-start | bytes 196616 | tf_op jit(solution)/shard_map/ppermute | solution.py:286
  17.0 0.3 collective-permute-start.5
  17.3 0.0 copy-done.4
  17.3 0.0 copy-done.5
  17.3 0.0 copy-done.6
  17.3 0.0 collective-permute-done.3.refs_1_
  17.3 2.6 %collective-permute-done.4.refs_2_ = bf16[128,256]{1,0:T(8,128)(2,1)S(1)} collective-permute-done((bf16[128,256]{1,0:T(8,128)(2,1)S(1)}, bf16[128,256]{1,0:T(8,128)(2,1)S(1)}, u32[]{:S(2)}, u32[]{:S(2)}) %collective-permute-start.4) | collective-permute-done | bytes 65568 | tf_op jit(solution)/shard_map/ppermute | solution.py:286
  19.9 1.1 %collective-permute-done.5.refs_3_ = bf16[128,256]{1,0:T(8,128)(2,1)S(1)} collective-permute-done((bf16[128,256]{1,0:T(8,128)(2,1)S(1)}, bf16[128,256]{1,0:T(8,128)(2,1)S(1)}, u32[]{:S(2)}, u32[]{:S(2)}) %collective-permute-start.5) | collective-permute-done | bytes 65568 | tf_op jit(solution)/shard_map/ppermute | solution.py:286
  21.0 0.0 copy-done
  21.0 0.0 copy-done.2
  21.0 9.9 %shard_map.138 = (bf16[512,128]{1,0:T(8,128)(2,1)S(1)}, f32[512,128]{1,0:T(8,128)S(1)}, bf16[136,256]{1,0:T(8,128)(2,1)S(1)}, bf16[136,256]{1,0:T(8,128)(2,1)S(1)}) custom-call(bf16[128,256]{1,0:T(8,128)(2,1)S(1)} %get-tuple-element.36.refs_0_, bf16[128,256]{1,0:T(8,128)(2,1)S(1)} %collective-permute-done.3.refs_1_, ...), custom_call_target="tpu_custom_call" | custom-call | tf_op jit(solution)/shard_map/pallas_call | solution.py:340
  30.9 0.2 collective-permute-start.6
  31.1 1.1 %shard_map.139 = (bf16[512,256]{1,0:T(8,128)(2,1)}, f32[8,128]{1,0:T(8,128)S(1)}) custom-call(bf16[128,256]{1,0:T(8,128)(2,1)S(1)} %get-tuple-element.36.refs_0_, bf16[128,256]{1,0:T(8,128)(2,1)S(1)} %collective-permute-done.3.refs_1_, bf16[128,256]{1,0:T(8,128)(2,1)S(1)} %collective-permute-done.4.refs_2_, ...), custom_call_target="tpu_custom_call" | custom-call | flops 536870912 | bytes 1048576 | tf_op jit(solution)/shard_map/pallas_call | solution.py:355
  32.2 0.0 collective-permute-done.6.refs_1_
  32.3 1.6 %collective-permute-start.7 = (bf16[136,256]{1,0:T(8,128)(2,1)S(1)}, bf16[136,256]{1,0:T(8,128)(2,1)S(1)}, u32[]{:S(2)}, u32[]{:S(2)}) collective-permute-start(bf16[136,256]{1,0:T(8,128)(2,1)S(1)} %shard_map.140.other_ref.refs_0_), channel_id=1, source_target_pairs={{0,8},{1,9},{2,10},{3,11},{4,12},{5,13},{6,14},{7,15},{8,0},{9,1},... | collective-permute-start | bytes 208904 | tf_op jit(solution)/shard_map/ppermute | solution.py:286
  33.9 3.6 %all-to-all-start = ((bf16[16,32,256]{2,1,0:T(8,128)(2,1)}), bf16[16,32,256]{2,1,0:T(8,128)(2,1)S(1)}, u32[]{:S(2)}, u32[]{:S(2)}) async-start(bf16[16,32,256]{2,1,0:T(8,128)(2,1)} %bitcast), calls=%async_computation | async-start | bytes 524288 | tf_op jit(solution)/shard_map/all_to_all | solution.py:280
  37.5 1.0 %collective-permute-done.7.refs_1_ = bf16[136,256]{1,0:T(8,128)(2,1)S(1)} collective-permute-done((bf16[136,256]{1,0:T(8,128)(2,1)S(1)}, bf16[136,256]{1,0:T(8,128)(2,1)S(1)}, u32[]{:S(2)}, u32[]{:S(2)}) %collective-permute-start.7) | collective-permute-done | bytes 69664 | tf_op jit(solution)/shard_map/ppermute | solution.py:286
  38.5 1.9 %collective-permute-start.10 = (bf16[136,256]{1,0:T(8,128)(2,1)S(1)}, bf16[136,256]{1,0:T(8,128)(2,1)S(1)}, u32[]{:S(2)}, u32[]{:S(2)}) collective-permute-start(bf16[136,256]{1,0:T(8,128)(2,1)S(1)} %shard_map.143.refs_0_), channel_id=1, source_target_pairs={{0,6},{1,7},{2,4},{3,5},{4,2},{5,3},{6,0},{7,1},{8,14},{9,15},{10,... | collective-permute-start | bytes 208904 | tf_op jit(solution)/shard_map/ppermute | solution.py:286
  40.4 0.9 %collective-permute-start.9 = (bf16[136,256]{1,0:T(8,128)(2,1)S(1)}, bf16[136,256]{1,0:T(8,128)(2,1)S(1)}, u32[]{:S(2)}, u32[]{:S(2)}) collective-permute-start(bf16[136,256]{1,0:T(8,128)(2,1)S(1)} %shard_map.143.refs_0_), channel_id=1, source_target_pairs={{0,4},{1,5},{2,6},{3,7},{4,0},{5,1},{6,2},{7,3},{8,12},{9,13},{10,... | collective-permute-start | bytes 208904 | tf_op jit(solution)/shard_map/ppermute | solution.py:286
  41.3 0.7 %collective-permute-start.8 = (bf16[136,256]{1,0:T(8,128)(2,1)S(1)}, bf16[136,256]{1,0:T(8,128)(2,1)S(1)}, u32[]{:S(2)}, u32[]{:S(2)}) collective-permute-start(bf16[136,256]{1,0:T(8,128)(2,1)S(1)} %shard_map.143.refs_0_), channel_id=1, source_target_pairs={{0,2},{1,3},{2,0},{3,1},{4,6},{5,7},{6,4},{7,5},{8,10},{9,11},{10,... | collective-permute-start | bytes 208904 | tf_op jit(solution)/shard_map/ppermute | solution.py:286
  42.0 5.3 %collective-permute-done.10.refs_3_ = bf16[136,256]{1,0:T(8,128)(2,1)S(1)} collective-permute-done((bf16[136,256]{1,0:T(8,128)(2,1)S(1)}, bf16[136,256]{1,0:T(8,128)(2,1)S(1)}, u32[]{:S(2)}, u32[]{:S(2)}) %collective-permute-start.10) | collective-permute-done | bytes 69664 | tf_op jit(solution)/shard_map/ppermute | solution.py:286
  47.3 0.5 collective-permute-done.9.refs_2_
  47.8 0.0 collective-permute-done.8.refs_1_
  47.9 0.1 collective-permute-start.11
  48.0 0.0 all-to-all-done
  48.0 0.9 %shard_map.142 = (bf16[256,128]{1,0:T(8,128)(2,1)}, bf16[256,128]{1,0:T(8,128)(2,1)}, f32[8,128]{1,0:T(8,128)S(1)}) custom-call(bf16[256,512]{1,0:T(8,128)(2,1)S(1)} %get-tuple-element.31.pick_ref, bf16[512,256]{1,0:T(8,128)(2,1)S(1)} %bitcast.2), custom_call_target="tpu_custom_call" | custom-call | tf_op jit(solution)/shard_map/pallas_call | solution.py:367
  48.9 0.3 collective-permute-done.11.refs_1_
  49.2 0.7 %shard_map.145 = (f32[128]{0:T(128)}, f32[128,384]{1,0:T(8,128)}, f32[384]{0:T(512)}, f32[128,128]{1,0:T(8,128)}, f32[128]{0:T(128)}) custom-call(bf16[136,256]{1,0:T(8,128)(2,1)S(1)} %shard_map.144.refs_0_, bf16[136,256]{1,0:T(8,128)(2,1)S(1)} %collective-permute-done.11.refs_1_, f32[8,128]{1,0:T(8,128)S(1)} %get-tuple-element.49.refs_2_), custom_call_target="tpu_custom_call" | custom-call | tf_op jit(solution)/shard_map/pallas_call | solution.py:403
  (7 shorter events, 0.1 us)
Async XLA Ops:
  2.5 6.3 %collective-permute-start = (bf16[128,256]{1,0:T(8,128)(2,1)}, bf16[128,256]{1,0:T(8,128)(2,1)S(1)}, u32[]{:S(2)}, u32[]{:S(2)}) collective-permute-start(bf16[128,256]{1,0:T(8,128)(2,1)} %get-tuple-element.33), channel_id=1, source_target_pairs={{0,4},{1,5},{2,6},{3,7},{4,0},{5,1},{6,2},{7,3},{8,12},{9,13},{10,... | collective-permute-start | bytes 196616 | tf_op jit(solution)/shard_map/ppermute | solution.py:286
  5.6 2.6 %copy-start.3 = (s32[2,8]{1,0:T(2,128)S(1)}, s32[2,8]{1,0:T(2,128)}, u32[]{:S(2)}) copy-start(s32[2,8]{1,0:T(2,128)} %route_hbm.3) | copy-start | bytes 196
  5.6 7.5 %collective-permute-start.1 = (bf16[128,256]{1,0:T(8,128)(2,1)}, bf16[128,256]{1,0:T(8,128)(2,1)S(1)}, u32[]{:S(2)}, u32[]{:S(2)}) collective-permute-start(bf16[128,256]{1,0:T(8,128)(2,1)} %get-tuple-element.34), channel_id=1, source_target_pairs={{0,8},{1,9},{2,10},{3,11},{4,12},{5,13},{6,14},{7,15},{8,0},{9,1},... | collective-permute-start | bytes 196616 | tf_op jit(solution)/shard_map/ppermute | solution.py:286
  8.2 6.3 %collective-permute-start.2 = (bf16[128,256]{1,0:T(8,128)(2,1)}, bf16[128,256]{1,0:T(8,128)(2,1)S(1)}, u32[]{:S(2)}, u32[]{:S(2)}) collective-permute-start(bf16[128,256]{1,0:T(8,128)(2,1)} %get-tuple-element.35), channel_id=1, source_target_pairs={{0,12},{1,13},{2,14},{3,15},{4,8},{5,9},{6,10},{7,11},{8,4},{9,5},... | collective-permute-start | bytes 196616 | tf_op jit(solution)/shard_map/ppermute | solution.py:286
  14.4 0.8 %copy-start.1 = (bf16[128,256]{1,0:T(8,128)(2,1)S(1)}, bf16[128,256]{1,0:T(8,128)(2,1)}, u32[]{:S(2)}) copy-start(bf16[128,256]{1,0:T(8,128)(2,1)} %get-tuple-element.32.refs_0_) | copy-start | bytes 196612
  15.3 5.8 %copy-start = (bf16[128,384]{1,0:T(8,128)(2,1)S(1)}, bf16[128,384]{1,0:T(8,128)(2,1)}, u32[]{:S(2)}) copy-start(bf16[128,384]{1,0:T(8,128)(2,1)} %refs_5_.1) | copy-start | bytes 294916
  15.3 5.8 %copy-start.2 = (bf16[128,128]{1,0:T(8,128)(2,1)S(1)}, bf16[128,128]{1,0:T(8,128)(2,1)}, u32[]{:S(2)}) copy-start(bf16[128,128]{1,0:T(8,128)(2,1)} %refs_7_.1) | copy-start | bytes 98308
  15.3 2.0 %copy-start.4 = (f32[384]{0:T(512)S(1)}, f32[384]{0:T(512)}, u32[]{:S(2)}) copy-start(f32[384]{0:T(512)} %param.14) | copy-start | bytes 4612
  15.3 2.0 %collective-permute-start.3 = (bf16[128,256]{1,0:T(8,128)(2,1)S(1)}, bf16[128,256]{1,0:T(8,128)(2,1)S(1)}, u32[]{:S(2)}, u32[]{:S(2)}) collective-permute-start(bf16[128,256]{1,0:T(8,128)(2,1)S(1)} %get-tuple-element.37), channel_id=1, source_target_pairs={{0,1},{1,0},{2,3},{3,2},{4,5},{5,4},{6,7},{7,6},{8,9},{9,8},{10,11... | collective-permute-start | bytes 196616 | tf_op jit(solution)/shard_map/ppermute | solution.py:286
  15.4 1.9 %copy-start.5 = (f32[128]{0:T(128)S(1)}, f32[128]{0:T(128)}, u32[]{:S(2)}) copy-start(f32[128]{0:T(128)} %param.16) | copy-start | bytes 1540
  15.4 1.9 %copy-start.6 = (f32[128]{0:T(128)S(1)}, f32[128]{0:T(128)}, u32[]{:S(2)}) copy-start(f32[128]{0:T(128)} %param.12) | copy-start | bytes 1540
  15.4 4.5 %collective-permute-start.4 = (bf16[128,256]{1,0:T(8,128)(2,1)S(1)}, bf16[128,256]{1,0:T(8,128)(2,1)S(1)}, u32[]{:S(2)}, u32[]{:S(2)}) collective-permute-start(bf16[128,256]{1,0:T(8,128)(2,1)S(1)} %get-tuple-element.38), channel_id=1, source_target_pairs={{0,2},{1,3},{2,0},{3,1},{4,6},{5,7},{6,4},{7,5},{8,10},{9,11},{10,... | collective-permute-start | bytes 196616 | tf_op jit(solution)/shard_map/ppermute | solution.py:286
  17.0 4.1 %collective-permute-start.5 = (bf16[128,256]{1,0:T(8,128)(2,1)S(1)}, bf16[128,256]{1,0:T(8,128)(2,1)S(1)}, u32[]{:S(2)}, u32[]{:S(2)}) collective-permute-start(bf16[128,256]{1,0:T(8,128)(2,1)S(1)} %get-tuple-element.39), channel_id=1, source_target_pairs={{0,3},{1,2},{2,1},{3,0},{4,7},{5,6},{6,5},{7,4},{8,11},{9,10},{10,... | collective-permute-start | bytes 196616 | tf_op jit(solution)/shard_map/ppermute | solution.py:286
  30.9 1.3 %collective-permute-start.6 = (bf16[136,256]{1,0:T(8,128)(2,1)S(1)}, bf16[136,256]{1,0:T(8,128)(2,1)S(1)}, u32[]{:S(2)}, u32[]{:S(2)}) collective-permute-start(bf16[136,256]{1,0:T(8,128)(2,1)S(1)} %get-tuple-element.45), channel_id=1, source_target_pairs={{0,1},{1,0},{2,3},{3,2},{4,5},{5,4},{6,7},{7,6},{8,9},{9,8},{10,11... | collective-permute-start | bytes 208904 | tf_op jit(solution)/shard_map/ppermute | solution.py:286
  32.3 6.2 %collective-permute-start.7 = (bf16[136,256]{1,0:T(8,128)(2,1)S(1)}, bf16[136,256]{1,0:T(8,128)(2,1)S(1)}, u32[]{:S(2)}, u32[]{:S(2)}) collective-permute-start(bf16[136,256]{1,0:T(8,128)(2,1)S(1)} %shard_map.140.other_ref.refs_0_), channel_id=1, source_target_pairs={{0,8},{1,9},{2,10},{3,11},{4,12},{5,13},{6,14},{7,15},{8,0},{9,1},... | collective-permute-start | bytes 208904 | tf_op jit(solution)/shard_map/ppermute | solution.py:286
  33.9 14.1 %all-to-all-start = ((bf16[16,32,256]{2,1,0:T(8,128)(2,1)}), bf16[16,32,256]{2,1,0:T(8,128)(2,1)S(1)}, u32[]{:S(2)}, u32[]{:S(2)}) async-start(bf16[16,32,256]{2,1,0:T(8,128)(2,1)} %bitcast), calls=%async_computation | async-start | bytes 524288 | tf_op jit(solution)/shard_map/all_to_all | solution.py:280
  38.5 8.8 %collective-permute-start.10 = (bf16[136,256]{1,0:T(8,128)(2,1)S(1)}, bf16[136,256]{1,0:T(8,128)(2,1)S(1)}, u32[]{:S(2)}, u32[]{:S(2)}) collective-permute-start(bf16[136,256]{1,0:T(8,128)(2,1)S(1)} %shard_map.143.refs_0_), channel_id=1, source_target_pairs={{0,6},{1,7},{2,4},{3,5},{4,2},{5,3},{6,0},{7,1},{8,14},{9,15},{10,... | collective-permute-start | bytes 208904 | tf_op jit(solution)/shard_map/ppermute | solution.py:286
  40.4 7.4 %collective-permute-start.9 = (bf16[136,256]{1,0:T(8,128)(2,1)S(1)}, bf16[136,256]{1,0:T(8,128)(2,1)S(1)}, u32[]{:S(2)}, u32[]{:S(2)}) collective-permute-start(bf16[136,256]{1,0:T(8,128)(2,1)S(1)} %shard_map.143.refs_0_), channel_id=1, source_target_pairs={{0,4},{1,5},{2,6},{3,7},{4,0},{5,1},{6,2},{7,3},{8,12},{9,13},{10,... | collective-permute-start | bytes 208904 | tf_op jit(solution)/shard_map/ppermute | solution.py:286
  41.3 6.5 %collective-permute-start.8 = (bf16[136,256]{1,0:T(8,128)(2,1)S(1)}, bf16[136,256]{1,0:T(8,128)(2,1)S(1)}, u32[]{:S(2)}, u32[]{:S(2)}) collective-permute-start(bf16[136,256]{1,0:T(8,128)(2,1)S(1)} %shard_map.143.refs_0_), channel_id=1, source_target_pairs={{0,2},{1,3},{2,0},{3,1},{4,6},{5,7},{6,4},{7,5},{8,10},{9,11},{10,... | collective-permute-start | bytes 208904 | tf_op jit(solution)/shard_map/ppermute | solution.py:286
  47.9 1.3 %collective-permute-start.11 = (bf16[136,256]{1,0:T(8,128)(2,1)S(1)}, bf16[136,256]{1,0:T(8,128)(2,1)S(1)}, u32[]{:S(2)}, u32[]{:S(2)}) collective-permute-start(bf16[136,256]{1,0:T(8,128)(2,1)S(1)} %shard_map.144.refs_0_), channel_id=1, source_target_pairs={{0,1},{1,0},{2,3},{3,2},{4,5},{5,4},{6,7},{7,6},{8,9},{9,8},{10,11... | collective-permute-start | bytes 208904 | tf_op jit(solution)/shard_map/ppermute | solution.py:286

commit v4 on v2

--- a/solution.py
+++ b/solution.py
@@ -54,12 +54,13 @@
     ]
     for copy in copies:
         copy.start()
-    for copy in copies:
-        copy.wait()
+    copies[0].wait()
     rows, width = points_ref.shape
     target = send_rows(route_ref, (1, rows), 1, block_rows, out_ref.shape[0] // block_rows)
     index = lax.broadcasted_iota(jnp.int32, (out_ref.shape[0], rows), 0)
     pick = jnp.where(index == target, 1.0, 0.0).astype(BF16)
+    for copy in copies[1:]:
+        copy.wait()
     ones = jnp.ones((rows, width), BF16)
     moved = matmul(pick, jnp.concatenate([points_ref[...], ones], axis=1))
     empty = (1.0 - moved[:, width:]) * EMPTY
@@ -108,22 +109,36 @@
     lane = lax.broadcasted_iota(jnp.int32, (rows, width), 1)
     hidden = jnp.where(points[:, :1] > EMPTY / 2, MASKED, 0.0)
 
+    def products(h):
+        mine = (lane >= h * head) & (lane < (h + 1) * head)
+        scores = matmul(jnp.where(mine, keys_s, 0), query, ((1,), (1,))) + hidden
+        return scores, matmul(jnp.where(mine, values, 0), d_attn_s, ((1,), (1,)))
+
+    def finish(h, probs_b, d_score):
+        lanes = slice(h * head, (h + 1) * head)
+        d_values_ref[:, lanes] = matmul(probs_b, d_attn)[:, lanes]
+        d_keys_ref[:, lanes] = matmul(d_score, query)[:, lanes]
+
     attn_t, dq_t = [], []
+    following = products(0)
+    done = None
     for h in range(HEADS):
         lo, hi = h * head, (h + 1) * head
-        mine = (lane >= lo) & (lane < hi)
-        scores = matmul(jnp.where(mine, keys_s, 0), query, ((1,), (1,))) + hidden
+        scores, d_probs = following
+        if h + 1 < HEADS:
+            following = products(h + 1)
+        if done is not None:
+            finish(h - 1, *done)
         expo = jnp.exp(scores - jnp.max(scores, axis=0, keepdims=True))
         probs = expo * (1.0 / jnp.sum(expo, axis=0, keepdims=True))
         probs_b = probs.astype(BF16)
         out_t = matmul(values_t[lo:hi, :], probs_b)
         attn_t.append(out_t)
         inner = jnp.sum(out_t * d_attn_t[lo:hi, :].astype(F32), axis=0, keepdims=True) * scale
-        d_probs = matmul(jnp.where(mine, values, 0), d_attn_s, ((1,), (1,)))
         d_score = (probs * (d_probs - inner)).astype(BF16)
         dq_t.append(matmul(keys_t[lo:hi, :], d_score))
-        d_values_ref[:, lo:hi] = matmul(probs_b, d_attn)[:, lo:hi]
-        d_keys_ref[:, lo:hi] = matmul(d_score, query)[:, lo:hi]
+        done = probs_b, d_score
+    finish(HEADS - 1, *done)
 
     attn_t = jnp.concatenate(attn_t, axis=0)
     attn_ref[...] = attn_t.T.astype(BF16)

time: 49.1 us -> 48.1 us (0.980)
  Pallas kernels: 15.2 us -> 14.2 us
    pallas_call x1, Pallas kernels: 9.87 us -> 8.9 us  [local(): pl.pallas_call(functools.partial(owner_kernel, near), out_shape=(shape(he...]
  transfers between devices with their start and end apart: 8 -> 8, of which waited for: 6 -> 6; matrix products, arithmetic and copies ran while one was open for 0% -> 0% of each run, Pallas kernels for 5% -> 6%
where the time goes in v4:
time: 48.1 us; the launch traced here: 47.7 us
  waiting for transfers between devices  16.7 us (35%)
  starting transfers between devices  15.9 us (33%)
  Pallas kernels  14.2 us (30%)
  between operations  0.81 us (2%)
    all_to_all x2, starting transfers between devices, exchange(): lax.all_to_all(message, 'seq', split_axis=0, concat_axis=0, axis_index_gr...  11.6 us
    all_to_all x2, waiting for transfers between devices, exchange(): lax.all_to_all(message, 'seq', split_axis=0, concat_axis=0, axis_index_gr...  9.48 us
    pallas_call x1, Pallas kernels, local(): pl.pallas_call(functools.partial(owner_kernel, near), out_shape=(shape(he...  8.9 us
    ppermute x6, waiting for transfers between devices, swap(): lax.ppermute(piece, 'seq', [(dev, dev ^ step) for dev in range(devs)])  7.25 us
    ppermute x6, starting transfers between devices, swap(): lax.ppermute(piece, 'seq', [(dev, dev ^ step) for dev in range(devs)])  4.34 us
    pallas_call x1, Pallas kernels, local(): pl.pallas_call(functools.partial(scatter_kernel, block_rows), out_shape=s...  1.89 us
    pallas_call x1, Pallas kernels, local(): pl.pallas_call(rows_kernel, out_shape=(shape(held, 2 * width), shape(8, 1...  1.09 us
  transfers between devices with their start and end apart: 8, of which 6 were waited for; matrix products, arithmetic and copies ran while one was open for 0% of the time, Pallas kernels for 6%

profile of v4, /device:TPU:0, one launch (start us, length us, event | category | flops | bytes accessed | tf_op | source)
XLA Modules:
  0.0 47.7 jit_solution(5838216327100676686)
XLA Ops:
  0.6 1.9 %shard_map.136 = bf16[512,256]{1,0:T(8,128)(2,1)} custom-call(s32[2,8]{1,0:T(2,128)} %route_hbm.3, bf16[256,128]{1,0:T(8,128)(2,1)} %points_hbm.1, bf16[256,128]{1,0:T(8,128)(2,1)} %cot_hbm.1), custom_call_target="tpu_custom_call" | custom-call | tf_op jit(solution)/shard_map/pallas_call | solution.py:277
  2.5 0.0 copy-start.2
  2.5 0.0 copy-start.3
  2.6 0.0 copy-start
  2.6 0.0 copy-start.1
  2.6 7.5 %all-to-all-start = ((bf16[16,32,256]{2,1,0:T(8,128)(2,1)}), bf16[16,32,256]{2,1,0:T(8,128)(2,1)S(1)}, u32[]{:S(2)}, u32[]{:S(2)}) async-start(bf16[16,32,256]{2,1,0:T(8,128)(2,1)} %bitcast.7), calls=%async_computation | async-start | bytes 524288 | tf_op jit(solution)/shard_map/all_to_all | solution.py:257
  10.1 0.0 copy-done.2
  10.1 0.0 copy-start.4
  10.1 0.0 copy-start.5
  10.1 0.6 %shard_map.135 = (bf16[256,512]{1,0:T(8,128)(2,1)S(1)}, f32[8,128]{1,0:T(8,128)S(1)}) custom-call(s32[2,8]{1,0:T(2,128)S(1)} %copy-done.2), custom_call_target="tpu_custom_call" | custom-call | tf_op jit(solution)/shard_map/pallas_call | solution.py:291
  10.8 0.0 copy-done.3
  10.8 0.0 copy-done.4
  10.8 0.0 copy-done.5
  10.8 9.5 %all-to-all-done = bf16[16,32,256]{2,1,0:T(8,128)(2,1)S(1)} async-done(((bf16[16,32,256]{2,1,0:T(8,128)(2,1)}), bf16[16,32,256]{2,1,0:T(8,128)(2,1)S(1)}, u32[]{:S(2)}, u32[]{:S(2)}) %all-to-all-start) | async-done | bytes 262176 | tf_op jit(solution)/shard_map/all_to_all | solution.py:257
  20.3 0.0 copy-done
  20.3 0.0 copy-done.1
  20.3 8.9 %shard_map.137 = (bf16[512,128]{1,0:T(8,128)(2,1)S(1)}, f32[512,128]{1,0:T(8,128)S(1)}, bf16[136,256]{1,0:T(8,128)(2,1)S(1)}, bf16[136,256]{1,0:T(8,128)(2,1)S(1)}) custom-call(bf16[512,256]{1,0:T(8,128)(2,1)S(1)} %bitcast.5, f32[1,640]{1,0:T(1,128)S(1)} %broadcast_in_dim.3.vectors_ref, bf16[128,384]{1,0:T(8,128)(2,1)S(1)} %copy-done, ...), custom_call_target="tpu_custom_call" | custom-call | tf_op jit(solution)/shard_map/pallas_call | solution.py:306
  29.2 0.1 collective-permute-start
  29.3 1.1 %shard_map.138 = (bf16[512,256]{1,0:T(8,128)(2,1)}, f32[8,128]{1,0:T(8,128)S(1)}) custom-call(bf16[512,256]{1,0:T(8,128)(2,1)S(1)} %bitcast.6, bf16[512,128]{1,0:T(8,128)(2,1)S(1)} %get-tuple-element.25.attn_ref, f32[512,128]{1,0:T(8,128)S(1)} %get-tuple-element.26.d_normed_ref, f32[1,640]{1,0:T(1,128)S(1)} %broadcast_in_dim.3.vectors_ref, ...), custom_call_target="tpu_custom_call" | custom-call | flops 536870912 | bytes 1048576 | tf_op jit(solution)/shard_map/pallas_call | solution.py:321
  30.4 0.2 collective-permute-done.refs_1_
  30.6 0.6 %collective-permute-start.1 = (bf16[136,256]{1,0:T(8,128)(2,1)S(1)}, bf16[136,256]{1,0:T(8,128)(2,1)S(1)}, u32[]{:S(2)}, u32[]{:S(2)}) collective-permute-start(bf16[136,256]{1,0:T(8,128)(2,1)S(1)} %shard_map.139.other_ref.refs_0_), channel_id=1, source_target_pairs={{0,8},{1,9},{2,10},{3,11},{4,12},{5,13},{6,14},{7,15},{8,0},{9,1},... | collective-permute-start | bytes 208904 | tf_op jit(solution)/shard_map/ppermute | solution.py:263
  31.2 4.1 %all-to-all-start.1 = ((bf16[16,32,256]{2,1,0:T(8,128)(2,1)}), bf16[16,32,256]{2,1,0:T(8,128)(2,1)S(1)}, u32[]{:S(2)}, u32[]{:S(2)}) async-start(bf16[16,32,256]{2,1,0:T(8,128)(2,1)} %bitcast.2), calls=%async_computation.1 | async-start | bytes 524288 | tf_op jit(solution)/shard_map/all_to_all | solution.py:257
  35.3 2.2 %collective-permute-done.1.refs_1_ = bf16[136,256]{1,0:T(8,128)(2,1)S(1)} collective-permute-done((bf16[136,256]{1,0:T(8,128)(2,1)S(1)}, bf16[136,256]{1,0:T(8,128)(2,1)S(1)}, u32[]{:S(2)}, u32[]{:S(2)}) %collective-permute-start.1) | collective-permute-done | bytes 69664 | tf_op jit(solution)/shard_map/ppermute | solution.py:263
  37.5 0.7 %collective-permute-start.4 = (bf16[136,256]{1,0:T(8,128)(2,1)S(1)}, bf16[136,256]{1,0:T(8,128)(2,1)S(1)}, u32[]{:S(2)}, u32[]{:S(2)}) collective-permute-start(bf16[136,256]{1,0:T(8,128)(2,1)S(1)} %shard_map.142.refs_0_), channel_id=1, source_target_pairs={{0,6},{1,7},{2,4},{3,5},{4,2},{5,3},{6,0},{7,1},{8,14},{9,15},{10,... | collective-permute-start | bytes 208904 | tf_op jit(solution)/shard_map/ppermute | solution.py:263
  38.2 1.0 %collective-permute-start.3 = (bf16[136,256]{1,0:T(8,128)(2,1)S(1)}, bf16[136,256]{1,0:T(8,128)(2,1)S(1)}, u32[]{:S(2)}, u32[]{:S(2)}) collective-permute-start(bf16[136,256]{1,0:T(8,128)(2,1)S(1)} %shard_map.142.refs_0_), channel_id=1, source_target_pairs={{0,4},{1,5},{2,6},{3,7},{4,0},{5,1},{6,2},{7,3},{8,12},{9,13},{10,... | collective-permute-start | bytes 208904 | tf_op jit(solution)/shard_map/ppermute | solution.py:263
  39.2 1.8 %collective-permute-start.2 = (bf16[136,256]{1,0:T(8,128)(2,1)S(1)}, bf16[136,256]{1,0:T(8,128)(2,1)S(1)}, u32[]{:S(2)}, u32[]{:S(2)}) collective-permute-start(bf16[136,256]{1,0:T(8,128)(2,1)S(1)} %shard_map.142.refs_0_), channel_id=1, source_target_pairs={{0,2},{1,3},{2,0},{3,1},{4,6},{5,7},{6,4},{7,5},{8,10},{9,11},{10,... | collective-permute-start | bytes 208904 | tf_op jit(solution)/shard_map/ppermute | solution.py:263
  41.0 3.7 %collective-permute-done.4.refs_3_ = bf16[136,256]{1,0:T(8,128)(2,1)S(1)} collective-permute-done((bf16[136,256]{1,0:T(8,128)(2,1)S(1)}, bf16[136,256]{1,0:T(8,128)(2,1)S(1)}, u32[]{:S(2)}, u32[]{:S(2)}) %collective-permute-start.4) | collective-permute-done | bytes 69664 | tf_op jit(solution)/shard_map/ppermute | solution.py:263
  44.7 0.9 %collective-permute-done.3.refs_2_ = bf16[136,256]{1,0:T(8,128)(2,1)S(1)} collective-permute-done((bf16[136,256]{1,0:T(8,128)(2,1)S(1)}, bf16[136,256]{1,0:T(8,128)(2,1)S(1)}, u32[]{:S(2)}, u32[]{:S(2)}) %collective-permute-start.3) | collective-permute-done | bytes 69664 | tf_op jit(solution)/shard_map/ppermute | solution.py:263
  45.6 0.0 collective-permute-done.2.refs_1_
  45.7 0.1 collective-permute-start.5
  45.7 0.0 all-to-all-done.1
  45.7 0.9 %shard_map.141 = (bf16[256,128]{1,0:T(8,128)(2,1)}, bf16[256,128]{1,0:T(8,128)(2,1)}, f32[8,128]{1,0:T(8,128)S(1)}) custom-call(bf16[256,512]{1,0:T(8,128)(2,1)S(1)} %get-tuple-element.23.pick_ref, bf16[512,256]{1,0:T(8,128)(2,1)S(1)} %bitcast.4), custom_call_target="tpu_custom_call" | custom-call | tf_op jit(solution)/shard_map/pallas_call | solution.py:333
  46.6 0.3 collective-permute-done.5.refs_1_
  47.0 0.7 %shard_map.144 = (f32[128]{0:T(128)}, f32[128,384]{1,0:T(8,128)}, f32[384]{0:T(512)}, f32[128,128]{1,0:T(8,128)}, f32[128]{0:T(128)}) custom-call(bf16[136,256]{1,0:T(8,128)(2,1)S(1)} %shard_map.143.refs_0_, bf16[136,256]{1,0:T(8,128)(2,1)S(1)} %collective-permute-done.5.refs_1_, f32[8,128]{1,0:T(8,128)S(1)} %get-tuple-element.33.refs_2_), custom_call_target="tpu_custom_call" | custom-call | tf_op jit(solution)/shard_map/pallas_call | solution.py:369
  (6 shorter events, 0.1 us)
Async XLA Ops:
  2.5 7.6 %copy-start.2 = (s32[2,8]{1,0:T(2,128)S(1)}, s32[2,8]{1,0:T(2,128)}, u32[]{:S(2)}) copy-start(s32[2,8]{1,0:T(2,128)} %route_hbm.3) | copy-start | bytes 196
  2.5 8.2 %copy-start.3 = (f32[384]{0:T(512)S(1)}, f32[384]{0:T(512)}, u32[]{:S(2)}) copy-start(f32[384]{0:T(512)} %param.14) | copy-start | bytes 4612
  2.6 17.7 %copy-start = (bf16[128,384]{1,0:T(8,128)(2,1)S(1)}, bf16[128,384]{1,0:T(8,128)(2,1)}, u32[]{:S(2)}) copy-start(bf16[128,384]{1,0:T(8,128)(2,1)} %w_qkv_hbm.1) | copy-start | bytes 294916
  2.6 17.7 %copy-start.1 = (bf16[128,128]{1,0:T(8,128)(2,1)S(1)}, bf16[128,128]{1,0:T(8,128)(2,1)}, u32[]{:S(2)}) copy-start(bf16[128,128]{1,0:T(8,128)(2,1)} %w_out_ref.1) | copy-start | bytes 98308
  2.6 17.7 %all-to-all-start = ((bf16[16,32,256]{2,1,0:T(8,128)(2,1)}), bf16[16,32,256]{2,1,0:T(8,128)(2,1)S(1)}, u32[]{:S(2)}, u32[]{:S(2)}) async-start(bf16[16,32,256]{2,1,0:T(8,128)(2,1)} %bitcast.7), calls=%async_computation | async-start | bytes 524288 | tf_op jit(solution)/shard_map/all_to_all | solution.py:257
  10.1 0.7 %copy-start.4 = (f32[128]{0:T(128)S(1)}, f32[128]{0:T(128)}, u32[]{:S(2)}) copy-start(f32[128]{0:T(128)} %param.16) | copy-start | bytes 1540
  10.1 0.7 %copy-start.5 = (f32[128]{0:T(128)S(1)}, f32[128]{0:T(128)}, u32[]{:S(2)}) copy-start(f32[128]{0:T(128)} %param.12) | copy-start | bytes 1540
  29.2 1.3 %collective-permute-start = (bf16[136,256]{1,0:T(8,128)(2,1)S(1)}, bf16[136,256]{1,0:T(8,128)(2,1)S(1)}, u32[]{:S(2)}, u32[]{:S(2)}) collective-permute-start(bf16[136,256]{1,0:T(8,128)(2,1)S(1)} %get-tuple-element.29), channel_id=1, source_target_pairs={{0,1},{1,0},{2,3},{3,2},{4,5},{5,4},{6,7},{7,6},{8,9},{9,8},{10,11... | collective-permute-start | bytes 208904 | tf_op jit(solution)/shard_map/ppermute | solution.py:263
  30.6 6.9 %collective-permute-start.1 = (bf16[136,256]{1,0:T(8,128)(2,1)S(1)}, bf16[136,256]{1,0:T(8,128)(2,1)S(1)}, u32[]{:S(2)}, u32[]{:S(2)}) collective-permute-start(bf16[136,256]{1,0:T(8,128)(2,1)S(1)} %shard_map.139.other_ref.refs_0_), channel_id=1, source_target_pairs={{0,8},{1,9},{2,10},{3,11},{4,12},{5,13},{6,14},{7,15},{8,0},{9,1},... | collective-permute-start | bytes 208904 | tf_op jit(solution)/shard_map/ppermute | solution.py:263
  31.2 14.5 %all-to-all-start.1 = ((bf16[16,32,256]{2,1,0:T(8,128)(2,1)}), bf16[16,32,256]{2,1,0:T(8,128)(2,1)S(1)}, u32[]{:S(2)}, u32[]{:S(2)}) async-start(bf16[16,32,256]{2,1,0:T(8,128)(2,1)} %bitcast.2), calls=%async_computation.1 | async-start | bytes 524288 | tf_op jit(solution)/shard_map/all_to_all | solution.py:257
  37.5 7.3 %collective-permute-start.4 = (bf16[136,256]{1,0:T(8,128)(2,1)S(1)}, bf16[136,256]{1,0:T(8,128)(2,1)S(1)}, u32[]{:S(2)}, u32[]{:S(2)}) collective-permute-start(bf16[136,256]{1,0:T(8,128)(2,1)S(1)} %shard_map.142.refs_0_), channel_id=1, source_target_pairs={{0,6},{1,7},{2,4},{3,5},{4,2},{5,3},{6,0},{7,1},{8,14},{9,15},{10,... | collective-permute-start | bytes 208904 | tf_op jit(solution)/shard_map/ppermute | solution.py:263
  38.2 7.4 %collective-permute-start.3 = (bf16[136,256]{1,0:T(8,128)(2,1)S(1)}, bf16[136,256]{1,0:T(8,128)(2,1)S(1)}, u32[]{:S(2)}, u32[]{:S(2)}) collective-permute-start(bf16[136,256]{1,0:T(8,128)(2,1)S(1)} %shard_map.142.refs_0_), channel_id=1, source_target_pairs={{0,4},{1,5},{2,6},{3,7},{4,0},{5,1},{6,2},{7,3},{8,12},{9,13},{10,... | collective-permute-start | bytes 208904 | tf_op jit(solution)/shard_map/ppermute | solution.py:263
  39.2 6.4 %collective-permute-start.2 = (bf16[136,256]{1,0:T(8,128)(2,1)S(1)}, bf16[136,256]{1,0:T(8,128)(2,1)S(1)}, u32[]{:S(2)}, u32[]{:S(2)}) collective-permute-start(bf16[136,256]{1,0:T(8,128)(2,1)S(1)} %shard_map.142.refs_0_), channel_id=1, source_target_pairs={{0,2},{1,3},{2,0},{3,1},{4,6},{5,7},{6,4},{7,5},{8,10},{9,11},{10,... | collective-permute-start | bytes 208904 | tf_op jit(solution)/shard_map/ppermute | solution.py:263
  45.7 1.3 %collective-permute-start.5 = (bf16[136,256]{1,0:T(8,128)(2,1)S(1)}, bf16[136,256]{1,0:T(8,128)(2,1)S(1)}, u32[]{:S(2)}, u32[]{:S(2)}) collective-permute-start(bf16[136,256]{1,0:T(8,128)(2,1)S(1)} %shard_map.143.refs_0_), channel_id=1, source_target_pairs={{0,1},{1,0},{2,3},{3,2},{4,5},{5,4},{6,7},{7,6},{8,9},{9,8},{10,11... | collective-permute-start | bytes 208904 | tf_op jit(solution)/shard_map/ppermute | solution.py:263

commit v5 on v2

--- a/solution.py
+++ b/solution.py
@@ -54,12 +54,13 @@
     ]
     for copy in copies:
         copy.start()
-    for copy in copies:
-        copy.wait()
+    copies[0].wait()
     rows, width = points_ref.shape
     target = send_rows(route_ref, (1, rows), 1, block_rows, out_ref.shape[0] // block_rows)
     index = lax.broadcasted_iota(jnp.int32, (out_ref.shape[0], rows), 0)
     pick = jnp.where(index == target, 1.0, 0.0).astype(BF16)
+    for copy in copies[1:]:
+        copy.wait()
     ones = jnp.ones((rows, width), BF16)
     moved = matmul(pick, jnp.concatenate([points_ref[...], ones], axis=1))
     empty = (1.0 - moved[:, width:]) * EMPTY
@@ -108,22 +109,39 @@
     lane = lax.broadcasted_iota(jnp.int32, (rows, width), 1)
     hidden = jnp.where(points[:, :1] > EMPTY / 2, MASKED, 0.0)
 
+    def own(h, array):
+        return jnp.where((lane >= h * head) & (lane < (h + 1) * head), array, 0)
+
+    def scores_of(h):
+        return matmul(own(h, keys_s), query, ((1,), (1,))) + hidden
+
+    scores, probs, probs_b, d_probs, d_score = {}, {}, {}, {}, {}
     attn_t, dq_t = [], []
-    for h in range(HEADS):
-        lo, hi = h * head, (h + 1) * head
-        mine = (lane >= lo) & (lane < hi)
-        scores = matmul(jnp.where(mine, keys_s, 0), query, ((1,), (1,))) + hidden
-        expo = jnp.exp(scores - jnp.max(scores, axis=0, keepdims=True))
-        probs = expo * (1.0 / jnp.sum(expo, axis=0, keepdims=True))
-        probs_b = probs.astype(BF16)
-        out_t = matmul(values_t[lo:hi, :], probs_b)
-        attn_t.append(out_t)
-        inner = jnp.sum(out_t * d_attn_t[lo:hi, :].astype(F32), axis=0, keepdims=True) * scale
-        d_probs = matmul(jnp.where(mine, values, 0), d_attn_s, ((1,), (1,)))
-        d_score = (probs * (d_probs - inner)).astype(BF16)
-        dq_t.append(matmul(keys_t[lo:hi, :], d_score))
-        d_values_ref[:, lo:hi] = matmul(probs_b, d_attn)[:, lo:hi]
-        d_keys_ref[:, lo:hi] = matmul(d_score, query)[:, lo:hi]
+    scores[0] = scores_of(0)
+    for step in range(HEADS + 2):
+        if step + 1 < HEADS:
+            scores[step + 1] = scores_of(step + 1)
+        if step < HEADS:
+            d_probs[step] = matmul(own(step, values), d_attn_s, ((1,), (1,)))
+        if 1 <= step <= HEADS:
+            lanes = slice((step - 1) * head, step * head)
+            attn_t.append(matmul(values_t[lanes, :], probs_b[step - 1]))
+        if step >= 2:
+            h = step - 2
+            lanes = slice(h * head, (h + 1) * head)
+            d_values_ref[:, lanes] = matmul(probs_b[h], d_attn)[:, lanes]
+            d_keys_ref[:, lanes] = matmul(d_score[h], query)[:, lanes]
+            dq_t.append(matmul(keys_t[lanes, :], d_score[h]))
+        if step < HEADS:
+            now = scores.pop(step)
+            expo = jnp.exp(now - jnp.max(now, axis=0, keepdims=True))
+            probs[step] = expo * (1.0 / jnp.sum(expo, axis=0, keepdims=True))
+            probs_b[step] = probs[step].astype(BF16)
+        if 1 <= step <= HEADS:
+            h = step - 1
+            inner = attn_t[h] * d_attn_t[h * head : (h + 1) * head, :].astype(F32)
+            inner = jnp.sum(inner, axis=0, keepdims=True) * scale
+            d_score[h] = (probs.pop(h) * (d_probs.pop(h) - inner)).astype(BF16)
 
     attn_t = jnp.concatenate(attn_t, axis=0)
     attn_ref[...] = attn_t.T.astype(BF16)

time: 49.1 us -> 47.3 us (0.963)
  Pallas kernels: 15.2 us -> 13.3 us
    pallas_call x1, Pallas kernels: 9.87 us -> 8.03 us  [local(): pl.pallas_call(functools.partial(owner_kernel, near), out_shape=(shape(he...]
  transfers between devices with their start and end apart: 8 -> 8, of which waited for: 6 -> 6; matrix products, arithmetic and copies ran while one was open for 0% -> 0% of each run, Pallas kernels for 5% -> 6%
where the time goes in v5:
time: 47.3 us; the launch traced here: 46.9 us
  waiting for transfers between devices  16.7 us (35%)
  starting transfers between devices  15.9 us (34%)
  Pallas kernels  13.3 us (28%)
  between operations  0.81 us (2%)
    all_to_all x2, starting transfers between devices, exchange(): lax.all_to_all(message, 'seq', split_axis=0, concat_axis=0, axis_index_gr...  11.6 us
    all_to_all x2, waiting for transfers between devices, exchange(): lax.all_to_all(message, 'seq', split_axis=0, concat_axis=0, axis_index_gr...  9.48 us
    pallas_call x1, Pallas kernels, local(): pl.pallas_call(functools.partial(owner_kernel, near), out_shape=(shape(he...  8.03 us
    ppermute x6, waiting for transfers between devices, swap(): lax.ppermute(piece, 'seq', [(dev, dev ^ step) for dev in range(devs)])  7.25 us
    ppermute x6, starting transfers between devices, swap(): lax.ppermute(piece, 'seq', [(dev, dev ^ step) for dev in range(devs)])  4.34 us
    pallas_call x1, Pallas kernels, local(): pl.pallas_call(functools.partial(scatter_kernel, block_rows), out_shape=s...  1.89 us
    pallas_call x1, Pallas kernels, local(): pl.pallas_call(rows_kernel, out_shape=(shape(held, 2 * width), shape(8, 1...  1.09 us
  transfers between devices with their start and end apart: 8, of which 6 were waited for; matrix products, arithmetic and copies ran while one was open for 0% of the time, Pallas kernels for 6%

profile of v5, /device:TPU:0, one launch (start us, length us, event | category | flops | bytes accessed | tf_op | source)
XLA Modules:
  0.0 46.9 jit_solution(4651789997853462094)
XLA Ops:
  0.6 1.9 %shard_map.136 = bf16[512,256]{1,0:T(8,128)(2,1)} custom-call(s32[2,8]{1,0:T(2,128)} %route_hbm.3, bf16[256,128]{1,0:T(8,128)(2,1)} %points_hbm.1, bf16[256,128]{1,0:T(8,128)(2,1)} %cot_hbm.1), custom_call_target="tpu_custom_call" | custom-call | tf_op jit(solution)/shard_map/pallas_call | solution.py:280
  2.5 0.0 copy-start.2
  2.5 0.0 copy-start.3
  2.6 0.0 copy-start
  2.6 0.0 copy-start.1
  2.6 7.5 %all-to-all-start = ((bf16[16,32,256]{2,1,0:T(8,128)(2,1)}), bf16[16,32,256]{2,1,0:T(8,128)(2,1)S(1)}, u32[]{:S(2)}, u32[]{:S(2)}) async-start(bf16[16,32,256]{2,1,0:T(8,128)(2,1)} %bitcast.7), calls=%async_computation | async-start | bytes 524288 | tf_op jit(solution)/shard_map/all_to_all | solution.py:260
  10.1 0.0 copy-done.2
  10.1 0.0 copy-start.4
  10.1 0.0 copy-start.5
  10.1 0.6 %shard_map.135 = (bf16[256,512]{1,0:T(8,128)(2,1)S(1)}, f32[8,128]{1,0:T(8,128)S(1)}) custom-call(s32[2,8]{1,0:T(2,128)S(1)} %copy-done.2), custom_call_target="tpu_custom_call" | custom-call | tf_op jit(solution)/shard_map/pallas_call | solution.py:294
  10.8 0.0 copy-done.3
  10.8 0.0 copy-done.4
  10.8 0.0 copy-done.5
  10.8 9.5 %all-to-all-done = bf16[16,32,256]{2,1,0:T(8,128)(2,1)S(1)} async-done(((bf16[16,32,256]{2,1,0:T(8,128)(2,1)}), bf16[16,32,256]{2,1,0:T(8,128)(2,1)S(1)}, u32[]{:S(2)}, u32[]{:S(2)}) %all-to-all-start) | async-done | bytes 262176 | tf_op jit(solution)/shard_map/all_to_all | solution.py:260
  20.3 0.0 copy-done
  20.3 0.0 copy-done.1
  20.3 8.0 %shard_map.137 = (bf16[512,128]{1,0:T(8,128)(2,1)S(1)}, f32[512,128]{1,0:T(8,128)S(1)}, bf16[136,256]{1,0:T(8,128)(2,1)S(1)}, bf16[136,256]{1,0:T(8,128)(2,1)S(1)}) custom-call(bf16[512,256]{1,0:T(8,128)(2,1)S(1)} %bitcast.5, f32[1,640]{1,0:T(1,128)S(1)} %broadcast_in_dim.3.vectors_ref, bf16[128,384]{1,0:T(8,128)(2,1)S(1)} %copy-done, ...), custom_call_target="tpu_custom_call" | custom-call | tf_op jit(solution)/shard_map/pallas_call | solution.py:309
  28.3 0.1 collective-permute-start
  28.4 1.1 %shard_map.138 = (bf16[512,256]{1,0:T(8,128)(2,1)}, f32[8,128]{1,0:T(8,128)S(1)}) custom-call(bf16[512,256]{1,0:T(8,128)(2,1)S(1)} %bitcast.6, bf16[512,128]{1,0:T(8,128)(2,1)S(1)} %get-tuple-element.25.attn_ref, f32[512,128]{1,0:T(8,128)S(1)} %get-tuple-element.26.d_normed_ref, f32[1,640]{1,0:T(1,128)S(1)} %broadcast_in_dim.3.vectors_ref, ...), custom_call_target="tpu_custom_call" | custom-call | flops 536870912 | bytes 1048576 | tf_op jit(solution)/shard_map/pallas_call | solution.py:324
  29.5 0.2 collective-permute-done.refs_1_
  29.7 0.6 %collective-permute-start.1 = (bf16[136,256]{1,0:T(8,128)(2,1)S(1)}, bf16[136,256]{1,0:T(8,128)(2,1)S(1)}, u32[]{:S(2)}, u32[]{:S(2)}) collective-permute-start(bf16[136,256]{1,0:T(8,128)(2,1)S(1)} %shard_map.139.other_ref.refs_0_), channel_id=1, source_target_pairs={{0,8},{1,9},{2,10},{3,11},{4,12},{5,13},{6,14},{7,15},{8,0},{9,1},... | collective-permute-start | bytes 208904 | tf_op jit(solution)/shard_map/ppermute | solution.py:266
  30.3 4.1 %all-to-all-start.1 = ((bf16[16,32,256]{2,1,0:T(8,128)(2,1)}), bf16[16,32,256]{2,1,0:T(8,128)(2,1)S(1)}, u32[]{:S(2)}, u32[]{:S(2)}) async-start(bf16[16,32,256]{2,1,0:T(8,128)(2,1)} %bitcast.2), calls=%async_computation.1 | async-start | bytes 524288 | tf_op jit(solution)/shard_map/all_to_all | solution.py:260
  34.4 2.2 %collective-permute-done.1.refs_1_ = bf16[136,256]{1,0:T(8,128)(2,1)S(1)} collective-permute-done((bf16[136,256]{1,0:T(8,128)(2,1)S(1)}, bf16[136,256]{1,0:T(8,128)(2,1)S(1)}, u32[]{:S(2)}, u32[]{:S(2)}) %collective-permute-start.1) | collective-permute-done | bytes 69664 | tf_op jit(solution)/shard_map/ppermute | solution.py:266
  36.6 0.7 %collective-permute-start.4 = (bf16[136,256]{1,0:T(8,128)(2,1)S(1)}, bf16[136,256]{1,0:T(8,128)(2,1)S(1)}, u32[]{:S(2)}, u32[]{:S(2)}) collective-permute-start(bf16[136,256]{1,0:T(8,128)(2,1)S(1)} %shard_map.142.refs_0_), channel_id=1, source_target_pairs={{0,6},{1,7},{2,4},{3,5},{4,2},{5,3},{6,0},{7,1},{8,14},{9,15},{10,... | collective-permute-start | bytes 208904 | tf_op jit(solution)/shard_map/ppermute | solution.py:266
  37.3 1.0 %collective-permute-start.3 = (bf16[136,256]{1,0:T(8,128)(2,1)S(1)}, bf16[136,256]{1,0:T(8,128)(2,1)S(1)}, u32[]{:S(2)}, u32[]{:S(2)}) collective-permute-start(bf16[136,256]{1,0:T(8,128)(2,1)S(1)} %shard_map.142.refs_0_), channel_id=1, source_target_pairs={{0,4},{1,5},{2,6},{3,7},{4,0},{5,1},{6,2},{7,3},{8,12},{9,13},{10,... | collective-permute-start | bytes 208904 | tf_op jit(solution)/shard_map/ppermute | solution.py:266
  38.4 1.8 %collective-permute-start.2 = (bf16[136,256]{1,0:T(8,128)(2,1)S(1)}, bf16[136,256]{1,0:T(8,128)(2,1)S(1)}, u32[]{:S(2)}, u32[]{:S(2)}) collective-permute-start(bf16[136,256]{1,0:T(8,128)(2,1)S(1)} %shard_map.142.refs_0_), channel_id=1, source_target_pairs={{0,2},{1,3},{2,0},{3,1},{4,6},{5,7},{6,4},{7,5},{8,10},{9,11},{10,... | collective-permute-start | bytes 208904 | tf_op jit(solution)/shard_map/ppermute | solution.py:266
  40.2 3.7 %collective-permute-done.4.refs_3_ = bf16[136,256]{1,0:T(8,128)(2,1)S(1)} collective-permute-done((bf16[136,256]{1,0:T(8,128)(2,1)S(1)}, bf16[136,256]{1,0:T(8,128)(2,1)S(1)}, u32[]{:S(2)}, u32[]{:S(2)}) %collective-permute-start.4) | collective-permute-done | bytes 69664 | tf_op jit(solution)/shard_map/ppermute | solution.py:266
  43.9 0.9 %collective-permute-done.3.refs_2_ = bf16[136,256]{1,0:T(8,128)(2,1)S(1)} collective-permute-done((bf16[136,256]{1,0:T(8,128)(2,1)S(1)}, bf16[136,256]{1,0:T(8,128)(2,1)S(1)}, u32[]{:S(2)}, u32[]{:S(2)}) %collective-permute-start.3) | collective-permute-done | bytes 69664 | tf_op jit(solution)/shard_map/ppermute | solution.py:266
  44.7 0.0 collective-permute-done.2.refs_1_
  44.8 0.1 collective-permute-start.5
  44.9 0.0 all-to-all-done.1
  44.9 0.9 %shard_map.141 = (bf16[256,128]{1,0:T(8,128)(2,1)}, bf16[256,128]{1,0:T(8,128)(2,1)}, f32[8,128]{1,0:T(8,128)S(1)}) custom-call(bf16[256,512]{1,0:T(8,128)(2,1)S(1)} %get-tuple-element.23.pick_ref, bf16[512,256]{1,0:T(8,128)(2,1)S(1)} %bitcast.4), custom_call_target="tpu_custom_call" | custom-call | tf_op jit(solution)/shard_map/pallas_call | solution.py:336
  45.8 0.3 collective-permute-done.5.refs_1_
  46.1 0.7 %shard_map.144 = (f32[128]{0:T(128)}, f32[128,384]{1,0:T(8,128)}, f32[384]{0:T(512)}, f32[128,128]{1,0:T(8,128)}, f32[128]{0:T(128)}) custom-call(bf16[136,256]{1,0:T(8,128)(2,1)S(1)} %shard_map.143.refs_0_, bf16[136,256]{1,0:T(8,128)(2,1)S(1)} %collective-permute-done.5.refs_1_, f32[8,128]{1,0:T(8,128)S(1)} %get-tuple-element.33.refs_2_), custom_call_target="tpu_custom_call" | custom-call | tf_op jit(solution)/shard_map/pallas_call | solution.py:372
  (6 shorter events, 0.1 us)
Async XLA Ops:
  2.5 7.6 %copy-start.2 = (s32[2,8]{1,0:T(2,128)S(1)}, s32[2,8]{1,0:T(2,128)}, u32[]{:S(2)}) copy-start(s32[2,8]{1,0:T(2,128)} %route_hbm.3) | copy-start | bytes 196
  2.5 8.2 %copy-start.3 = (f32[384]{0:T(512)S(1)}, f32[384]{0:T(512)}, u32[]{:S(2)}) copy-start(f32[384]{0:T(512)} %param.14) | copy-start | bytes 4612
  2.6 17.7 %copy-start = (bf16[128,384]{1,0:T(8,128)(2,1)S(1)}, bf16[128,384]{1,0:T(8,128)(2,1)}, u32[]{:S(2)}) copy-start(bf16[128,384]{1,0:T(8,128)(2,1)} %w_qkv_hbm.1) | copy-start | bytes 294916
  2.6 17.7 %copy-start.1 = (bf16[128,128]{1,0:T(8,128)(2,1)S(1)}, bf16[128,128]{1,0:T(8,128)(2,1)}, u32[]{:S(2)}) copy-start(bf16[128,128]{1,0:T(8,128)(2,1)} %w_out_ref.1) | copy-start | bytes 98308
  2.6 17.7 %all-to-all-start = ((bf16[16,32,256]{2,1,0:T(8,128)(2,1)}), bf16[16,32,256]{2,1,0:T(8,128)(2,1)S(1)}, u32[]{:S(2)}, u32[]{:S(2)}) async-start(bf16[16,32,256]{2,1,0:T(8,128)(2,1)} %bitcast.7), calls=%async_computation | async-start | bytes 524288 | tf_op jit(solution)/shard_map/all_to_all | solution.py:260
  10.1 0.7 %copy-start.4 = (f32[128]{0:T(128)S(1)}, f32[128]{0:T(128)}, u32[]{:S(2)}) copy-start(f32[128]{0:T(128)} %param.16) | copy-start | bytes 1540
  10.1 0.7 %copy-start.5 = (f32[128]{0:T(128)S(1)}, f32[128]{0:T(128)}, u32[]{:S(2)}) copy-start(f32[128]{0:T(128)} %param.12) | copy-start | bytes 1540
  28.3 1.3 %collective-permute-start = (bf16[136,256]{1,0:T(8,128)(2,1)S(1)}, bf16[136,256]{1,0:T(8,128)(2,1)S(1)}, u32[]{:S(2)}, u32[]{:S(2)}) collective-permute-start(bf16[136,256]{1,0:T(8,128)(2,1)S(1)} %get-tuple-element.29), channel_id=1, source_target_pairs={{0,1},{1,0},{2,3},{3,2},{4,5},{5,4},{6,7},{7,6},{8,9},{9,8},{10,11... | collective-permute-start | bytes 208904 | tf_op jit(solution)/shard_map/ppermute | solution.py:266
  29.7 6.9 %collective-permute-start.1 = (bf16[136,256]{1,0:T(8,128)(2,1)S(1)}, bf16[136,256]{1,0:T(8,128)(2,1)S(1)}, u32[]{:S(2)}, u32[]{:S(2)}) collective-permute-start(bf16[136,256]{1,0:T(8,128)(2,1)S(1)} %shard_map.139.other_ref.refs_0_), channel_id=1, source_target_pairs={{0,8},{1,9},{2,10},{3,11},{4,12},{5,13},{6,14},{7,15},{8,0},{9,1},... | collective-permute-start | bytes 208904 | tf_op jit(solution)/shard_map/ppermute | solution.py:266
  30.3 14.5 %all-to-all-start.1 = ((bf16[16,32,256]{2,1,0:T(8,128)(2,1)}), bf16[16,32,256]{2,1,0:T(8,128)(2,1)S(1)}, u32[]{:S(2)}, u32[]{:S(2)}) async-start(bf16[16,32,256]{2,1,0:T(8,128)(2,1)} %bitcast.2), calls=%async_computation.1 | async-start | bytes 524288 | tf_op jit(solution)/shard_map/all_to_all | solution.py:260
  36.6 7.3 %collective-permute-start.4 = (bf16[136,256]{1,0:T(8,128)(2,1)S(1)}, bf16[136,256]{1,0:T(8,128)(2,1)S(1)}, u32[]{:S(2)}, u32[]{:S(2)}) collective-permute-start(bf16[136,256]{1,0:T(8,128)(2,1)S(1)} %shard_map.142.refs_0_), channel_id=1, source_target_pairs={{0,6},{1,7},{2,4},{3,5},{4,2},{5,3},{6,0},{7,1},{8,14},{9,15},{10,... | collective-permute-start | bytes 208904 | tf_op jit(solution)/shard_map/ppermute | solution.py:266
  37.3 7.4 %collective-permute-start.3 = (bf16[136,256]{1,0:T(8,128)(2,1)S(1)}, bf16[136,256]{1,0:T(8,128)(2,1)S(1)}, u32[]{:S(2)}, u32[]{:S(2)}) collective-permute-start(bf16[136,256]{1,0:T(8,128)(2,1)S(1)} %shard_map.142.refs_0_), channel_id=1, source_target_pairs={{0,4},{1,5},{2,6},{3,7},{4,0},{5,1},{6,2},{7,3},{8,12},{9,13},{10,... | collective-permute-start | bytes 208904 | tf_op jit(solution)/shard_map/ppermute | solution.py:266
  38.4 6.4 %collective-permute-start.2 = (bf16[136,256]{1,0:T(8,128)(2,1)S(1)}, bf16[136,256]{1,0:T(8,128)(2,1)S(1)}, u32[]{:S(2)}, u32[]{:S(2)}) collective-permute-start(bf16[136,256]{1,0:T(8,128)(2,1)S(1)} %shard_map.142.refs_0_), channel_id=1, source_target_pairs={{0,2},{1,3},{2,0},{3,1},{4,6},{5,7},{6,4},{7,5},{8,10},{9,11},{10,... | collective-permute-start | bytes 208904 | tf_op jit(solution)/shard_map/ppermute | solution.py:266
  44.8 1.3 %collective-permute-start.5 = (bf16[136,256]{1,0:T(8,128)(2,1)S(1)}, bf16[136,256]{1,0:T(8,128)(2,1)S(1)}, u32[]{:S(2)}, u32[]{:S(2)}) collective-permute-start(bf16[136,256]{1,0:T(8,128)(2,1)S(1)} %shard_map.143.refs_0_), channel_id=1, source_target_pairs={{0,1},{1,0},{2,3},{3,2},{4,5},{5,4},{6,7},{7,6},{8,9},{9,8},{10,11... | collective-permute-start | bytes 208904 | tf_op jit(solution)/shard_map/ppermute | solution.py:266

commit v6 on v5

--- a/solution.py
+++ b/solution.py
@@ -31,7 +31,7 @@
     top = devs.bit_length() - 2
     place = 0
     for bit in range(top + 1):
-        place = place + (((index >> bit) & 1) << (top - bit))
+        place = place + ((((index >> bit) & 1) ^ 1) << (top - bit))
     return place
 
 
@@ -107,13 +107,15 @@
     values_t = values.T
     keys_s = (keys.astype(F32) * scale).astype(BF16)
     lane = lax.broadcasted_iota(jnp.int32, (rows, width), 1)
-    hidden = jnp.where(points[:, :1] > EMPTY / 2, MASKED, 0.0)
+    hidden = jnp.where(points > EMPTY / 2, MASKED, 0.0).astype(BF16)
+    query_x = jnp.concatenate([query, jnp.where(lane == 0, 1.0, 0.0).astype(BF16)], axis=1)
 
     def own(h, array):
         return jnp.where((lane >= h * head) & (lane < (h + 1) * head), array, 0)
 
     def scores_of(h):
-        return matmul(own(h, keys_s), query, ((1,), (1,))) + hidden
+        keys_x = jnp.concatenate([own(h, keys_s), hidden], axis=1)
+        return matmul(keys_x, query_x, ((1,), (1,)))
 
     scores, probs, probs_b, d_probs, d_score = {}, {}, {}, {}, {}
     attn_t, dq_t = [], []

time: 47.3 us -> 47.1 us (level)
  waiting for transfers between devices: 16.7 us -> 11.5 us
  starting transfers between devices: 15.9 us -> 20.9 us
    all_to_all x2, starting transfers between devices: 11.6 us -> 15.3 us  [exchange(): lax.all_to_all(message, 'seq', split_axis=0, concat_axis=0, axis_index_gr...]
    all_to_all x2, waiting for transfers between devices: 9.48 us -> 5.8 us  [exchange(): lax.all_to_all(message, 'seq', split_axis=0, concat_axis=0, axis_index_gr...]
    ppermute x6, waiting for transfers between devices: 7.25 us -> 5.66 us  [swap(): lax.ppermute(piece, 'seq', [(dev, dev ^ step) for dev in range(devs)])]
    ppermute x6, starting transfers between devices: 4.34 us -> 5.61 us  [swap(): lax.ppermute(piece, 'seq', [(dev, dev ^ step) for dev in range(devs)])]
  transfers between devices with their start and end apart: 8 -> 8, of which waited for: 6 -> 4; matrix products, arithmetic and copies ran while one was open for 0% -> 0% of each run, Pallas kernels for 6% -> 6%
where the time goes in v6:
time: 47.1 us; the launch traced here: 46.7 us
  starting transfers between devices  20.9 us (44%)
  Pallas kernels  13.5 us (29%)
  waiting for transfers between devices  11.5 us (24%)
  between operations  0.79 us (2%)
    all_to_all x2, starting transfers between devices, exchange(): lax.all_to_all(message, 'seq', split_axis=0, concat_axis=0, axis_index_gr...  15.3 us
    pallas_call x1, Pallas kernels, local(): pl.pallas_call(functools.partial(owner_kernel, near), out_shape=(shape(he...  8.18 us
    all_to_all x2, waiting for transfers between devices, exchange(): lax.all_to_all(message, 'seq', split_axis=0, concat_axis=0, axis_index_gr...  5.8 us
    ppermute x6, waiting for transfers between devices, swap(): lax.ppermute(piece, 'seq', [(dev, dev ^ step) for dev in range(devs)])  5.66 us
    ppermute x6, starting transfers between devices, swap(): lax.ppermute(piece, 'seq', [(dev, dev ^ step) for dev in range(devs)])  5.61 us
    pallas_call x1, Pallas kernels, local(): pl.pallas_call(functools.partial(scatter_kernel, block_rows), out_shape=s...  1.89 us
    pallas_call x1, Pallas kernels, local(): pl.pallas_call(rows_kernel, out_shape=(shape(held, 2 * width), shape(8, 1...  1.09 us
  transfers between devices with their start and end apart: 8, of which 4 were waited for; matrix products, arithmetic and copies ran while one was open for 0% of the time, Pallas kernels for 6%

profile of v6, /device:TPU:0, one launch (start us, length us, event | category | flops | bytes accessed | tf_op | source)
XLA Modules:
  0.0 46.7 jit_solution(7482091448941608)
XLA Ops:
  0.6 1.9 %shard_map.136 = bf16[512,256]{1,0:T(8,128)(2,1)} custom-call(s32[2,8]{1,0:T(2,128)} %route_hbm.3, bf16[256,128]{1,0:T(8,128)(2,1)} %points_hbm.1, bf16[256,128]{1,0:T(8,128)(2,1)} %cot_hbm.1), custom_call_target="tpu_custom_call" | custom-call | tf_op jit(solution)/shard_map/pallas_call | solution.py:282
  2.5 0.0 copy-start.2
  2.5 0.0 copy-start.3
  2.6 0.0 copy-start
  2.6 0.0 copy-start.1
  2.6 9.0 %all-to-all-start = ((bf16[16,32,256]{2,1,0:T(8,128)(2,1)}), bf16[16,32,256]{2,1,0:T(8,128)(2,1)S(1)}, u32[]{:S(2)}, u32[]{:S(2)}) async-start(bf16[16,32,256]{2,1,0:T(8,128)(2,1)} %bitcast.7), calls=%async_computation | async-start | bytes 524288 | tf_op jit(solution)/shard_map/all_to_all | solution.py:262
  11.6 0.0 copy-done.2
  11.6 0.0 copy-start.4
  11.6 0.0 copy-start.5
  11.6 0.6 %shard_map.135 = (bf16[256,512]{1,0:T(8,128)(2,1)S(1)}, f32[8,128]{1,0:T(8,128)S(1)}) custom-call(s32[2,8]{1,0:T(2,128)S(1)} %copy-done.2), custom_call_target="tpu_custom_call" | custom-call | tf_op jit(solution)/shard_map/pallas_call | solution.py:296
  12.2 0.0 copy-done.3
  12.2 0.0 copy-done.4
  12.2 0.0 copy-done.5
  12.3 5.8 %all-to-all-done = bf16[16,32,256]{2,1,0:T(8,128)(2,1)S(1)} async-done(((bf16[16,32,256]{2,1,0:T(8,128)(2,1)}), bf16[16,32,256]{2,1,0:T(8,128)(2,1)S(1)}, u32[]{:S(2)}, u32[]{:S(2)}) %all-to-all-start) | async-done | bytes 262176 | tf_op jit(solution)/shard_map/all_to_all | solution.py:262
  18.1 0.0 copy-done
  18.1 0.0 copy-done.1
  18.1 8.2 %shard_map.137 = (bf16[512,128]{1,0:T(8,128)(2,1)S(1)}, f32[512,128]{1,0:T(8,128)S(1)}, bf16[136,256]{1,0:T(8,128)(2,1)S(1)}, bf16[136,256]{1,0:T(8,128)(2,1)S(1)}) custom-call(bf16[512,256]{1,0:T(8,128)(2,1)S(1)} %bitcast.5, f32[1,640]{1,0:T(1,128)S(1)} %broadcast_in_dim.3.vectors_ref, bf16[128,384]{1,0:T(8,128)(2,1)S(1)} %copy-done, ...), custom_call_target="tpu_custom_call" | custom-call | tf_op jit(solution)/shard_map/pallas_call | solution.py:311
  26.3 0.5 collective-permute-start
  26.7 1.1 %shard_map.138 = (bf16[512,256]{1,0:T(8,128)(2,1)}, f32[8,128]{1,0:T(8,128)S(1)}) custom-call(bf16[512,256]{1,0:T(8,128)(2,1)S(1)} %bitcast.6, bf16[512,128]{1,0:T(8,128)(2,1)S(1)} %get-tuple-element.25.attn_ref, f32[512,128]{1,0:T(8,128)S(1)} %get-tuple-element.26.d_normed_ref, f32[1,640]{1,0:T(1,128)S(1)} %broadcast_in_dim.3.vectors_ref, ...), custom_call_target="tpu_custom_call" | custom-call | flops 536870912 | bytes 1048576 | tf_op jit(solution)/shard_map/pallas_call | solution.py:326
  27.8 0.0 collective-permute-done.refs_1_
  27.9 1.5 %collective-permute-start.1 = (bf16[136,256]{1,0:T(8,128)(2,1)S(1)}, bf16[136,256]{1,0:T(8,128)(2,1)S(1)}, u32[]{:S(2)}, u32[]{:S(2)}) collective-permute-start(bf16[136,256]{1,0:T(8,128)(2,1)S(1)} %shard_map.139.other_ref.refs_0_), channel_id=1, source_target_pairs={{0,8},{1,9},{2,10},{3,11},{4,12},{5,13},{6,14},{7,15},{8,0},{9,1},... | collective-permute-start | bytes 208904 | tf_op jit(solution)/shard_map/ppermute | solution.py:268
  29.4 6.3 %all-to-all-start.1 = ((bf16[16,32,256]{2,1,0:T(8,128)(2,1)}), bf16[16,32,256]{2,1,0:T(8,128)(2,1)S(1)}, u32[]{:S(2)}, u32[]{:S(2)}) async-start(bf16[16,32,256]{2,1,0:T(8,128)(2,1)} %bitcast.2), calls=%async_computation.1 | async-start | bytes 524288 | tf_op jit(solution)/shard_map/all_to_all | solution.py:262
  35.7 0.0 collective-permute-done.1.refs_1_
  35.7 0.6 %collective-permute-start.4 = (bf16[136,256]{1,0:T(8,128)(2,1)S(1)}, bf16[136,256]{1,0:T(8,128)(2,1)S(1)}, u32[]{:S(2)}, u32[]{:S(2)}) collective-permute-start(bf16[136,256]{1,0:T(8,128)(2,1)S(1)} %shard_map.142.refs_0_), channel_id=1, source_target_pairs={{0,6},{1,7},{2,4},{3,5},{4,2},{5,3},{6,0},{7,1},{8,14},{9,15},{10,... | collective-permute-start | bytes 208904 | tf_op jit(solution)/shard_map/ppermute | solution.py:268
  36.3 1.6 %collective-permute-start.3 = (bf16[136,256]{1,0:T(8,128)(2,1)S(1)}, bf16[136,256]{1,0:T(8,128)(2,1)S(1)}, u32[]{:S(2)}, u32[]{:S(2)}) collective-permute-start(bf16[136,256]{1,0:T(8,128)(2,1)S(1)} %shard_map.142.refs_0_), channel_id=1, source_target_pairs={{0,4},{1,5},{2,6},{3,7},{4,0},{5,1},{6,2},{7,3},{8,12},{9,13},{10,... | collective-permute-start | bytes 208904 | tf_op jit(solution)/shard_map/ppermute | solution.py:268
  38.0 1.3 %collective-permute-start.2 = (bf16[136,256]{1,0:T(8,128)(2,1)S(1)}, bf16[136,256]{1,0:T(8,128)(2,1)S(1)}, u32[]{:S(2)}, u32[]{:S(2)}) collective-permute-start(bf16[136,256]{1,0:T(8,128)(2,1)S(1)} %shard_map.142.refs_0_), channel_id=1, source_target_pairs={{0,2},{1,3},{2,0},{3,1},{4,6},{5,7},{6,4},{7,5},{8,10},{9,11},{10,... | collective-permute-start | bytes 208904 | tf_op jit(solution)/shard_map/ppermute | solution.py:268
  39.3 4.1 %collective-permute-done.4.refs_3_ = bf16[136,256]{1,0:T(8,128)(2,1)S(1)} collective-permute-done((bf16[136,256]{1,0:T(8,128)(2,1)S(1)}, bf16[136,256]{1,0:T(8,128)(2,1)S(1)}, u32[]{:S(2)}, u32[]{:S(2)}) %collective-permute-start.4) | collective-permute-done | bytes 69664 | tf_op jit(solution)/shard_map/ppermute | solution.py:268
  43.4 1.2 %collective-permute-done.3.refs_2_ = bf16[136,256]{1,0:T(8,128)(2,1)S(1)} collective-permute-done((bf16[136,256]{1,0:T(8,128)(2,1)S(1)}, bf16[136,256]{1,0:T(8,128)(2,1)S(1)}, u32[]{:S(2)}, u32[]{:S(2)}) %collective-permute-start.3) | collective-permute-done | bytes 69664 | tf_op jit(solution)/shard_map/ppermute | solution.py:268
  44.6 0.0 collective-permute-done.2.refs_1_
  44.6 0.1 collective-permute-start.5
  44.7 0.0 all-to-all-done.1
  44.7 0.9 %shard_map.141 = (bf16[256,128]{1,0:T(8,128)(2,1)}, bf16[256,128]{1,0:T(8,128)(2,1)}, f32[8,128]{1,0:T(8,128)S(1)}) custom-call(bf16[256,512]{1,0:T(8,128)(2,1)S(1)} %get-tuple-element.23.pick_ref, bf16[512,256]{1,0:T(8,128)(2,1)S(1)} %bitcast.4), custom_call_target="tpu_custom_call" | custom-call | tf_op jit(solution)/shard_map/pallas_call | solution.py:338
  45.6 0.3 collective-permute-done.5.refs_1_
  46.0 0.7 %shard_map.144 = (f32[128]{0:T(128)}, f32[128,384]{1,0:T(8,128)}, f32[384]{0:T(512)}, f32[128,128]{1,0:T(8,128)}, f32[128]{0:T(128)}) custom-call(bf16[136,256]{1,0:T(8,128)(2,1)S(1)} %shard_map.143.refs_0_, bf16[136,256]{1,0:T(8,128)(2,1)S(1)} %collective-permute-done.5.refs_1_, f32[8,128]{1,0:T(8,128)S(1)} %get-tuple-element.33.refs_2_), custom_call_target="tpu_custom_call" | custom-call | tf_op jit(solution)/shard_map/pallas_call | solution.py:374
  (6 shorter events, 0.1 us)
Async XLA Ops:
  2.5 9.0 %copy-start.2 = (s32[2,8]{1,0:T(2,128)S(1)}, s32[2,8]{1,0:T(2,128)}, u32[]{:S(2)}) copy-start(s32[2,8]{1,0:T(2,128)} %route_hbm.3) | copy-start | bytes 196
  2.5 9.7 %copy-start.3 = (f32[384]{0:T(512)S(1)}, f32[384]{0:T(512)}, u32[]{:S(2)}) copy-start(f32[384]{0:T(512)} %param.14) | copy-start | bytes 4612
  2.6 15.5 %copy-start = (bf16[128,384]{1,0:T(8,128)(2,1)S(1)}, bf16[128,384]{1,0:T(8,128)(2,1)}, u32[]{:S(2)}) copy-start(bf16[128,384]{1,0:T(8,128)(2,1)} %w_qkv_hbm.1) | copy-start | bytes 294916
  2.6 15.5 %copy-start.1 = (bf16[128,128]{1,0:T(8,128)(2,1)S(1)}, bf16[128,128]{1,0:T(8,128)(2,1)}, u32[]{:S(2)}) copy-start(bf16[128,128]{1,0:T(8,128)(2,1)} %w_out_ref.1) | copy-start | bytes 98308
  2.6 15.5 %all-to-all-start = ((bf16[16,32,256]{2,1,0:T(8,128)(2,1)}), bf16[16,32,256]{2,1,0:T(8,128)(2,1)S(1)}, u32[]{:S(2)}, u32[]{:S(2)}) async-start(bf16[16,32,256]{2,1,0:T(8,128)(2,1)} %bitcast.7), calls=%async_computation | async-start | bytes 524288 | tf_op jit(solution)/shard_map/all_to_all | solution.py:262
  11.6 0.7 %copy-start.4 = (f32[128]{0:T(128)S(1)}, f32[128]{0:T(128)}, u32[]{:S(2)}) copy-start(f32[128]{0:T(128)} %param.16) | copy-start | bytes 1540
  11.6 0.7 %copy-start.5 = (f32[128]{0:T(128)S(1)}, f32[128]{0:T(128)}, u32[]{:S(2)}) copy-start(f32[128]{0:T(128)} %param.12) | copy-start | bytes 1540
  26.3 1.6 %collective-permute-start = (bf16[136,256]{1,0:T(8,128)(2,1)S(1)}, bf16[136,256]{1,0:T(8,128)(2,1)S(1)}, u32[]{:S(2)}, u32[]{:S(2)}) collective-permute-start(bf16[136,256]{1,0:T(8,128)(2,1)S(1)} %get-tuple-element.29), channel_id=1, source_target_pairs={{0,1},{1,0},{2,3},{3,2},{4,5},{5,4},{6,7},{7,6},{8,9},{9,8},{10,11... | collective-permute-start | bytes 208904 | tf_op jit(solution)/shard_map/ppermute | solution.py:268
  27.9 7.8 %collective-permute-start.1 = (bf16[136,256]{1,0:T(8,128)(2,1)S(1)}, bf16[136,256]{1,0:T(8,128)(2,1)S(1)}, u32[]{:S(2)}, u32[]{:S(2)}) collective-permute-start(bf16[136,256]{1,0:T(8,128)(2,1)S(1)} %shard_map.139.other_ref.refs_0_), channel_id=1, source_target_pairs={{0,8},{1,9},{2,10},{3,11},{4,12},{5,13},{6,14},{7,15},{8,0},{9,1},... | collective-permute-start | bytes 208904 | tf_op jit(solution)/shard_map/ppermute | solution.py:268
  29.4 15.3 %all-to-all-start.1 = ((bf16[16,32,256]{2,1,0:T(8,128)(2,1)}), bf16[16,32,256]{2,1,0:T(8,128)(2,1)S(1)}, u32[]{:S(2)}, u32[]{:S(2)}) async-start(bf16[16,32,256]{2,1,0:T(8,128)(2,1)} %bitcast.2), calls=%async_computation.1 | async-start | bytes 524288 | tf_op jit(solution)/shard_map/all_to_all | solution.py:262
  35.7 7.7 %collective-permute-start.4 = (bf16[136,256]{1,0:T(8,128)(2,1)S(1)}, bf16[136,256]{1,0:T(8,128)(2,1)S(1)}, u32[]{:S(2)}, u32[]{:S(2)}) collective-permute-start(bf16[136,256]{1,0:T(8,128)(2,1)S(1)} %shard_map.142.refs_0_), channel_id=1, source_target_pairs={{0,6},{1,7},{2,4},{3,5},{4,2},{5,3},{6,0},{7,1},{8,14},{9,15},{10,... | collective-permute-start | bytes 208904 | tf_op jit(solution)/shard_map/ppermute | solution.py:268
  36.3 8.2 %collective-permute-start.3 = (bf16[136,256]{1,0:T(8,128)(2,1)S(1)}, bf16[136,256]{1,0:T(8,128)(2,1)S(1)}, u32[]{:S(2)}, u32[]{:S(2)}) collective-permute-start(bf16[136,256]{1,0:T(8,128)(2,1)S(1)} %shard_map.142.refs_0_), channel_id=1, source_target_pairs={{0,4},{1,5},{2,6},{3,7},{4,0},{5,1},{6,2},{7,3},{8,12},{9,13},{10,... | collective-permute-start | bytes 208904 | tf_op jit(solution)/shard_map/ppermute | solution.py:268
  38.0 6.6 %collective-permute-start.2 = (bf16[136,256]{1,0:T(8,128)(2,1)S(1)}, bf16[136,256]{1,0:T(8,128)(2,1)S(1)}, u32[]{:S(2)}, u32[]{:S(2)}) collective-permute-start(bf16[136,256]{1,0:T(8,128)(2,1)S(1)} %shard_map.142.refs_0_), channel_id=1, source_target_pairs={{0,2},{1,3},{2,0},{3,1},{4,6},{5,7},{6,4},{7,5},{8,10},{9,11},{10,... | collective-permute-start | bytes 208904 | tf_op jit(solution)/shard_map/ppermute | solution.py:268
  44.6 1.3 %collective-permute-start.5 = (bf16[136,256]{1,0:T(8,128)(2,1)S(1)}, bf16[136,256]{1,0:T(8,128)(2,1)S(1)}, u32[]{:S(2)}, u32[]{:S(2)}) collective-permute-start(bf16[136,256]{1,0:T(8,128)(2,1)S(1)} %shard_map.143.refs_0_), channel_id=1, source_target_pairs={{0,1},{1,0},{2,3},{3,2},{4,5},{5,4},{6,7},{7,6},{8,9},{9,8},{10,11... | collective-permute-start | bytes 208904 | tf_op jit(solution)/shard_map/ppermute | solution.py:268

commit v7 on v5

--- a/solution.py
+++ b/solution.py
@@ -31,7 +31,7 @@
     top = devs.bit_length() - 2
     place = 0
     for bit in range(top + 1):
-        place = place + (((index >> bit) & 1) << (top - bit))
+        place = place + ((((index >> bit) & 1) ^ 1) << (top - bit))
     return place
 
 
@@ -45,7 +45,8 @@
     return target
 
 
-def scatter_kernel(block_rows, route_hbm, points_hbm, cot_hbm, out_ref, route_ref, points_ref, cot_ref, sems):
+def scatter_kernel(block_rows, route_hbm, points_hbm, cot_hbm, out_hbm, *refs):
+    route_ref, points_ref, cot_ref, points_out, cot_out, sems = refs
     copies = [
         pltpu.make_async_copy(source, target, sems.at[at])
         for at, (source, target) in enumerate(
@@ -56,16 +57,24 @@
         copy.start()
     copies[0].wait()
     rows, width = points_ref.shape
-    target = send_rows(route_ref, (1, rows), 1, block_rows, out_ref.shape[0] // block_rows)
-    index = lax.broadcasted_iota(jnp.int32, (out_ref.shape[0], rows), 0)
+    target = send_rows(route_ref, (1, rows), 1, block_rows, out_hbm.shape[0] // block_rows)
+    index = lax.broadcasted_iota(jnp.int32, (out_hbm.shape[0], rows), 0)
     pick = jnp.where(index == target, 1.0, 0.0).astype(BF16)
-    for copy in copies[1:]:
-        copy.wait()
+    backs = [
+        pltpu.make_async_copy(cot_out, out_hbm.at[:, width:], sems.at[3]),
+        pltpu.make_async_copy(points_out, out_hbm.at[:, :width], sems.at[4]),
+    ]
+    copies[2].wait()
+    cot_out[...] = matmul(pick, cot_ref[...]).astype(BF16)
+    backs[0].start()
+    copies[1].wait()
     ones = jnp.ones((rows, width), BF16)
     moved = matmul(pick, jnp.concatenate([points_ref[...], ones], axis=1))
     empty = (1.0 - moved[:, width:]) * EMPTY
-    out_ref[:, :width] = (moved[:, :width] + empty).astype(BF16)
-    out_ref[:, width:] = matmul(pick, cot_ref[...]).astype(BF16)
+    points_out[...] = (moved[:, :width] + empty).astype(BF16)
+    backs[1].start()
+    for back in backs:
+        back.wait()
 
 
 def normalize(points):
@@ -281,12 +290,14 @@
         functools.partial(scatter_kernel, block_rows),
         out_shape=shape(held, 2 * width),
         in_specs=[ANY] * 3,
-        out_specs=VMEM,
+        out_specs=ANY,
         scratch_shapes=[
             pltpu.SMEM(route.shape, route.dtype),
             pltpu.VMEM(points.shape, points.dtype),
             pltpu.VMEM(cotangent.shape, cotangent.dtype),
-            pltpu.SemaphoreType.DMA((3,)),
+            pltpu.VMEM((held, width), BF16),
+            pltpu.VMEM((held, width), BF16),
+            pltpu.SemaphoreType.DMA((5,)),
         ],
     )(route, points, cotangent)
     got = exchange(sent.reshape(devs, block_rows, 2 * width)).reshape(held, 2 * width)

time: 47.3 us -> 47.2 us (level)
  waiting for transfers between devices: 16.7 us -> 11.5 us
  starting transfers between devices: 15.9 us -> 20.9 us
    all_to_all x2, starting transfers between devices: 11.6 us -> 15.3 us  [exchange(): lax.all_to_all(message, 'seq', split_axis=0, concat_axis=0, axis_index_gr...]
    all_to_all x2, waiting for transfers between devices: 9.48 us -> 5.8 us  [exchange(): lax.all_to_all(message, 'seq', split_axis=0, concat_axis=0, axis_index_gr...]
    ppermute x6, waiting for transfers between devices: 7.25 us -> 5.66 us  [swap(): lax.ppermute(piece, 'seq', [(dev, dev ^ step) for dev in range(devs)])]
    ppermute x6, starting transfers between devices: 4.34 us -> 5.61 us  [swap(): lax.ppermute(piece, 'seq', [(dev, dev ^ step) for dev in range(devs)])]
  transfers between devices with their start and end apart: 8 -> 8, of which waited for: 6 -> 4; matrix products, arithmetic and copies ran while one was open for 0% -> 0% of each run, Pallas kernels for 6% -> 6%
where the time goes in v7:
time: 47.2 us; the launch traced here: 46.8 us
  starting transfers between devices  20.9 us (44%)
  Pallas kernels  13.6 us (29%)
  waiting for transfers between devices  11.5 us (24%)
  between operations  0.79 us (2%)
    all_to_all x2, starting transfers between devices, exchange(): lax.all_to_all(message, 'seq', split_axis=0, concat_axis=0, axis_index_gr...  15.3 us
    pallas_call x1, Pallas kernels, local(): pl.pallas_call(functools.partial(owner_kernel, near), out_shape=(shape(he...  8.04 us
    all_to_all x2, waiting for transfers between devices, exchange(): lax.all_to_all(message, 'seq', split_axis=0, concat_axis=0, axis_index_gr...  5.8 us
    ppermute x6, waiting for transfers between devices, swap(): lax.ppermute(piece, 'seq', [(dev, dev ^ step) for dev in range(devs)])  5.66 us
    ppermute x6, starting transfers between devices, swap(): lax.ppermute(piece, 'seq', [(dev, dev ^ step) for dev in range(devs)])  5.61 us
    pallas_call x1, Pallas kernels, local(): pl.pallas_call(functools.partial(scatter_kernel, block_rows), out_shape=s...  2.15 us
    pallas_call x1, Pallas kernels, local(): pl.pallas_call(rows_kernel, out_shape=(shape(held, 2 * width), shape(8, 1...  1.09 us
  transfers between devices with their start and end apart: 8, of which 4 were waited for; matrix products, arithmetic and copies ran while one was open for 0% of the time, Pallas kernels for 6%

profile of v7, /device:TPU:0, one launch (start us, length us, event | category | flops | bytes accessed | tf_op | source)
XLA Modules:
  0.0 46.8 jit_solution(455462863882939682)
XLA Ops:
  0.6 2.1 %shard_map.136 = bf16[512,256]{1,0:T(8,128)(2,1)} custom-call(s32[2,8]{1,0:T(2,128)} %route_hbm.3, bf16[256,128]{1,0:T(8,128)(2,1)} %points_hbm.1, bf16[256,128]{1,0:T(8,128)(2,1)} %cot_hbm.1), custom_call_target="tpu_custom_call" | custom-call | tf_op jit(solution)/shard_map/pallas_call | solution.py:289
  2.8 0.0 copy-start.2
  2.8 0.0 copy-start.3
  2.8 0.0 copy-start
  2.8 0.0 copy-start.1
  2.8 9.0 %all-to-all-start = ((bf16[16,32,256]{2,1,0:T(8,128)(2,1)}), bf16[16,32,256]{2,1,0:T(8,128)(2,1)S(1)}, u32[]{:S(2)}, u32[]{:S(2)}) async-start(bf16[16,32,256]{2,1,0:T(8,128)(2,1)} %bitcast.7), calls=%async_computation | async-start | bytes 524288 | tf_op jit(solution)/shard_map/all_to_all | solution.py:269
  11.8 0.0 copy-done.2
  11.8 0.0 copy-start.4
  11.8 0.0 copy-start.5
  11.8 0.6 %shard_map.135 = (bf16[256,512]{1,0:T(8,128)(2,1)S(1)}, f32[8,128]{1,0:T(8,128)S(1)}) custom-call(s32[2,8]{1,0:T(2,128)S(1)} %copy-done.2), custom_call_target="tpu_custom_call" | custom-call | tf_op jit(solution)/shard_map/pallas_call | solution.py:305
  12.5 0.0 copy-done.3
  12.5 0.0 copy-done.4
  12.5 0.0 copy-done.5
  12.5 5.8 %all-to-all-done = bf16[16,32,256]{2,1,0:T(8,128)(2,1)S(1)} async-done(((bf16[16,32,256]{2,1,0:T(8,128)(2,1)}), bf16[16,32,256]{2,1,0:T(8,128)(2,1)S(1)}, u32[]{:S(2)}, u32[]{:S(2)}) %all-to-all-start) | async-done | bytes 262176 | tf_op jit(solution)/shard_map/all_to_all | solution.py:269
  18.3 0.0 copy-done
  18.3 0.0 copy-done.1
  18.3 8.0 %shard_map.137 = (bf16[512,128]{1,0:T(8,128)(2,1)S(1)}, f32[512,128]{1,0:T(8,128)S(1)}, bf16[136,256]{1,0:T(8,128)(2,1)S(1)}, bf16[136,256]{1,0:T(8,128)(2,1)S(1)}) custom-call(bf16[512,256]{1,0:T(8,128)(2,1)S(1)} %bitcast.5, f32[1,640]{1,0:T(1,128)S(1)} %broadcast_in_dim.3.vectors_ref, bf16[128,384]{1,0:T(8,128)(2,1)S(1)} %copy-done, ...), custom_call_target="tpu_custom_call" | custom-call | tf_op jit(solution)/shard_map/pallas_call | solution.py:320
  26.4 0.5 collective-permute-start
  26.8 1.1 %shard_map.138 = (bf16[512,256]{1,0:T(8,128)(2,1)}, f32[8,128]{1,0:T(8,128)S(1)}) custom-call(bf16[512,256]{1,0:T(8,128)(2,1)S(1)} %bitcast.6, bf16[512,128]{1,0:T(8,128)(2,1)S(1)} %get-tuple-element.25.attn_ref, f32[512,128]{1,0:T(8,128)S(1)} %get-tuple-element.26.d_normed_ref, f32[1,640]{1,0:T(1,128)S(1)} %broadcast_in_dim.3.vectors_ref, ...), custom_call_target="tpu_custom_call" | custom-call | flops 536870912 | bytes 1048576 | tf_op jit(solution)/shard_map/pallas_call | solution.py:335
  27.9 0.0 collective-permute-done.refs_1_
  28.0 1.5 %collective-permute-start.1 = (bf16[136,256]{1,0:T(8,128)(2,1)S(1)}, bf16[136,256]{1,0:T(8,128)(2,1)S(1)}, u32[]{:S(2)}, u32[]{:S(2)}) collective-permute-start(bf16[136,256]{1,0:T(8,128)(2,1)S(1)} %shard_map.139.other_ref.refs_0_), channel_id=1, source_target_pairs={{0,8},{1,9},{2,10},{3,11},{4,12},{5,13},{6,14},{7,15},{8,0},{9,1},... | collective-permute-start | bytes 208904 | tf_op jit(solution)/shard_map/ppermute | solution.py:275
  29.5 6.3 %all-to-all-start.1 = ((bf16[16,32,256]{2,1,0:T(8,128)(2,1)}), bf16[16,32,256]{2,1,0:T(8,128)(2,1)S(1)}, u32[]{:S(2)}, u32[]{:S(2)}) async-start(bf16[16,32,256]{2,1,0:T(8,128)(2,1)} %bitcast.2), calls=%async_computation.1 | async-start | bytes 524288 | tf_op jit(solution)/shard_map/all_to_all | solution.py:269
  35.8 0.0 collective-permute-done.1.refs_1_
  35.8 0.6 %collective-permute-start.4 = (bf16[136,256]{1,0:T(8,128)(2,1)S(1)}, bf16[136,256]{1,0:T(8,128)(2,1)S(1)}, u32[]{:S(2)}, u32[]{:S(2)}) collective-permute-start(bf16[136,256]{1,0:T(8,128)(2,1)S(1)} %shard_map.142.refs_0_), channel_id=1, source_target_pairs={{0,6},{1,7},{2,4},{3,5},{4,2},{5,3},{6,0},{7,1},{8,14},{9,15},{10,... | collective-permute-start | bytes 208904 | tf_op jit(solution)/shard_map/ppermute | solution.py:275
  36.4 1.6 %collective-permute-start.3 = (bf16[136,256]{1,0:T(8,128)(2,1)S(1)}, bf16[136,256]{1,0:T(8,128)(2,1)S(1)}, u32[]{:S(2)}, u32[]{:S(2)}) collective-permute-start(bf16[136,256]{1,0:T(8,128)(2,1)S(1)} %shard_map.142.refs_0_), channel_id=1, source_target_pairs={{0,4},{1,5},{2,6},{3,7},{4,0},{5,1},{6,2},{7,3},{8,12},{9,13},{10,... | collective-permute-start | bytes 208904 | tf_op jit(solution)/shard_map/ppermute | solution.py:275
  38.1 1.3 %collective-permute-start.2 = (bf16[136,256]{1,0:T(8,128)(2,1)S(1)}, bf16[136,256]{1,0:T(8,128)(2,1)S(1)}, u32[]{:S(2)}, u32[]{:S(2)}) collective-permute-start(bf16[136,256]{1,0:T(8,128)(2,1)S(1)} %shard_map.142.refs_0_), channel_id=1, source_target_pairs={{0,2},{1,3},{2,0},{3,1},{4,6},{5,7},{6,4},{7,5},{8,10},{9,11},{10,... | collective-permute-start | bytes 208904 | tf_op jit(solution)/shard_map/ppermute | solution.py:275
  39.4 4.1 %collective-permute-done.4.refs_3_ = bf16[136,256]{1,0:T(8,128)(2,1)S(1)} collective-permute-done((bf16[136,256]{1,0:T(8,128)(2,1)S(1)}, bf16[136,256]{1,0:T(8,128)(2,1)S(1)}, u32[]{:S(2)}, u32[]{:S(2)}) %collective-permute-start.4) | collective-permute-done | bytes 69664 | tf_op jit(solution)/shard_map/ppermute | solution.py:275
  43.5 1.2 %collective-permute-done.3.refs_2_ = bf16[136,256]{1,0:T(8,128)(2,1)S(1)} collective-permute-done((bf16[136,256]{1,0:T(8,128)(2,1)S(1)}, bf16[136,256]{1,0:T(8,128)(2,1)S(1)}, u32[]{:S(2)}, u32[]{:S(2)}) %collective-permute-start.3) | collective-permute-done | bytes 69664 | tf_op jit(solution)/shard_map/ppermute | solution.py:275
  44.7 0.0 collective-permute-done.2.refs_1_
  44.7 0.1 collective-permute-start.5
  44.8 0.0 all-to-all-done.1
  44.8 0.9 %shard_map.141 = (bf16[256,128]{1,0:T(8,128)(2,1)}, bf16[256,128]{1,0:T(8,128)(2,1)}, f32[8,128]{1,0:T(8,128)S(1)}) custom-call(bf16[256,512]{1,0:T(8,128)(2,1)S(1)} %get-tuple-element.23.pick_ref, bf16[512,256]{1,0:T(8,128)(2,1)S(1)} %bitcast.4), custom_call_target="tpu_custom_call" | custom-call | tf_op jit(solution)/shard_map/pallas_call | solution.py:347
  45.7 0.3 collective-permute-done.5.refs_1_
  46.0 0.7 %shard_map.144 = (f32[128]{0:T(128)}, f32[128,384]{1,0:T(8,128)}, f32[384]{0:T(512)}, f32[128,128]{1,0:T(8,128)}, f32[128]{0:T(128)}) custom-call(bf16[136,256]{1,0:T(8,128)(2,1)S(1)} %shard_map.143.refs_0_, bf16[136,256]{1,0:T(8,128)(2,1)S(1)} %collective-permute-done.5.refs_1_, f32[8,128]{1,0:T(8,128)S(1)} %get-tuple-element.33.refs_2_), custom_call_target="tpu_custom_call" | custom-call | tf_op jit(solution)/shard_map/pallas_call | solution.py:383
  (6 shorter events, 0.1 us)
Async XLA Ops:
  2.8 9.0 %copy-start.2 = (s32[2,8]{1,0:T(2,128)S(1)}, s32[2,8]{1,0:T(2,128)}, u32[]{:S(2)}) copy-start(s32[2,8]{1,0:T(2,128)} %route_hbm.3) | copy-start | bytes 196
  2.8 9.7 %copy-start.3 = (f32[384]{0:T(512)S(1)}, f32[384]{0:T(512)}, u32[]{:S(2)}) copy-start(f32[384]{0:T(512)} %param.14) | copy-start | bytes 4612
  2.8 15.5 %copy-start = (bf16[128,384]{1,0:T(8,128)(2,1)S(1)}, bf16[128,384]{1,0:T(8,128)(2,1)}, u32[]{:S(2)}) copy-start(bf16[128,384]{1,0:T(8,128)(2,1)} %w_qkv_hbm.1) | copy-start | bytes 294916
  2.8 15.5 %copy-start.1 = (bf16[128,128]{1,0:T(8,128)(2,1)S(1)}, bf16[128,128]{1,0:T(8,128)(2,1)}, u32[]{:S(2)}) copy-start(bf16[128,128]{1,0:T(8,128)(2,1)} %w_out_ref.1) | copy-start | bytes 98308
  2.8 15.5 %all-to-all-start = ((bf16[16,32,256]{2,1,0:T(8,128)(2,1)}), bf16[16,32,256]{2,1,0:T(8,128)(2,1)S(1)}, u32[]{:S(2)}, u32[]{:S(2)}) async-start(bf16[16,32,256]{2,1,0:T(8,128)(2,1)} %bitcast.7), calls=%async_computation | async-start | bytes 524288 | tf_op jit(solution)/shard_map/all_to_all | solution.py:269
  11.8 0.7 %copy-start.4 = (f32[128]{0:T(128)S(1)}, f32[128]{0:T(128)}, u32[]{:S(2)}) copy-start(f32[128]{0:T(128)} %param.16) | copy-start | bytes 1540
  11.8 0.7 %copy-start.5 = (f32[128]{0:T(128)S(1)}, f32[128]{0:T(128)}, u32[]{:S(2)}) copy-start(f32[128]{0:T(128)} %param.12) | copy-start | bytes 1540
  26.4 1.6 %collective-permute-start = (bf16[136,256]{1,0:T(8,128)(2,1)S(1)}, bf16[136,256]{1,0:T(8,128)(2,1)S(1)}, u32[]{:S(2)}, u32[]{:S(2)}) collective-permute-start(bf16[136,256]{1,0:T(8,128)(2,1)S(1)} %get-tuple-element.29), channel_id=1, source_target_pairs={{0,1},{1,0},{2,3},{3,2},{4,5},{5,4},{6,7},{7,6},{8,9},{9,8},{10,11... | collective-permute-start | bytes 208904 | tf_op jit(solution)/shard_map/ppermute | solution.py:275
  28.0 7.8 %collective-permute-start.1 = (bf16[136,256]{1,0:T(8,128)(2,1)S(1)}, bf16[136,256]{1,0:T(8,128)(2,1)S(1)}, u32[]{:S(2)}, u32[]{:S(2)}) collective-permute-start(bf16[136,256]{1,0:T(8,128)(2,1)S(1)} %shard_map.139.other_ref.refs_0_), channel_id=1, source_target_pairs={{0,8},{1,9},{2,10},{3,11},{4,12},{5,13},{6,14},{7,15},{8,0},{9,1},... | collective-permute-start | bytes 208904 | tf_op jit(solution)/shard_map/ppermute | solution.py:275
  29.5 15.3 %all-to-all-start.1 = ((bf16[16,32,256]{2,1,0:T(8,128)(2,1)}), bf16[16,32,256]{2,1,0:T(8,128)(2,1)S(1)}, u32[]{:S(2)}, u32[]{:S(2)}) async-start(bf16[16,32,256]{2,1,0:T(8,128)(2,1)} %bitcast.2), calls=%async_computation.1 | async-start | bytes 524288 | tf_op jit(solution)/shard_map/all_to_all | solution.py:269
  35.8 7.7 %collective-permute-start.4 = (bf16[136,256]{1,0:T(8,128)(2,1)S(1)}, bf16[136,256]{1,0:T(8,128)(2,1)S(1)}, u32[]{:S(2)}, u32[]{:S(2)}) collective-permute-start(bf16[136,256]{1,0:T(8,128)(2,1)S(1)} %shard_map.142.refs_0_), channel_id=1, source_target_pairs={{0,6},{1,7},{2,4},{3,5},{4,2},{5,3},{6,0},{7,1},{8,14},{9,15},{10,... | collective-permute-start | bytes 208904 | tf_op jit(solution)/shard_map/ppermute | solution.py:275
  36.4 8.2 %collective-permute-start.3 = (bf16[136,256]{1,0:T(8,128)(2,1)S(1)}, bf16[136,256]{1,0:T(8,128)(2,1)S(1)}, u32[]{:S(2)}, u32[]{:S(2)}) collective-permute-start(bf16[136,256]{1,0:T(8,128)(2,1)S(1)} %shard_map.142.refs_0_), channel_id=1, source_target_pairs={{0,4},{1,5},{2,6},{3,7},{4,0},{5,1},{6,2},{7,3},{8,12},{9,13},{10,... | collective-permute-start | bytes 208904 | tf_op jit(solution)/shard_map/ppermute | solution.py:275
  38.1 6.6 %collective-permute-start.2 = (bf16[136,256]{1,0:T(8,128)(2,1)S(1)}, bf16[136,256]{1,0:T(8,128)(2,1)S(1)}, u32[]{:S(2)}, u32[]{:S(2)}) collective-permute-start(bf16[136,256]{1,0:T(8,128)(2,1)S(1)} %shard_map.142.refs_0_), channel_id=1, source_target_pairs={{0,2},{1,3},{2,0},{3,1},{4,6},{5,7},{6,4},{7,5},{8,10},{9,11},{10,... | collective-permute-start | bytes 208904 | tf_op jit(solution)/shard_map/ppermute | solution.py:275
  44.7 1.3 %collective-permute-start.5 = (bf16[136,256]{1,0:T(8,128)(2,1)S(1)}, bf16[136,256]{1,0:T(8,128)(2,1)S(1)}, u32[]{:S(2)}, u32[]{:S(2)}) collective-permute-start(bf16[136,256]{1,0:T(8,128)(2,1)S(1)} %shard_map.143.refs_0_), channel_id=1, source_target_pairs={{0,1},{1,0},{2,3},{3,2},{4,5},{5,4},{6,7},{7,6},{8,9},{9,8},{10,11... | collective-permute-start | bytes 208904 | tf_op jit(solution)/shard_map/ppermute | solution.py:275

commit v8 on v5

--- a/solution.py
+++ b/solution.py
@@ -35,17 +35,17 @@
     return place
 
 
-def send_rows(route_ref, shape, axis, block_rows, devs):
+def send_rows(route_ref, shape, axis, block_rows, devs, flip=0):
     place = lax.broadcasted_iota(jnp.int32, shape, axis)
     target = jnp.zeros(shape, jnp.int32)
     for block in range(shape[axis] // block_rows):
         first = block * block_rows
-        moved = turned(route_ref[0, block], devs) * block_rows + place - first
+        moved = (turned(route_ref[0, block], devs) ^ flip) * block_rows + place - first
         target = jnp.where(place >= first, moved, target)
     return target
 
 
-def scatter_kernel(block_rows, route_hbm, points_hbm, cot_hbm, out_ref, route_ref, points_ref, cot_ref, sems):
+def scatter_kernel(block_rows, flip, route_hbm, points_hbm, cot_hbm, out_ref, route_ref, points_ref, cot_ref, sems):
     copies = [
         pltpu.make_async_copy(source, target, sems.at[at])
         for at, (source, target) in enumerate(
@@ -56,7 +56,8 @@
         copy.start()
     copies[0].wait()
     rows, width = points_ref.shape
-    target = send_rows(route_ref, (1, rows), 1, block_rows, out_ref.shape[0] // block_rows)
+    devs = out_ref.shape[0] // block_rows
+    target = send_rows(route_ref, (1, rows), 1, block_rows, devs, flip)
     index = lax.broadcasted_iota(jnp.int32, (out_ref.shape[0], rows), 0)
     pick = jnp.where(index == target, 1.0, 0.0).astype(BF16)
     for copy in copies[1:]:
@@ -182,7 +183,7 @@
         half_ref[width:] = sums.astype(half_ref.dtype)
 
 
-def rows_kernel(got_ref, attn_ref, d_normed_ref, vectors_ref, w_out_ref, back_ref, token_ref):
+def rows_kernel(blocks, got_ref, attn_ref, d_normed_ref, vectors_ref, w_out_ref, back_ref, token_ref):
     token_ref[...] = jnp.zeros_like(token_ref)
     width = attn_ref.shape[1]
     gain = vectors_ref[:, :width]
@@ -197,8 +198,11 @@
         - jnp.mean(d_xhat, axis=-1, keepdims=True)
         - xhat * jnp.mean(d_xhat * xhat, axis=-1, keepdims=True)
     )
-    back_ref[:, :width] = mixed.astype(BF16)
-    back_ref[:, width:] = (cot + rstd * inner).astype(BF16)
+    both = jnp.concatenate([mixed.astype(BF16), (cot + rstd * inner).astype(BF16)], axis=1)
+    rows = both.shape[0] // blocks
+    for block in range(blocks):
+        end = (blocks - block) * rows
+        back_ref[end - rows : end] = both[block * rows : (block + 1) * rows]
 
 
 def sum_kernel(count, *refs):
@@ -254,9 +258,9 @@
     w_out_ref[...] = both_ref[width:, width:]
 
 
-def exchange(message):
+def exchange(message, flip=0):
     devs = message.shape[0]
-    order = [turned(place, devs) for place in range(devs)]
+    order = [turned(place ^ flip, devs) for place in range(devs)]
     return lax.all_to_all(
         message, "seq", split_axis=0, concat_axis=0, axis_index_groups=[order], tiled=True
     )
@@ -273,12 +277,13 @@
     held = devs * block_rows
     share = width // devs
     near = 4 if devs == 16 and width % 64 == 0 else 1
+    flip = devs - 1 if near > 1 else 0
 
     def shape(*dims, dtype=BF16):
         return jax.ShapeDtypeStruct(dims, dtype)
 
     sent = pl.pallas_call(
-        functools.partial(scatter_kernel, block_rows),
+        functools.partial(scatter_kernel, block_rows, flip),
         out_shape=shape(held, 2 * width),
         in_specs=[ANY] * 3,
         out_specs=VMEM,
@@ -289,7 +294,7 @@
             pltpu.SemaphoreType.DMA((3,)),
         ],
     )(route, points, cotangent)
-    got = exchange(sent.reshape(devs, block_rows, 2 * width)).reshape(held, 2 * width)
+    got = exchange(sent.reshape(devs, block_rows, 2 * width), flip).reshape(held, 2 * width)
 
     pick, early = pl.pallas_call(
         functools.partial(pick_kernel, block_rows),
@@ -322,7 +327,7 @@
         compiler_params=LARGE,
     )(got, vectors, w_qkv, w_out, early)
     back, token = pl.pallas_call(
-        rows_kernel,
+        functools.partial(rows_kernel, devs if flip else 1),
         out_shape=(shape(held, 2 * width), shape(8, 128, dtype=F32)),
         in_specs=[VMEM] * 5,
         out_specs=(VMEM,) * 2,

time: 47.3 us -> 46.3 us (0.979)
  waiting for transfers between devices: 16.7 us -> 13 us
  starting transfers between devices: 15.9 us -> 18.7 us
    all_to_all x2, waiting for transfers between devices: 9.48 us -> 5.8 us  [exchange(): lax.all_to_all(message, 'seq', split_axis=0, concat_axis=0, axis_index_gr...]
    all_to_all x2, starting transfers between devices: 11.6 us -> 13.1 us  [exchange(): lax.all_to_all(message, 'seq', split_axis=0, concat_axis=0, axis_index_gr...]
    ppermute x6, starting transfers between devices: 4.34 us -> 5.61 us  [swap(): lax.ppermute(piece, 'seq', [(dev, dev ^ step) for dev in range(devs)])]
  transfers between devices with their start and end apart: 8 -> 8, of which waited for: 6 -> 5; matrix products, arithmetic and copies ran while one was open for 0% -> 0% of each run, Pallas kernels for 6% -> 6%
where the time goes in v8:
time: 46.3 us; the launch traced here: 45.9 us
  starting transfers between devices  18.7 us (40%)
  Pallas kernels  13.3 us (29%)
  waiting for transfers between devices  13 us (28%)
  between operations  0.79 us (2%)
    all_to_all x2, starting transfers between devices, exchange(): lax.all_to_all(message, 'seq', split_axis=0, concat_axis=0, axis_index_gr...  13.1 us
    pallas_call x1, Pallas kernels, local(): pl.pallas_call(functools.partial(owner_kernel, near), out_shape=(shape(he...  8.03 us
    ppermute x6, waiting for transfers between devices, swap(): lax.ppermute(piece, 'seq', [(dev, dev ^ step) for dev in range(devs)])  7.19 us
    all_to_all x2, waiting for transfers between devices, exchange(): lax.all_to_all(message, 'seq', split_axis=0, concat_axis=0, axis_index_gr...  5.8 us
    ppermute x6, starting transfers between devices, swap(): lax.ppermute(piece, 'seq', [(dev, dev ^ step) for dev in range(devs)])  5.61 us
    pallas_call x1, Pallas kernels, local(): pl.pallas_call(functools.partial(scatter_kernel, block_rows, flip), out_s...  1.89 us
    pallas_call x1, Pallas kernels, local(): pl.pallas_call(functools.partial(rows_kernel, devs if flip else 1), out_s...  1.08 us
  transfers between devices with their start and end apart: 8, of which 5 were waited for; matrix products, arithmetic and copies ran while one was open for 0% of the time, Pallas kernels for 6%

profile of v8, /device:TPU:0, one launch (start us, length us, event | category | flops | bytes accessed | tf_op | source)
XLA Modules:
  0.0 45.9 jit_solution(15103782062604083179)
XLA Ops:
  0.6 1.9 %shard_map.136 = bf16[512,256]{1,0:T(8,128)(2,1)} custom-call(s32[2,8]{1,0:T(2,128)} %route_hbm.3, bf16[256,128]{1,0:T(8,128)(2,1)} %points_hbm.1, bf16[256,128]{1,0:T(8,128)(2,1)} %cot_hbm.1), custom_call_target="tpu_custom_call" | custom-call | tf_op jit(solution)/shard_map/pallas_call | solution.py:285
  2.5 0.0 copy-start.2
  2.5 0.0 copy-start.3
  2.6 0.0 copy-start
  2.6 0.0 copy-start.1
  2.6 9.0 %all-to-all-start = ((bf16[16,32,256]{2,1,0:T(8,128)(2,1)}), bf16[16,32,256]{2,1,0:T(8,128)(2,1)S(1)}, u32[]{:S(2)}, u32[]{:S(2)}) async-start(bf16[16,32,256]{2,1,0:T(8,128)(2,1)} %bitcast.7), calls=%async_computation | async-start | bytes 524288 | tf_op jit(solution)/shard_map/all_to_all | solution.py:264
  11.6 0.0 copy-done.2
  11.6 0.0 copy-start.4
  11.6 0.0 copy-start.5
  11.6 0.6 %shard_map.135 = (bf16[256,512]{1,0:T(8,128)(2,1)S(1)}, f32[8,128]{1,0:T(8,128)S(1)}) custom-call(s32[2,8]{1,0:T(2,128)S(1)} %copy-done.2), custom_call_target="tpu_custom_call" | custom-call | tf_op jit(solution)/shard_map/pallas_call | solution.py:299
  12.2 0.0 copy-done.3
  12.2 0.0 copy-done.4
  12.2 0.0 copy-done.5
  12.3 5.8 %all-to-all-done = bf16[16,32,256]{2,1,0:T(8,128)(2,1)S(1)} async-done(((bf16[16,32,256]{2,1,0:T(8,128)(2,1)}), bf16[16,32,256]{2,1,0:T(8,128)(2,1)S(1)}, u32[]{:S(2)}, u32[]{:S(2)}) %all-to-all-start) | async-done | bytes 262176 | tf_op jit(solution)/shard_map/all_to_all | solution.py:264
  18.1 0.0 copy-done
  18.1 0.0 copy-done.1
  18.1 8.0 %shard_map.137 = (bf16[512,128]{1,0:T(8,128)(2,1)S(1)}, f32[512,128]{1,0:T(8,128)S(1)}, bf16[136,256]{1,0:T(8,128)(2,1)S(1)}, bf16[136,256]{1,0:T(8,128)(2,1)S(1)}) custom-call(bf16[512,256]{1,0:T(8,128)(2,1)S(1)} %bitcast.5, f32[1,640]{1,0:T(1,128)S(1)} %broadcast_in_dim.3.vectors_ref, bf16[128,384]{1,0:T(8,128)(2,1)S(1)} %copy-done, ...), custom_call_target="tpu_custom_call" | custom-call | tf_op jit(solution)/shard_map/pallas_call | solution.py:314
  26.1 0.5 %collective-permute-start = (bf16[136,256]{1,0:T(8,128)(2,1)S(1)}, bf16[136,256]{1,0:T(8,128)(2,1)S(1)}, u32[]{:S(2)}, u32[]{:S(2)}) collective-permute-start(bf16[136,256]{1,0:T(8,128)(2,1)S(1)} %get-tuple-element.29), channel_id=1, source_target_pairs={{0,1},{1,0},{2,3},{3,2},{4,5},{5,4},{6,7},{7,6},{8,9},{9,8},{10,11... | collective-permute-start | bytes 208904 | tf_op jit(solution)/shard_map/ppermute | solution.py:270
  26.6 1.1 %shard_map.138 = (bf16[512,256]{1,0:T(8,128)(2,1)}, f32[8,128]{1,0:T(8,128)S(1)}) custom-call(bf16[512,256]{1,0:T(8,128)(2,1)S(1)} %bitcast.6, bf16[512,128]{1,0:T(8,128)(2,1)S(1)} %get-tuple-element.25.attn_ref, f32[512,128]{1,0:T(8,128)S(1)} %get-tuple-element.26.d_normed_ref, f32[1,640]{1,0:T(1,128)S(1)} %broadcast_in_dim.3.vectors_ref, ...), custom_call_target="tpu_custom_call" | custom-call | flops 536870912 | bytes 1048576 | tf_op jit(solution)/shard_map/pallas_call | solution.py:329
  27.7 0.0 collective-permute-done.refs_1_
  27.7 1.5 %collective-permute-start.1 = (bf16[136,256]{1,0:T(8,128)(2,1)S(1)}, bf16[136,256]{1,0:T(8,128)(2,1)S(1)}, u32[]{:S(2)}, u32[]{:S(2)}) collective-permute-start(bf16[136,256]{1,0:T(8,128)(2,1)S(1)} %shard_map.139.other_ref.refs_0_), channel_id=1, source_target_pairs={{0,8},{1,9},{2,10},{3,11},{4,12},{5,13},{6,14},{7,15},{8,0},{9,1},... | collective-permute-start | bytes 208904 | tf_op jit(solution)/shard_map/ppermute | solution.py:270
  29.2 4.1 %all-to-all-start.1 = ((bf16[16,32,256]{2,1,0:T(8,128)(2,1)}), bf16[16,32,256]{2,1,0:T(8,128)(2,1)S(1)}, u32[]{:S(2)}, u32[]{:S(2)}) async-start(bf16[16,32,256]{2,1,0:T(8,128)(2,1)} %bitcast.2), calls=%async_computation.1 | async-start | bytes 524288 | tf_op jit(solution)/shard_map/all_to_all | solution.py:264
  33.4 1.1 %collective-permute-done.1.refs_1_ = bf16[136,256]{1,0:T(8,128)(2,1)S(1)} collective-permute-done((bf16[136,256]{1,0:T(8,128)(2,1)S(1)}, bf16[136,256]{1,0:T(8,128)(2,1)S(1)}, u32[]{:S(2)}, u32[]{:S(2)}) %collective-permute-start.1) | collective-permute-done | bytes 69664 | tf_op jit(solution)/shard_map/ppermute | solution.py:270
  34.4 1.8 %collective-permute-start.4 = (bf16[136,256]{1,0:T(8,128)(2,1)S(1)}, bf16[136,256]{1,0:T(8,128)(2,1)S(1)}, u32[]{:S(2)}, u32[]{:S(2)}) collective-permute-start(bf16[136,256]{1,0:T(8,128)(2,1)S(1)} %shard_map.142.refs_0_), channel_id=1, source_target_pairs={{0,6},{1,7},{2,4},{3,5},{4,2},{5,3},{6,0},{7,1},{8,14},{9,15},{10,... | collective-permute-start | bytes 208904 | tf_op jit(solution)/shard_map/ppermute | solution.py:270
  36.3 1.5 %collective-permute-start.3 = (bf16[136,256]{1,0:T(8,128)(2,1)S(1)}, bf16[136,256]{1,0:T(8,128)(2,1)S(1)}, u32[]{:S(2)}, u32[]{:S(2)}) collective-permute-start(bf16[136,256]{1,0:T(8,128)(2,1)S(1)} %shard_map.142.refs_0_), channel_id=1, source_target_pairs={{0,4},{1,5},{2,6},{3,7},{4,0},{5,1},{6,2},{7,3},{8,12},{9,13},{10,... | collective-permute-start | bytes 208904 | tf_op jit(solution)/shard_map/ppermute | solution.py:270
  37.8 0.2 collective-permute-start.2
  38.0 5.2 %collective-permute-done.4.refs_3_ = bf16[136,256]{1,0:T(8,128)(2,1)S(1)} collective-permute-done((bf16[136,256]{1,0:T(8,128)(2,1)S(1)}, bf16[136,256]{1,0:T(8,128)(2,1)S(1)}, u32[]{:S(2)}, u32[]{:S(2)}) %collective-permute-start.4) | collective-permute-done | bytes 69664 | tf_op jit(solution)/shard_map/ppermute | solution.py:270
  43.2 0.6 %collective-permute-done.3.refs_2_ = bf16[136,256]{1,0:T(8,128)(2,1)S(1)} collective-permute-done((bf16[136,256]{1,0:T(8,128)(2,1)S(1)}, bf16[136,256]{1,0:T(8,128)(2,1)S(1)}, u32[]{:S(2)}, u32[]{:S(2)}) %collective-permute-start.3) | collective-permute-done | bytes 69664 | tf_op jit(solution)/shard_map/ppermute | solution.py:270
  43.8 0.0 collective-permute-done.2.refs_1_
  43.8 0.1 collective-permute-start.5
  43.9 0.0 all-to-all-done.1
  43.9 0.9 %shard_map.141 = (bf16[256,128]{1,0:T(8,128)(2,1)}, bf16[256,128]{1,0:T(8,128)(2,1)}, f32[8,128]{1,0:T(8,128)S(1)}) custom-call(bf16[256,512]{1,0:T(8,128)(2,1)S(1)} %get-tuple-element.23.pick_ref, bf16[512,256]{1,0:T(8,128)(2,1)S(1)} %bitcast.4), custom_call_target="tpu_custom_call" | custom-call | tf_op jit(solution)/shard_map/pallas_call | solution.py:341
  44.8 0.3 collective-permute-done.5.refs_1_
  45.1 0.7 %shard_map.144 = (f32[128]{0:T(128)}, f32[128,384]{1,0:T(8,128)}, f32[384]{0:T(512)}, f32[128,128]{1,0:T(8,128)}, f32[128]{0:T(128)}) custom-call(bf16[136,256]{1,0:T(8,128)(2,1)S(1)} %shard_map.143.refs_0_, bf16[136,256]{1,0:T(8,128)(2,1)S(1)} %collective-permute-done.5.refs_1_, f32[8,128]{1,0:T(8,128)S(1)} %get-tuple-element.33.refs_2_), custom_call_target="tpu_custom_call" | custom-call | tf_op jit(solution)/shard_map/pallas_call | solution.py:377
  (6 shorter events, 0.1 us)
Async XLA Ops:
  2.5 9.0 %copy-start.2 = (s32[2,8]{1,0:T(2,128)S(1)}, s32[2,8]{1,0:T(2,128)}, u32[]{:S(2)}) copy-start(s32[2,8]{1,0:T(2,128)} %route_hbm.3) | copy-start | bytes 196
  2.5 9.7 %copy-start.3 = (f32[384]{0:T(512)S(1)}, f32[384]{0:T(512)}, u32[]{:S(2)}) copy-start(f32[384]{0:T(512)} %param.14) | copy-start | bytes 4612
  2.6 15.5 %copy-start = (bf16[128,384]{1,0:T(8,128)(2,1)S(1)}, bf16[128,384]{1,0:T(8,128)(2,1)}, u32[]{:S(2)}) copy-start(bf16[128,384]{1,0:T(8,128)(2,1)} %w_qkv_hbm.1) | copy-start | bytes 294916
  2.6 15.5 %copy-start.1 = (bf16[128,128]{1,0:T(8,128)(2,1)S(1)}, bf16[128,128]{1,0:T(8,128)(2,1)}, u32[]{:S(2)}) copy-start(bf16[128,128]{1,0:T(8,128)(2,1)} %w_out_ref.1) | copy-start | bytes 98308
  2.6 15.5 %all-to-all-start = ((bf16[16,32,256]{2,1,0:T(8,128)(2,1)}), bf16[16,32,256]{2,1,0:T(8,128)(2,1)S(1)}, u32[]{:S(2)}, u32[]{:S(2)}) async-start(bf16[16,32,256]{2,1,0:T(8,128)(2,1)} %bitcast.7), calls=%async_computation | async-start | bytes 524288 | tf_op jit(solution)/shard_map/all_to_all | solution.py:264
  11.6 0.7 %copy-start.4 = (f32[128]{0:T(128)S(1)}, f32[128]{0:T(128)}, u32[]{:S(2)}) copy-start(f32[128]{0:T(128)} %param.16) | copy-start | bytes 1540
  11.6 0.7 %copy-start.5 = (f32[128]{0:T(128)S(1)}, f32[128]{0:T(128)}, u32[]{:S(2)}) copy-start(f32[128]{0:T(128)} %param.12) | copy-start | bytes 1540
  26.1 1.6 %collective-permute-start = (bf16[136,256]{1,0:T(8,128)(2,1)S(1)}, bf16[136,256]{1,0:T(8,128)(2,1)S(1)}, u32[]{:S(2)}, u32[]{:S(2)}) collective-permute-start(bf16[136,256]{1,0:T(8,128)(2,1)S(1)} %get-tuple-element.29), channel_id=1, source_target_pairs={{0,1},{1,0},{2,3},{3,2},{4,5},{5,4},{6,7},{7,6},{8,9},{9,8},{10,11... | collective-permute-start | bytes 208904 | tf_op jit(solution)/shard_map/ppermute | solution.py:270
  27.7 6.7 %collective-permute-start.1 = (bf16[136,256]{1,0:T(8,128)(2,1)S(1)}, bf16[136,256]{1,0:T(8,128)(2,1)S(1)}, u32[]{:S(2)}, u32[]{:S(2)}) collective-permute-start(bf16[136,256]{1,0:T(8,128)(2,1)S(1)} %shard_map.139.other_ref.refs_0_), channel_id=1, source_target_pairs={{0,8},{1,9},{2,10},{3,11},{4,12},{5,13},{6,14},{7,15},{8,0},{9,1},... | collective-permute-start | bytes 208904 | tf_op jit(solution)/shard_map/ppermute | solution.py:270
  29.2 14.7 %all-to-all-start.1 = ((bf16[16,32,256]{2,1,0:T(8,128)(2,1)}), bf16[16,32,256]{2,1,0:T(8,128)(2,1)S(1)}, u32[]{:S(2)}, u32[]{:S(2)}) async-start(bf16[16,32,256]{2,1,0:T(8,128)(2,1)} %bitcast.2), calls=%async_computation.1 | async-start | bytes 524288 | tf_op jit(solution)/shard_map/all_to_all | solution.py:264
  34.4 8.7 %collective-permute-start.4 = (bf16[136,256]{1,0:T(8,128)(2,1)S(1)}, bf16[136,256]{1,0:T(8,128)(2,1)S(1)}, u32[]{:S(2)}, u32[]{:S(2)}) collective-permute-start(bf16[136,256]{1,0:T(8,128)(2,1)S(1)} %shard_map.142.refs_0_), channel_id=1, source_target_pairs={{0,6},{1,7},{2,4},{3,5},{4,2},{5,3},{6,0},{7,1},{8,14},{9,15},{10,... | collective-permute-start | bytes 208904 | tf_op jit(solution)/shard_map/ppermute | solution.py:270
  36.3 7.5 %collective-permute-start.3 = (bf16[136,256]{1,0:T(8,128)(2,1)S(1)}, bf16[136,256]{1,0:T(8,128)(2,1)S(1)}, u32[]{:S(2)}, u32[]{:S(2)}) collective-permute-start(bf16[136,256]{1,0:T(8,128)(2,1)S(1)} %shard_map.142.refs_0_), channel_id=1, source_target_pairs={{0,4},{1,5},{2,6},{3,7},{4,0},{5,1},{6,2},{7,3},{8,12},{9,13},{10,... | collective-permute-start | bytes 208904 | tf_op jit(solution)/shard_map/ppermute | solution.py:270
  37.8 5.9 %collective-permute-start.2 = (bf16[136,256]{1,0:T(8,128)(2,1)S(1)}, bf16[136,256]{1,0:T(8,128)(2,1)S(1)}, u32[]{:S(2)}, u32[]{:S(2)}) collective-permute-start(bf16[136,256]{1,0:T(8,128)(2,1)S(1)} %shard_map.142.refs_0_), channel_id=1, source_target_pairs={{0,2},{1,3},{2,0},{3,1},{4,6},{5,7},{6,4},{7,5},{8,10},{9,11},{10,... | collective-permute-start | bytes 208904 | tf_op jit(solution)/shard_map/ppermute | solution.py:270
  43.8 1.3 %collective-permute-start.5 = (bf16[136,256]{1,0:T(8,128)(2,1)S(1)}, bf16[136,256]{1,0:T(8,128)(2,1)S(1)}, u32[]{:S(2)}, u32[]{:S(2)}) collective-permute-start(bf16[136,256]{1,0:T(8,128)(2,1)S(1)} %shard_map.143.refs_0_), channel_id=1, source_target_pairs={{0,1},{1,0},{2,3},{3,2},{4,5},{5,4},{6,7},{7,6},{8,9},{9,8},{10,11... | collective-permute-start | bytes 208904 | tf_op jit(solution)/shard_map/ppermute | solution.py:270

commit v9 on v8

--- a/solution.py
+++ b/solution.py
@@ -70,8 +70,13 @@
 
 
 def normalize(points):
-    centered = points - jnp.mean(points, axis=-1, keepdims=True)
-    rstd = lax.rsqrt(jnp.mean(centered * centered, axis=-1, keepdims=True) + EPS)
+    width = points.shape[1]
+    mean_of = jnp.full((width, width), 1.0 / width, BF16)
+    centered = points - matmul(points.astype(BF16), mean_of)
+    squares = centered * centered
+    high = squares.astype(BF16)
+    low = (squares - high.astype(F32)).astype(BF16)
+    rstd = lax.rsqrt(matmul(high, mean_of) + matmul(low, mean_of) + EPS)
     return centered * rstd, rstd
 
 

time: 46.3 us -> 46.8 us (1.011)
  Pallas kernels: 13.3 us -> 13.8 us
where the time goes in v9:
time: 46.8 us; the launch traced here: 46.3 us
  starting transfers between devices  18.6 us (40%)
  Pallas kernels  13.8 us (29%)
  waiting for transfers between devices  13.1 us (28%)
  between operations  0.79 us (2%)
    all_to_all x2, starting transfers between devices, exchange(): lax.all_to_all(message, 'seq', split_axis=0, concat_axis=0, axis_index_gr...  13 us
    pallas_call x1, Pallas kernels, local(): pl.pallas_call(functools.partial(owner_kernel, near), out_shape=(shape(he...  8.4 us
    ppermute x6, waiting for transfers between devices, swap(): lax.ppermute(piece, 'seq', [(dev, dev ^ step) for dev in range(devs)])  7.26 us
    all_to_all x2, waiting for transfers between devices, exchange(): lax.all_to_all(message, 'seq', split_axis=0, concat_axis=0, axis_index_gr...  5.8 us
    ppermute x6, starting transfers between devices, swap(): lax.ppermute(piece, 'seq', [(dev, dev ^ step) for dev in range(devs)])  5.61 us
    pallas_call x1, Pallas kernels, local(): pl.pallas_call(functools.partial(scatter_kernel, block_rows, flip), out_s...  1.89 us
    pallas_call x1, Pallas kernels, local(): pl.pallas_call(functools.partial(rows_kernel, devs if flip else 1), out_s...  1.21 us
  transfers between devices with their start and end apart: 8, of which 5 were waited for; matrix products, arithmetic and copies ran while one was open for 0% of the time, Pallas kernels for 6%

profile of v9, /device:TPU:0, one launch (start us, length us, event | category | flops | bytes accessed | tf_op | source)
XLA Modules:
  0.0 46.3 jit_solution(2549811948631231738)
XLA Ops:
  0.6 1.9 %shard_map.136 = bf16[512,256]{1,0:T(8,128)(2,1)} custom-call(s32[2,8]{1,0:T(2,128)} %route_hbm.3, bf16[256,128]{1,0:T(8,128)(2,1)} %points_hbm.1, bf16[256,128]{1,0:T(8,128)(2,1)} %cot_hbm.1), custom_call_target="tpu_custom_call" | custom-call | tf_op jit(solution)/shard_map/pallas_call | solution.py:290
  2.5 0.0 copy-start.2
  2.5 0.0 copy-start.3
  2.6 0.0 copy-start
  2.6 0.0 copy-start.1
  2.6 9.0 %all-to-all-start = ((bf16[16,32,256]{2,1,0:T(8,128)(2,1)}), bf16[16,32,256]{2,1,0:T(8,128)(2,1)S(1)}, u32[]{:S(2)}, u32[]{:S(2)}) async-start(bf16[16,32,256]{2,1,0:T(8,128)(2,1)} %bitcast.7), calls=%async_computation | async-start | bytes 524288 | tf_op jit(solution)/shard_map/all_to_all | solution.py:269
  11.6 0.0 copy-done.2
  11.6 0.0 copy-start.4
  11.6 0.0 copy-start.5
  11.6 0.6 %shard_map.135 = (bf16[256,512]{1,0:T(8,128)(2,1)S(1)}, f32[8,128]{1,0:T(8,128)S(1)}) custom-call(s32[2,8]{1,0:T(2,128)S(1)} %copy-done.2), custom_call_target="tpu_custom_call" | custom-call | tf_op jit(solution)/shard_map/pallas_call | solution.py:304
  12.2 0.0 copy-done.3
  12.2 0.0 copy-done.4
  12.2 0.0 copy-done.5
  12.3 5.8 %all-to-all-done = bf16[16,32,256]{2,1,0:T(8,128)(2,1)S(1)} async-done(((bf16[16,32,256]{2,1,0:T(8,128)(2,1)}), bf16[16,32,256]{2,1,0:T(8,128)(2,1)S(1)}, u32[]{:S(2)}, u32[]{:S(2)}) %all-to-all-start) | async-done | bytes 262176 | tf_op jit(solution)/shard_map/all_to_all | solution.py:269
  18.1 0.0 copy-done
  18.1 0.0 copy-done.1
  18.1 8.4 %shard_map.137 = (bf16[512,128]{1,0:T(8,128)(2,1)S(1)}, f32[512,128]{1,0:T(8,128)S(1)}, bf16[136,256]{1,0:T(8,128)(2,1)S(1)}, bf16[136,256]{1,0:T(8,128)(2,1)S(1)}) custom-call(bf16[512,256]{1,0:T(8,128)(2,1)S(1)} %bitcast.5, f32[1,640]{1,0:T(1,128)S(1)} %broadcast_in_dim.3.vectors_ref, bf16[128,384]{1,0:T(8,128)(2,1)S(1)} %copy-done, ...), custom_call_target="tpu_custom_call" | custom-call | tf_op jit(solution)/shard_map/pallas_call | solution.py:319
  26.5 0.5 %collective-permute-start = (bf16[136,256]{1,0:T(8,128)(2,1)S(1)}, bf16[136,256]{1,0:T(8,128)(2,1)S(1)}, u32[]{:S(2)}, u32[]{:S(2)}) collective-permute-start(bf16[136,256]{1,0:T(8,128)(2,1)S(1)} %get-tuple-element.29), channel_id=1, source_target_pairs={{0,1},{1,0},{2,3},{3,2},{4,5},{5,4},{6,7},{7,6},{8,9},{9,8},{10,11... | collective-permute-start | bytes 208904 | tf_op jit(solution)/shard_map/ppermute | solution.py:275
  27.0 1.2 %shard_map.138 = (bf16[512,256]{1,0:T(8,128)(2,1)}, f32[8,128]{1,0:T(8,128)S(1)}) custom-call(bf16[512,256]{1,0:T(8,128)(2,1)S(1)} %bitcast.6, bf16[512,128]{1,0:T(8,128)(2,1)S(1)} %get-tuple-element.25.attn_ref, f32[512,128]{1,0:T(8,128)S(1)} %get-tuple-element.26.d_normed_ref, f32[1,640]{1,0:T(1,128)S(1)} %broadcast_in_dim.3.vectors_ref, ...), custom_call_target="tpu_custom_call" | custom-call | flops 536870912 | bytes 1048576 | tf_op jit(solution)/shard_map/pallas_call | solution.py:334
  28.2 0.0 collective-permute-done.refs_1_
  28.2 1.5 %collective-permute-start.1 = (bf16[136,256]{1,0:T(8,128)(2,1)S(1)}, bf16[136,256]{1,0:T(8,128)(2,1)S(1)}, u32[]{:S(2)}, u32[]{:S(2)}) collective-permute-start(bf16[136,256]{1,0:T(8,128)(2,1)S(1)} %shard_map.139.other_ref.refs_0_), channel_id=1, source_target_pairs={{0,8},{1,9},{2,10},{3,11},{4,12},{5,13},{6,14},{7,15},{8,0},{9,1},... | collective-permute-start | bytes 208904 | tf_op jit(solution)/shard_map/ppermute | solution.py:275
  29.7 4.0 %all-to-all-start.1 = ((bf16[16,32,256]{2,1,0:T(8,128)(2,1)}), bf16[16,32,256]{2,1,0:T(8,128)(2,1)S(1)}, u32[]{:S(2)}, u32[]{:S(2)}) async-start(bf16[16,32,256]{2,1,0:T(8,128)(2,1)} %bitcast.2), calls=%async_computation.1 | async-start | bytes 524288 | tf_op jit(solution)/shard_map/all_to_all | solution.py:269
  33.7 1.1 %collective-permute-done.1.refs_1_ = bf16[136,256]{1,0:T(8,128)(2,1)S(1)} collective-permute-done((bf16[136,256]{1,0:T(8,128)(2,1)S(1)}, bf16[136,256]{1,0:T(8,128)(2,1)S(1)}, u32[]{:S(2)}, u32[]{:S(2)}) %collective-permute-start.1) | collective-permute-done | bytes 69664 | tf_op jit(solution)/shard_map/ppermute | solution.py:275
  34.9 1.8 %collective-permute-start.4 = (bf16[136,256]{1,0:T(8,128)(2,1)S(1)}, bf16[136,256]{1,0:T(8,128)(2,1)S(1)}, u32[]{:S(2)}, u32[]{:S(2)}) collective-permute-start(bf16[136,256]{1,0:T(8,128)(2,1)S(1)} %shard_map.142.refs_0_), channel_id=1, source_target_pairs={{0,6},{1,7},{2,4},{3,5},{4,2},{5,3},{6,0},{7,1},{8,14},{9,15},{10,... | collective-permute-start | bytes 208904 | tf_op jit(solution)/shard_map/ppermute | solution.py:275
  36.7 1.7 %collective-permute-start.3 = (bf16[136,256]{1,0:T(8,128)(2,1)S(1)}, bf16[136,256]{1,0:T(8,128)(2,1)S(1)}, u32[]{:S(2)}, u32[]{:S(2)}) collective-permute-start(bf16[136,256]{1,0:T(8,128)(2,1)S(1)} %shard_map.142.refs_0_), channel_id=1, source_target_pairs={{0,4},{1,5},{2,6},{3,7},{4,0},{5,1},{6,2},{7,3},{8,12},{9,13},{10,... | collective-permute-start | bytes 208904 | tf_op jit(solution)/shard_map/ppermute | solution.py:275
  38.3 0.1 collective-permute-start.2
  38.5 5.1 %collective-permute-done.4.refs_3_ = bf16[136,256]{1,0:T(8,128)(2,1)S(1)} collective-permute-done((bf16[136,256]{1,0:T(8,128)(2,1)S(1)}, bf16[136,256]{1,0:T(8,128)(2,1)S(1)}, u32[]{:S(2)}, u32[]{:S(2)}) %collective-permute-start.4) | collective-permute-done | bytes 69664 | tf_op jit(solution)/shard_map/ppermute | solution.py:275
  43.6 0.7 %collective-permute-done.3.refs_2_ = bf16[136,256]{1,0:T(8,128)(2,1)S(1)} collective-permute-done((bf16[136,256]{1,0:T(8,128)(2,1)S(1)}, bf16[136,256]{1,0:T(8,128)(2,1)S(1)}, u32[]{:S(2)}, u32[]{:S(2)}) %collective-permute-start.3) | collective-permute-done | bytes 69664 | tf_op jit(solution)/shard_map/ppermute | solution.py:275
  44.2 0.0 collective-permute-done.2.refs_1_
  44.3 0.1 collective-permute-start.5
  44.3 0.0 all-to-all-done.1
  44.3 0.9 %shard_map.141 = (bf16[256,128]{1,0:T(8,128)(2,1)}, bf16[256,128]{1,0:T(8,128)(2,1)}, f32[8,128]{1,0:T(8,128)S(1)}) custom-call(bf16[256,512]{1,0:T(8,128)(2,1)S(1)} %get-tuple-element.23.pick_ref, bf16[512,256]{1,0:T(8,128)(2,1)S(1)} %bitcast.4), custom_call_target="tpu_custom_call" | custom-call | tf_op jit(solution)/shard_map/pallas_call | solution.py:346
  45.2 0.3 collective-permute-done.5.refs_1_
  45.6 0.7 %shard_map.144 = (f32[128]{0:T(128)}, f32[128,384]{1,0:T(8,128)}, f32[384]{0:T(512)}, f32[128,128]{1,0:T(8,128)}, f32[128]{0:T(128)}) custom-call(bf16[136,256]{1,0:T(8,128)(2,1)S(1)} %shard_map.143.refs_0_, bf16[136,256]{1,0:T(8,128)(2,1)S(1)} %collective-permute-done.5.refs_1_, f32[8,128]{1,0:T(8,128)S(1)} %get-tuple-element.33.refs_2_), custom_call_target="tpu_custom_call" | custom-call | tf_op jit(solution)/shard_map/pallas_call | solution.py:382
  (6 shorter events, 0.1 us)
Async XLA Ops:
  2.5 9.0 %copy-start.2 = (s32[2,8]{1,0:T(2,128)S(1)}, s32[2,8]{1,0:T(2,128)}, u32[]{:S(2)}) copy-start(s32[2,8]{1,0:T(2,128)} %route_hbm.3) | copy-start | bytes 196
  2.5 9.7 %copy-start.3 = (f32[384]{0:T(512)S(1)}, f32[384]{0:T(512)}, u32[]{:S(2)}) copy-start(f32[384]{0:T(512)} %param.14) | copy-start | bytes 4612
  2.6 15.5 %copy-start = (bf16[128,384]{1,0:T(8,128)(2,1)S(1)}, bf16[128,384]{1,0:T(8,128)(2,1)}, u32[]{:S(2)}) copy-start(bf16[128,384]{1,0:T(8,128)(2,1)} %w_qkv_hbm.1) | copy-start | bytes 294916
  2.6 15.5 %copy-start.1 = (bf16[128,128]{1,0:T(8,128)(2,1)S(1)}, bf16[128,128]{1,0:T(8,128)(2,1)}, u32[]{:S(2)}) copy-start(bf16[128,128]{1,0:T(8,128)(2,1)} %w_out_ref.1) | copy-start | bytes 98308
  2.6 15.5 %all-to-all-start = ((bf16[16,32,256]{2,1,0:T(8,128)(2,1)}), bf16[16,32,256]{2,1,0:T(8,128)(2,1)S(1)}, u32[]{:S(2)}, u32[]{:S(2)}) async-start(bf16[16,32,256]{2,1,0:T(8,128)(2,1)} %bitcast.7), calls=%async_computation | async-start | bytes 524288 | tf_op jit(solution)/shard_map/all_to_all | solution.py:269
  11.6 0.7 %copy-start.4 = (f32[128]{0:T(128)S(1)}, f32[128]{0:T(128)}, u32[]{:S(2)}) copy-start(f32[128]{0:T(128)} %param.16) | copy-start | bytes 1540
  11.6 0.7 %copy-start.5 = (f32[128]{0:T(128)S(1)}, f32[128]{0:T(128)}, u32[]{:S(2)}) copy-start(f32[128]{0:T(128)} %param.12) | copy-start | bytes 1540
  26.5 1.7 %collective-permute-start = (bf16[136,256]{1,0:T(8,128)(2,1)S(1)}, bf16[136,256]{1,0:T(8,128)(2,1)S(1)}, u32[]{:S(2)}, u32[]{:S(2)}) collective-permute-start(bf16[136,256]{1,0:T(8,128)(2,1)S(1)} %get-tuple-element.29), channel_id=1, source_target_pairs={{0,1},{1,0},{2,3},{3,2},{4,5},{5,4},{6,7},{7,6},{8,9},{9,8},{10,11... | collective-permute-start | bytes 208904 | tf_op jit(solution)/shard_map/ppermute | solution.py:275
  28.2 6.7 %collective-permute-start.1 = (bf16[136,256]{1,0:T(8,128)(2,1)S(1)}, bf16[136,256]{1,0:T(8,128)(2,1)S(1)}, u32[]{:S(2)}, u32[]{:S(2)}) collective-permute-start(bf16[136,256]{1,0:T(8,128)(2,1)S(1)} %shard_map.139.other_ref.refs_0_), channel_id=1, source_target_pairs={{0,8},{1,9},{2,10},{3,11},{4,12},{5,13},{6,14},{7,15},{8,0},{9,1},... | collective-permute-start | bytes 208904 | tf_op jit(solution)/shard_map/ppermute | solution.py:275
  29.7 14.6 %all-to-all-start.1 = ((bf16[16,32,256]{2,1,0:T(8,128)(2,1)}), bf16[16,32,256]{2,1,0:T(8,128)(2,1)S(1)}, u32[]{:S(2)}, u32[]{:S(2)}) async-start(bf16[16,32,256]{2,1,0:T(8,128)(2,1)} %bitcast.2), calls=%async_computation.1 | async-start | bytes 524288 | tf_op jit(solution)/shard_map/all_to_all | solution.py:269
  34.9 8.7 %collective-permute-start.4 = (bf16[136,256]{1,0:T(8,128)(2,1)S(1)}, bf16[136,256]{1,0:T(8,128)(2,1)S(1)}, u32[]{:S(2)}, u32[]{:S(2)}) collective-permute-start(bf16[136,256]{1,0:T(8,128)(2,1)S(1)} %shard_map.142.refs_0_), channel_id=1, source_target_pairs={{0,6},{1,7},{2,4},{3,5},{4,2},{5,3},{6,0},{7,1},{8,14},{9,15},{10,... | collective-permute-start | bytes 208904 | tf_op jit(solution)/shard_map/ppermute | solution.py:275
  36.7 7.6 %collective-permute-start.3 = (bf16[136,256]{1,0:T(8,128)(2,1)S(1)}, bf16[136,256]{1,0:T(8,128)(2,1)S(1)}, u32[]{:S(2)}, u32[]{:S(2)}) collective-permute-start(bf16[136,256]{1,0:T(8,128)(2,1)S(1)} %shard_map.142.refs_0_), channel_id=1, source_target_pairs={{0,4},{1,5},{2,6},{3,7},{4,0},{5,1},{6,2},{7,3},{8,12},{9,13},{10,... | collective-permute-start | bytes 208904 | tf_op jit(solution)/shard_map/ppermute | solution.py:275
  38.3 5.9 %collective-permute-start.2 = (bf16[136,256]{1,0:T(8,128)(2,1)S(1)}, bf16[136,256]{1,0:T(8,128)(2,1)S(1)}, u32[]{:S(2)}, u32[]{:S(2)}) collective-permute-start(bf16[136,256]{1,0:T(8,128)(2,1)S(1)} %shard_map.142.refs_0_), channel_id=1, source_target_pairs={{0,2},{1,3},{2,0},{3,1},{4,6},{5,7},{6,4},{7,5},{8,10},{9,11},{10,... | collective-permute-start | bytes 208904 | tf_op jit(solution)/shard_map/ppermute | solution.py:275
  44.3 1.3 %collective-permute-start.5 = (bf16[136,256]{1,0:T(8,128)(2,1)S(1)}, bf16[136,256]{1,0:T(8,128)(2,1)S(1)}, u32[]{:S(2)}, u32[]{:S(2)}) collective-permute-start(bf16[136,256]{1,0:T(8,128)(2,1)S(1)} %shard_map.143.refs_0_), channel_id=1, source_target_pairs={{0,1},{1,0},{2,3},{3,2},{4,5},{5,4},{6,7},{7,6},{8,9},{9,8},{10,11... | collective-permute-start | bytes 208904 | tf_op jit(solution)/shard_map/ppermute | solution.py:275

commit v10 on v8

--- a/solution.py
+++ b/solution.py
@@ -116,14 +116,12 @@
     def scores_of(h):
         return matmul(own(h, keys_s), query, ((1,), (1,))) + hidden
 
-    scores, probs, probs_b, d_probs, d_score = {}, {}, {}, {}, {}
+    scores, probs, probs_b, d_score = {}, {}, {}, {}
     attn_t, dq_t = [], []
     scores[0] = scores_of(0)
     for step in range(HEADS + 2):
         if step + 1 < HEADS:
             scores[step + 1] = scores_of(step + 1)
-        if step < HEADS:
-            d_probs[step] = matmul(own(step, values), d_attn_s, ((1,), (1,)))
         if 1 <= step <= HEADS:
             lanes = slice((step - 1) * head, step * head)
             attn_t.append(matmul(values_t[lanes, :], probs_b[step - 1]))
@@ -142,7 +140,8 @@
             h = step - 1
             inner = attn_t[h] * d_attn_t[h * head : (h + 1) * head, :].astype(F32)
             inner = jnp.sum(inner, axis=0, keepdims=True) * scale
-            d_score[h] = (probs.pop(h) * (d_probs.pop(h) - inner)).astype(BF16)
+            d_probs = matmul(own(h, values), d_attn_s, ((1,), (1,)))
+            d_score[h] = (probs.pop(h) * (d_probs - inner)).astype(BF16)
 
     attn_t = jnp.concatenate(attn_t, axis=0)
     attn_ref[...] = attn_t.T.astype(BF16)

time: 46.3 us -> 45.8 us (0.989)
  Pallas kernels: 13.3 us -> 12.8 us
    pallas_call x1, Pallas kernels: 8.03 us -> 7.5 us  [local(): pl.pallas_call(functools.partial(owner_kernel, near), out_shape=(shape(he...]
where the time goes in v10:
time: 45.8 us; the launch traced here: 45.3 us
  starting transfers between devices  18.7 us (41%)
  waiting for transfers between devices  13 us (28%)
  Pallas kernels  12.8 us (28%)
  between operations  0.79 us (2%)
    all_to_all x2, starting transfers between devices, exchange(): lax.all_to_all(message, 'seq', split_axis=0, concat_axis=0, axis_index_gr...  13.1 us
    pallas_call x1, Pallas kernels, local(): pl.pallas_call(functools.partial(owner_kernel, near), out_shape=(shape(he...  7.5 us
    ppermute x6, waiting for transfers between devices, swap(): lax.ppermute(piece, 'seq', [(dev, dev ^ step) for dev in range(devs)])  7.19 us
    all_to_all x2, waiting for transfers between devices, exchange(): lax.all_to_all(message, 'seq', split_axis=0, concat_axis=0, axis_index_gr...  5.8 us
    ppermute x6, starting transfers between devices, swap(): lax.ppermute(piece, 'seq', [(dev, dev ^ step) for dev in range(devs)])  5.61 us
    pallas_call x1, Pallas kernels, local(): pl.pallas_call(functools.partial(scatter_kernel, block_rows, flip), out_s...  1.89 us
    pallas_call x1, Pallas kernels, local(): pl.pallas_call(functools.partial(rows_kernel, devs if flip else 1), out_s...  1.08 us
  transfers between devices with their start and end apart: 8, of which 5 were waited for; matrix products, arithmetic and copies ran while one was open for 0% of the time, Pallas kernels for 6%

profile of v10, /device:TPU:0, one launch (start us, length us, event | category | flops | bytes accessed | tf_op | source)
XLA Modules:
  0.0 45.3 jit_solution(16456234803556238132)
XLA Ops:
  0.6 1.9 %shard_map.136 = bf16[512,256]{1,0:T(8,128)(2,1)} custom-call(s32[2,8]{1,0:T(2,128)} %route_hbm.3, bf16[256,128]{1,0:T(8,128)(2,1)} %points_hbm.1, bf16[256,128]{1,0:T(8,128)(2,1)} %cot_hbm.1), custom_call_target="tpu_custom_call" | custom-call | tf_op jit(solution)/shard_map/pallas_call | solution.py:284
  2.5 0.0 copy-start.2
  2.5 0.0 copy-start.3
  2.6 0.0 copy-start
  2.6 0.0 copy-start.1
  2.6 9.0 %all-to-all-start = ((bf16[16,32,256]{2,1,0:T(8,128)(2,1)}), bf16[16,32,256]{2,1,0:T(8,128)(2,1)S(1)}, u32[]{:S(2)}, u32[]{:S(2)}) async-start(bf16[16,32,256]{2,1,0:T(8,128)(2,1)} %bitcast.7), calls=%async_computation | async-start | bytes 524288 | tf_op jit(solution)/shard_map/all_to_all | solution.py:263
  11.6 0.0 copy-done.2
  11.6 0.0 copy-start.4
  11.6 0.0 copy-start.5
  11.6 0.6 %shard_map.135 = (bf16[256,512]{1,0:T(8,128)(2,1)S(1)}, f32[8,128]{1,0:T(8,128)S(1)}) custom-call(s32[2,8]{1,0:T(2,128)S(1)} %copy-done.2), custom_call_target="tpu_custom_call" | custom-call | tf_op jit(solution)/shard_map/pallas_call | solution.py:298
  12.2 0.0 copy-done.3
  12.2 0.0 copy-done.4
  12.2 0.0 copy-done.5
  12.3 5.8 %all-to-all-done = bf16[16,32,256]{2,1,0:T(8,128)(2,1)S(1)} async-done(((bf16[16,32,256]{2,1,0:T(8,128)(2,1)}), bf16[16,32,256]{2,1,0:T(8,128)(2,1)S(1)}, u32[]{:S(2)}, u32[]{:S(2)}) %all-to-all-start) | async-done | bytes 262176 | tf_op jit(solution)/shard_map/all_to_all | solution.py:263
  18.1 0.0 copy-done
  18.1 0.0 copy-done.1
  18.1 7.5 %shard_map.137 = (bf16[512,128]{1,0:T(8,128)(2,1)S(1)}, f32[512,128]{1,0:T(8,128)S(1)}, bf16[136,256]{1,0:T(8,128)(2,1)S(1)}, bf16[136,256]{1,0:T(8,128)(2,1)S(1)}) custom-call(bf16[512,256]{1,0:T(8,128)(2,1)S(1)} %bitcast.5, f32[1,640]{1,0:T(1,128)S(1)} %broadcast_in_dim.3.vectors_ref, bf16[128,384]{1,0:T(8,128)(2,1)S(1)} %copy-done, ...), custom_call_target="tpu_custom_call" | custom-call | tf_op jit(solution)/shard_map/pallas_call | solution.py:313
  25.6 0.5 %collective-permute-start = (bf16[136,256]{1,0:T(8,128)(2,1)S(1)}, bf16[136,256]{1,0:T(8,128)(2,1)S(1)}, u32[]{:S(2)}, u32[]{:S(2)}) collective-permute-start(bf16[136,256]{1,0:T(8,128)(2,1)S(1)} %get-tuple-element.29), channel_id=1, source_target_pairs={{0,1},{1,0},{2,3},{3,2},{4,5},{5,4},{6,7},{7,6},{8,9},{9,8},{10,11... | collective-permute-start | bytes 208904 | tf_op jit(solution)/shard_map/ppermute | solution.py:269
  26.1 1.1 %shard_map.138 = (bf16[512,256]{1,0:T(8,128)(2,1)}, f32[8,128]{1,0:T(8,128)S(1)}) custom-call(bf16[512,256]{1,0:T(8,128)(2,1)S(1)} %bitcast.6, bf16[512,128]{1,0:T(8,128)(2,1)S(1)} %get-tuple-element.25.attn_ref, f32[512,128]{1,0:T(8,128)S(1)} %get-tuple-element.26.d_normed_ref, f32[1,640]{1,0:T(1,128)S(1)} %broadcast_in_dim.3.vectors_ref, ...), custom_call_target="tpu_custom_call" | custom-call | flops 536870912 | bytes 1048576 | tf_op jit(solution)/shard_map/pallas_call | solution.py:328
  27.1 0.0 collective-permute-done.refs_1_
  27.2 1.5 %collective-permute-start.1 = (bf16[136,256]{1,0:T(8,128)(2,1)S(1)}, bf16[136,256]{1,0:T(8,128)(2,1)S(1)}, u32[]{:S(2)}, u32[]{:S(2)}) collective-permute-start(bf16[136,256]{1,0:T(8,128)(2,1)S(1)} %shard_map.139.other_ref.refs_0_), channel_id=1, source_target_pairs={{0,8},{1,9},{2,10},{3,11},{4,12},{5,13},{6,14},{7,15},{8,0},{9,1},... | collective-permute-start | bytes 208904 | tf_op jit(solution)/shard_map/ppermute | solution.py:269
  28.7 4.1 %all-to-all-start.1 = ((bf16[16,32,256]{2,1,0:T(8,128)(2,1)}), bf16[16,32,256]{2,1,0:T(8,128)(2,1)S(1)}, u32[]{:S(2)}, u32[]{:S(2)}) async-start(bf16[16,32,256]{2,1,0:T(8,128)(2,1)} %bitcast.2), calls=%async_computation.1 | async-start | bytes 524288 | tf_op jit(solution)/shard_map/all_to_all | solution.py:263
  32.8 1.1 %collective-permute-done.1.refs_1_ = bf16[136,256]{1,0:T(8,128)(2,1)S(1)} collective-permute-done((bf16[136,256]{1,0:T(8,128)(2,1)S(1)}, bf16[136,256]{1,0:T(8,128)(2,1)S(1)}, u32[]{:S(2)}, u32[]{:S(2)}) %collective-permute-start.1) | collective-permute-done | bytes 69664 | tf_op jit(solution)/shard_map/ppermute | solution.py:269
  33.9 1.8 %collective-permute-start.4 = (bf16[136,256]{1,0:T(8,128)(2,1)S(1)}, bf16[136,256]{1,0:T(8,128)(2,1)S(1)}, u32[]{:S(2)}, u32[]{:S(2)}) collective-permute-start(bf16[136,256]{1,0:T(8,128)(2,1)S(1)} %shard_map.142.refs_0_), channel_id=1, source_target_pairs={{0,6},{1,7},{2,4},{3,5},{4,2},{5,3},{6,0},{7,1},{8,14},{9,15},{10,... | collective-permute-start | bytes 208904 | tf_op jit(solution)/shard_map/ppermute | solution.py:269
  35.7 1.5 %collective-permute-start.3 = (bf16[136,256]{1,0:T(8,128)(2,1)S(1)}, bf16[136,256]{1,0:T(8,128)(2,1)S(1)}, u32[]{:S(2)}, u32[]{:S(2)}) collective-permute-start(bf16[136,256]{1,0:T(8,128)(2,1)S(1)} %shard_map.142.refs_0_), channel_id=1, source_target_pairs={{0,4},{1,5},{2,6},{3,7},{4,0},{5,1},{6,2},{7,3},{8,12},{9,13},{10,... | collective-permute-start | bytes 208904 | tf_op jit(solution)/shard_map/ppermute | solution.py:269
  37.3 0.2 collective-permute-start.2
  37.5 5.2 %collective-permute-done.4.refs_3_ = bf16[136,256]{1,0:T(8,128)(2,1)S(1)} collective-permute-done((bf16[136,256]{1,0:T(8,128)(2,1)S(1)}, bf16[136,256]{1,0:T(8,128)(2,1)S(1)}, u32[]{:S(2)}, u32[]{:S(2)}) %collective-permute-start.4) | collective-permute-done | bytes 69664 | tf_op jit(solution)/shard_map/ppermute | solution.py:269
  42.6 0.6 %collective-permute-done.3.refs_2_ = bf16[136,256]{1,0:T(8,128)(2,1)S(1)} collective-permute-done((bf16[136,256]{1,0:T(8,128)(2,1)S(1)}, bf16[136,256]{1,0:T(8,128)(2,1)S(1)}, u32[]{:S(2)}, u32[]{:S(2)}) %collective-permute-start.3) | collective-permute-done | bytes 69664 | tf_op jit(solution)/shard_map/ppermute | solution.py:269
  43.2 0.0 collective-permute-done.2.refs_1_
  43.3 0.1 collective-permute-start.5
  43.4 0.0 all-to-all-done.1
  43.4 0.9 %shard_map.141 = (bf16[256,128]{1,0:T(8,128)(2,1)}, bf16[256,128]{1,0:T(8,128)(2,1)}, f32[8,128]{1,0:T(8,128)S(1)}) custom-call(bf16[256,512]{1,0:T(8,128)(2,1)S(1)} %get-tuple-element.23.pick_ref, bf16[512,256]{1,0:T(8,128)(2,1)S(1)} %bitcast.4), custom_call_target="tpu_custom_call" | custom-call | tf_op jit(solution)/shard_map/pallas_call | solution.py:340
  44.3 0.3 collective-permute-done.5.refs_1_
  44.6 0.7 %shard_map.144 = (f32[128]{0:T(128)}, f32[128,384]{1,0:T(8,128)}, f32[384]{0:T(512)}, f32[128,128]{1,0:T(8,128)}, f32[128]{0:T(128)}) custom-call(bf16[136,256]{1,0:T(8,128)(2,1)S(1)} %shard_map.143.refs_0_, bf16[136,256]{1,0:T(8,128)(2,1)S(1)} %collective-permute-done.5.refs_1_, f32[8,128]{1,0:T(8,128)S(1)} %get-tuple-element.33.refs_2_), custom_call_target="tpu_custom_call" | custom-call | tf_op jit(solution)/shard_map/pallas_call | solution.py:376
  (6 shorter events, 0.1 us)
Async XLA Ops:
  2.5 9.0 %copy-start.2 = (s32[2,8]{1,0:T(2,128)S(1)}, s32[2,8]{1,0:T(2,128)}, u32[]{:S(2)}) copy-start(s32[2,8]{1,0:T(2,128)} %route_hbm.3) | copy-start | bytes 196
  2.5 9.7 %copy-start.3 = (f32[384]{0:T(512)S(1)}, f32[384]{0:T(512)}, u32[]{:S(2)}) copy-start(f32[384]{0:T(512)} %param.14) | copy-start | bytes 4612
  2.6 15.5 %copy-start = (bf16[128,384]{1,0:T(8,128)(2,1)S(1)}, bf16[128,384]{1,0:T(8,128)(2,1)}, u32[]{:S(2)}) copy-start(bf16[128,384]{1,0:T(8,128)(2,1)} %w_qkv_hbm.1) | copy-start | bytes 294916
  2.6 15.5 %copy-start.1 = (bf16[128,128]{1,0:T(8,128)(2,1)S(1)}, bf16[128,128]{1,0:T(8,128)(2,1)}, u32[]{:S(2)}) copy-start(bf16[128,128]{1,0:T(8,128)(2,1)} %w_out_ref.1) | copy-start | bytes 98308
  2.6 15.5 %all-to-all-start = ((bf16[16,32,256]{2,1,0:T(8,128)(2,1)}), bf16[16,32,256]{2,1,0:T(8,128)(2,1)S(1)}, u32[]{:S(2)}, u32[]{:S(2)}) async-start(bf16[16,32,256]{2,1,0:T(8,128)(2,1)} %bitcast.7), calls=%async_computation | async-start | bytes 524288 | tf_op jit(solution)/shard_map/all_to_all | solution.py:263
  11.6 0.7 %copy-start.4 = (f32[128]{0:T(128)S(1)}, f32[128]{0:T(128)}, u32[]{:S(2)}) copy-start(f32[128]{0:T(128)} %param.16) | copy-start | bytes 1540
  11.6 0.7 %copy-start.5 = (f32[128]{0:T(128)S(1)}, f32[128]{0:T(128)}, u32[]{:S(2)}) copy-start(f32[128]{0:T(128)} %param.12) | copy-start | bytes 1540
  25.6 1.5 %collective-permute-start = (bf16[136,256]{1,0:T(8,128)(2,1)S(1)}, bf16[136,256]{1,0:T(8,128)(2,1)S(1)}, u32[]{:S(2)}, u32[]{:S(2)}) collective-permute-start(bf16[136,256]{1,0:T(8,128)(2,1)S(1)} %get-tuple-element.29), channel_id=1, source_target_pairs={{0,1},{1,0},{2,3},{3,2},{4,5},{5,4},{6,7},{7,6},{8,9},{9,8},{10,11... | collective-permute-start | bytes 208904 | tf_op jit(solution)/shard_map/ppermute | solution.py:269
  27.2 6.7 %collective-permute-start.1 = (bf16[136,256]{1,0:T(8,128)(2,1)S(1)}, bf16[136,256]{1,0:T(8,128)(2,1)S(1)}, u32[]{:S(2)}, u32[]{:S(2)}) collective-permute-start(bf16[136,256]{1,0:T(8,128)(2,1)S(1)} %shard_map.139.other_ref.refs_0_), channel_id=1, source_target_pairs={{0,8},{1,9},{2,10},{3,11},{4,12},{5,13},{6,14},{7,15},{8,0},{9,1},... | collective-permute-start | bytes 208904 | tf_op jit(solution)/shard_map/ppermute | solution.py:269
  28.7 14.7 %all-to-all-start.1 = ((bf16[16,32,256]{2,1,0:T(8,128)(2,1)}), bf16[16,32,256]{2,1,0:T(8,128)(2,1)S(1)}, u32[]{:S(2)}, u32[]{:S(2)}) async-start(bf16[16,32,256]{2,1,0:T(8,128)(2,1)} %bitcast.2), calls=%async_computation.1 | async-start | bytes 524288 | tf_op jit(solution)/shard_map/all_to_all | solution.py:263
  33.9 8.7 %collective-permute-start.4 = (bf16[136,256]{1,0:T(8,128)(2,1)S(1)}, bf16[136,256]{1,0:T(8,128)(2,1)S(1)}, u32[]{:S(2)}, u32[]{:S(2)}) collective-permute-start(bf16[136,256]{1,0:T(8,128)(2,1)S(1)} %shard_map.142.refs_0_), channel_id=1, source_target_pairs={{0,6},{1,7},{2,4},{3,5},{4,2},{5,3},{6,0},{7,1},{8,14},{9,15},{10,... | collective-permute-start | bytes 208904 | tf_op jit(solution)/shard_map/ppermute | solution.py:269
  35.7 7.5 %collective-permute-start.3 = (bf16[136,256]{1,0:T(8,128)(2,1)S(1)}, bf16[136,256]{1,0:T(8,128)(2,1)S(1)}, u32[]{:S(2)}, u32[]{:S(2)}) collective-permute-start(bf16[136,256]{1,0:T(8,128)(2,1)S(1)} %shard_map.142.refs_0_), channel_id=1, source_target_pairs={{0,4},{1,5},{2,6},{3,7},{4,0},{5,1},{6,2},{7,3},{8,12},{9,13},{10,... | collective-permute-start | bytes 208904 | tf_op jit(solution)/shard_map/ppermute | solution.py:269
  37.3 6.0 %collective-permute-start.2 = (bf16[136,256]{1,0:T(8,128)(2,1)S(1)}, bf16[136,256]{1,0:T(8,128)(2,1)S(1)}, u32[]{:S(2)}, u32[]{:S(2)}) collective-permute-start(bf16[136,256]{1,0:T(8,128)(2,1)S(1)} %shard_map.142.refs_0_), channel_id=1, source_target_pairs={{0,2},{1,3},{2,0},{3,1},{4,6},{5,7},{6,4},{7,5},{8,10},{9,11},{10,... | collective-permute-start | bytes 208904 | tf_op jit(solution)/shard_map/ppermute | solution.py:269
  43.3 1.3 %collective-permute-start.5 = (bf16[136,256]{1,0:T(8,128)(2,1)S(1)}, bf16[136,256]{1,0:T(8,128)(2,1)S(1)}, u32[]{:S(2)}, u32[]{:S(2)}) collective-permute-start(bf16[136,256]{1,0:T(8,128)(2,1)S(1)} %shard_map.143.refs_0_), channel_id=1, source_target_pairs={{0,1},{1,0},{2,3},{3,2},{4,5},{5,4},{6,7},{7,6},{8,9},{9,8},{10,11... | collective-permute-start | bytes 208904 | tf_op jit(solution)/shard_map/ppermute | solution.py:269
